TPU v7x, 256 devices: a whole 4x4x8 slice. The times are simulated.
256 devices in a mesh: scan: 16 (over x, y_lo, core), cuts: 16 (over y_hi, z).
Axes of the slice: x: 4, y: 4 (y_hi: 2, y_lo: 2; y = y_hi * 2 + y_lo), z: 8, core: 2. Of those that a mesh axis runs over, the one named last changes fastest.
Arguments:
- partials: bfloat16 [16, 2, 96, 128, 2048], P('scan', None, 'cuts'), may hold values from -1.5 to 1.5
- inverses: bfloat16 [8, 96, 96], replicated, may hold values from -0.625 to 0.625
- classes: int32 [128, 2048], P('scan', 'cuts'), may hold values from 0 to 7
Outputs:
- object_update: float32 [2, 96, 128, 2048], P(None, 'cuts', 'scan')
All inputs are finite; a program needn't handle non-finite values.
Results may differ from a plain program's by a relative error of at most 0.0031.
Values may be sent and summed in bfloat16 or wider, within the bound.
No kernel may reach another device: no remote copies, remote signals or barrier semaphores. Data moves between devices by JAX's collectives and lax.ppermute only.
A program may use at most 128 MiB of HBM per device.

v0:
```python
import jax
import jax.numpy as jnp
from jax import lax
from jax.sharding import PartitionSpec as P

ITERS = 5


def extended(cells, sides, width):
    for axis, dim in sides:
        count = lax.axis_size(axis)
        ends = count - 1
        head = lax.slice_in_dim(cells, 0, width, axis=dim)
        tail = lax.slice_in_dim(cells, cells.shape[dim] - width, cells.shape[dim], axis=dim)
        cells = jnp.concatenate(
            [
                lax.ppermute(tail, axis, [(i, (i + 1) % count) for i in range(ends)]),
                cells,
                lax.ppermute(head, axis, [((i + 1) % count, i) for i in range(ends)]),
            ],
            axis=dim,
        )
    return cells


def tv_step(field, row_first, rows_total):
    count = field.shape[2]
    width = field.shape[3]
    rows = row_first + jnp.arange(count, dtype=jnp.int32)
    cols = jnp.arange(width, dtype=jnp.int32)
    row_ok = ((rows >= 0) & (rows <= rows_total - 2)).astype(jnp.float32)[:, None]
    col_ok = (cols <= width - 2).astype(jnp.float32)
    zero_row = jnp.zeros_like(field[:, :, :1, :])
    zero_col = jnp.zeros_like(field[:, :, :, :1])
    grad_y = (jnp.concatenate([field[:, :, 1:, :], zero_row], axis=2) - field) * row_ok
    grad_x = (jnp.concatenate([field[:, :, :, 1:], zero_col], axis=3) - field) * col_ok
    magnitude = jnp.sqrt(jnp.sum(grad_x * grad_x + grad_y * grad_y, axis=0, keepdims=True) + 1.0)
    flux_y = grad_y / magnitude
    flux_x = grad_x / magnitude
    spread = flux_y - jnp.concatenate([zero_row, flux_y[:, :, :-1, :]], axis=2)
    spread = spread + flux_x - jnp.concatenate([zero_col, flux_x[:, :, :, :-1]], axis=3)
    return field + 0.2 * spread


def on_device(partials, inverses, classes):
    own_part = partials[0]
    summed = lax.psum_scatter(own_part.astype(jnp.float32), "scan", scatter_dimension=2, tiled=True)
    grad = lax.all_to_all(
        summed.astype(jnp.bfloat16), "cuts", split_axis=3, concat_axis=1, tiled=True
    )
    stacked = jnp.einsum("kij,cjrx->kcirx", inverses, grad, preferred_element_type=jnp.float32)
    labels = jnp.arange(inverses.shape[0], dtype=jnp.int32)[:, None, None, None, None]
    chosen = classes[None, None, None, :, :] == labels
    filtered = jnp.sum(jnp.where(chosen, stacked, 0.0), axis=0)
    field = lax.all_to_all(filtered, "cuts", split_axis=1, concat_axis=3, tiled=True)
    own_rows = field.shape[2]
    rows_total = own_rows * lax.axis_size("scan")
    row_base = lax.axis_index("scan") * own_rows
    for step in range(ITERS):
        wider = extended(field, (("scan", 2),), 1)
        wider = tv_step(wider, row_base - 1, rows_total)
        field = wider[:, :, 1 : 1 + own_rows, :]
    return field


def solution(mesh):
    placed = (P("scan", None, "cuts", None, None), P(), P("scan", "cuts"))
    return jax.shard_map(
        on_device,
        mesh=mesh,
        in_specs=placed,
        out_specs=P(None, "cuts", "scan", None),
        check_vma=False,
    )
```

profile of v0, /device:TPU:1, one launch (start us, length us, event | category | flops | bytes accessed | tf_op | source)
XLA Modules:
  0.0 454.9 jit_solution(3355569488202894548)
XLA Ops:
  0.0 13.8 %bitcast_convert_fusion = f32[2,6,128,2048]{3,0,1,2:T(2,128)} fusion(bf16[1,2,6,128,2048]{4,3,2,1,0:T(8,128)(2,1)} %param.3), kind=kLoop, calls=%fused_computation | loop fusion | flops 3145728 | bytes 18874368 | tf_op jit(solution)/shard_map/convert_element_type | solution.py:47
  13.8 270.6 %all-reduce.22 = bf16[2,6,128,2048]{3,0,1,2:T(2,128)(2,1)} all-reduce(f32[2,6,128,2048]{3,0,1,2:T(2,128)} %bitcast_convert_fusion), channel_id=2, replica_groups=mesh['scan'=16,'cuts'=16] {'scan'}, use_global_device_ids=true, to_apply=%region_0.0.clone | all-reduce | flops 3145728 | bytes 18874368
  285.7 1.3 dynamic-slice_convert_fusion
  287.0 11.2 %copy.17 = bf16[2,6,8,2048]{2,0,1,3:T(2,128)(2,1)} copy(bf16[2,6,8,2048]{3,0,1,2:T(2,128)(2,1)S(1)} %dynamic-slice_convert_fusion) | data formatting | bytes 786432 | tf_op jit(solution)/shard_map/convert_element_type | solution.py:49
  298.2 18.4 %reshape.57 = bf16[16,2,6144]{2,1,0:T(2,128)(2,1)} reshape(bf16[2048,6,2,8]{3,2,1,0:T(2,128)(2,1)} %bitcast.37) | data formatting | bytes 786432
  316.6 9.5 %all-to-all-start = ((bf16[16,2,6144]{2,1,0:T(2,128)(2,1)}), bf16[16,2,6144]{2,1,0:T(2,128)(2,1)S(1)}, u32[]{:S(2)}, u32[]{:S(2)}) async-start(bf16[16,2,6144]{2,1,0:T(2,128)(2,1)} %reshape.57), calls=%async_computation | async-start | bytes 786432 | tf_op jit(solution)/shard_map/all_to_all | solution.py:48
  326.2 12.2 %all-to-all-done = bf16[16,2,6144]{2,1,0:T(2,128)(2,1)S(1)} async-done(((bf16[16,2,6144]{2,1,0:T(2,128)(2,1)}), bf16[16,2,6144]{2,1,0:T(2,128)(2,1)S(1)}, u32[]{:S(2)}, u32[]{:S(2)}) %all-to-all-start) | async-done | bytes 393248 | tf_op jit(solution)/shard_map/all_to_all | solution.py:48
  338.4 8.3 %reshape.58 = bf16[2048,6,2,8]{3,2,1,0:T(2,128)(2,1)} reshape(bf16[16,2,6144]{2,1,0:T(2,128)(2,1)S(1)} %all-to-all-done) | data formatting | bytes 786432
  346.7 13.3 %copy.27 = bf16[2,6,8,16,128]{4,2,1,3,0:T(8,128)(2,1)S(1)} copy(bf16[2,6,8,16,128]{2,0,1,4,3:T(2,128)(2,1)} %bitcast.38) | data formatting | bytes 786432 | tf_op jit(solution)/shard_map/all_to_all | solution.py:48
  361.0 1.3 copy.21
  362.4 4.5 all-to-all-start.1
  366.9 21.7 %all-to-all-done.1 = f32[2,96,8,128]{3,2,0,1:T(8,128)S(1)} async-done(((f32[2,96,8,128]{3,2,0,1:T(8,128)}), f32[2,96,8,128]{3,2,0,1:T(8,128)S(1)}, u32[]{:S(2)}, u32[]{:S(2)}) %all-to-all-start.1) | async-done | bytes 786464 | tf_op jit(solution)/shard_map/all_to_all | solution.py:55
  389.4 1.9 collective-permute-start
  391.3 4.1 collective-permute-start.1
  395.4 1.8 collective-permute-done.1
  399.8 1.1 multiply_add_fusion.3
  401.0 3.7 collective-permute-start.2
  404.7 1.9 collective-permute-start.3
  406.8 6.3 %collective-permute-done.3 = f32[2,6,1,2048]{3,2,1,0:T(1,128)S(1)} collective-permute-done((f32[2,6,1,2048]{3,2,1,0:T(1,128)S(1)}, f32[2,6,1,2048]{3,2,1,0:T(1,128)S(1)}, u32[]{:S(2)}, u32[]{:S(2)}) %collective-permute-start.3) | collective-permute-done | bytes 98336 | tf_op jit(solution)/shard_map/ppermute | solution.py:19
  415.6 1.1 multiply_add_fusion.2
  416.9 1.9 collective-permute-start.4
  418.8 2.4 collective-permute-start.5
  421.3 4.3 collective-permute-done.5
  428.2 1.1 multiply_add_fusion.1
  429.5 1.9 collective-permute-start.6
  431.4 2.6 collective-permute-start.7
  434.1 4.1 collective-permute-done.7
  440.8 1.1 multiply_add_fusion
  442.0 1.9 collective-permute-start.8
  444.0 2.4 collective-permute-start.9
  446.5 4.3 collective-permute-done.9
  453.4 1.6 slice_add_fusion
  (54 shorter events, 16.0 us)
Async XLA Ops:
  0.0 360.0 %copy-start = (bf16[8,96,96]{2,1,0:T(8,128)(2,1)S(1)}, bf16[8,96,96]{2,1,0:T(8,128)(2,1)}, u32[]{:S(2)}) copy-start(bf16[8,96,96]{2,1,0:T(8,128)(2,1)} %param.4) | copy-start | bytes 442372
  13.8 270.6 %copy-start.3 = (u32[256]{0:T(256)S(1)}, u32[256]{0:T(256)}, u32[]{:S(2)}) copy-start(u32[256]{0:T(256)} %constant.68) | copy-start | bytes 3076
  298.2 27.9 %copy-start.2 = (s32[8,128]{1,0:T(8,128)S(1)}, s32[8,128]{1,0:T(8,128)}, u32[]{:S(2)}) copy-start(s32[8,128]{1,0:T(8,128)} %param.5) | copy-start | bytes 12292
  316.6 21.8 %all-to-all-start = ((bf16[16,2,6144]{2,1,0:T(2,128)(2,1)}), bf16[16,2,6144]{2,1,0:T(2,128)(2,1)S(1)}, u32[]{:S(2)}, u32[]{:S(2)}) async-start(bf16[16,2,6144]{2,1,0:T(2,128)(2,1)} %reshape.57), calls=%async_computation | async-start | bytes 786432 | tf_op jit(solution)/shard_map/all_to_all | solution.py:48
  362.4 26.3 %all-to-all-start.1 = ((f32[2,96,8,128]{3,2,0,1:T(8,128)}), f32[2,96,8,128]{3,2,0,1:T(8,128)S(1)}, u32[]{:S(2)}, u32[]{:S(2)}) async-start(f32[2,96,8,128]{3,2,0,1:T(8,128)} %copy.21), calls=%async_computation.1 | async-start | bytes 1572864 | tf_op jit(solution)/shard_map/all_to_all | solution.py:55
  389.4 6.0 %collective-permute-start = (f32[2,6,1,2048]{3,2,1,0:T(1,128)S(1)}, f32[2,6,1,2048]{3,2,1,0:T(1,128)S(1)}, u32[]{:S(2)}, u32[]{:S(2)}) collective-permute-start(f32[2,6,1,2048]{3,2,1,0:T(1,128)S(1)} %get-tuple-element.23), channel_id=1, source_target_pairs={{0,16},{16,32},{32,48},{48,64},{64,80},{80,96},{96,112},{112,128},... | collective-permute-start | bytes 294920 | tf_op jit(solution)/shard_map/ppermute | solution.py:17
  391.3 5.9 %collective-permute-start.1 = (f32[2,6,1,2048]{3,2,1,0:T(1,128)S(1)}, f32[2,6,1,2048]{3,2,1,0:T(1,128)S(1)}, u32[]{:S(2)}, u32[]{:S(2)}) collective-permute-start(f32[2,6,1,2048]{3,2,1,0:T(1,128)S(1)} %get-tuple-element.24), channel_id=1, source_target_pairs={{16,0},{32,16},{48,32},{64,48},{80,64},{96,80},{112,96},{128,112},... | collective-permute-start | bytes 294920 | tf_op jit(solution)/shard_map/ppermute | solution.py:19
  401.0 5.8 %collective-permute-start.2 = (f32[2,6,1,2048]{3,2,1,0:T(1,128)S(1)}, f32[2,6,1,2048]{3,2,1,0:T(1,128)S(1)}, u32[]{:S(2)}, u32[]{:S(2)}) collective-permute-start(f32[2,6,1,2048]{3,2,1,0:T(1,128)S(1)} %get-tuple-element.21), channel_id=1, source_target_pairs={{0,16},{16,32},{32,48},{48,64},{64,80},{80,96},{96,112},{112,128},... | collective-permute-start | bytes 294920 | tf_op jit(solution)/shard_map/ppermute | solution.py:17
  404.7 8.3 %collective-permute-start.3 = (f32[2,6,1,2048]{3,2,1,0:T(1,128)S(1)}, f32[2,6,1,2048]{3,2,1,0:T(1,128)S(1)}, u32[]{:S(2)}, u32[]{:S(2)}) collective-permute-start(f32[2,6,1,2048]{3,2,1,0:T(1,128)S(1)} %get-tuple-element.22), channel_id=1, source_target_pairs={{16,0},{32,16},{48,32},{64,48},{80,64},{96,80},{112,96},{128,112},... | collective-permute-start | bytes 294920 | tf_op jit(solution)/shard_map/ppermute | solution.py:19
  416.9 4.4 collective-permute-start.4
  418.8 6.8 %collective-permute-start.5 = (f32[2,6,1,2048]{3,2,1,0:T(1,128)S(1)}, f32[2,6,1,2048]{3,2,1,0:T(1,128)S(1)}, u32[]{:S(2)}, u32[]{:S(2)}) collective-permute-start(f32[2,6,1,2048]{3,2,1,0:T(1,128)S(1)} %get-tuple-element.20), channel_id=1, source_target_pairs={{16,0},{32,16},{48,32},{64,48},{80,64},{96,80},{112,96},{128,112},... | collective-permute-start | bytes 294920 | tf_op jit(solution)/shard_map/ppermute | solution.py:19
  429.5 4.7 %collective-permute-start.6 = (f32[2,6,1,2048]{3,2,1,0:T(1,128)S(1)}, f32[2,6,1,2048]{3,2,1,0:T(1,128)S(1)}, u32[]{:S(2)}, u32[]{:S(2)}) collective-permute-start(f32[2,6,1,2048]{3,2,1,0:T(1,128)S(1)} %get-tuple-element.17), channel_id=1, source_target_pairs={{0,16},{16,32},{32,48},{48,64},{64,80},{80,96},{96,112},{112,128},... | collective-permute-start | bytes 294920 | tf_op jit(solution)/shard_map/ppermute | solution.py:17
  431.4 6.8 %collective-permute-start.7 = (f32[2,6,1,2048]{3,2,1,0:T(1,128)S(1)}, f32[2,6,1,2048]{3,2,1,0:T(1,128)S(1)}, u32[]{:S(2)}, u32[]{:S(2)}) collective-permute-start(f32[2,6,1,2048]{3,2,1,0:T(1,128)S(1)} %get-tuple-element.18), channel_id=1, source_target_pairs={{16,0},{32,16},{48,32},{64,48},{80,64},{96,80},{112,96},{128,112},... | collective-permute-start | bytes 294920 | tf_op jit(solution)/shard_map/ppermute | solution.py:19
  442.0 4.4 collective-permute-start.8
  444.0 6.8 %collective-permute-start.9 = (f32[2,6,1,2048]{3,2,1,0:T(1,128)S(1)}, f32[2,6,1,2048]{3,2,1,0:T(1,128)S(1)}, u32[]{:S(2)}, u32[]{:S(2)}) collective-permute-start(f32[2,6,1,2048]{3,2,1,0:T(1,128)S(1)} %get-tuple-element.16), channel_id=1, source_target_pairs={{16,0},{32,16},{48,32},{64,48},{80,64},{96,80},{112,96},{128,112},... | collective-permute-start | bytes 294920 | tf_op jit(solution)/shard_map/ppermute | solution.py:19
  453.4 1.6 copy-start.1
where the time goes:
time: 457 us; the launch traced here: 455 us
  blocking collectives  271 us (59%)
  local copies, waits for them, and re-layouts  58.4 us (13%)
  waiting for transfers between devices  54.8 us (12%)
  starting transfers between devices  38.9 us (9%)
  other arithmetic  30.1 us (7%)
    unnamed x1, blocking collectives  271 us
    unnamed x11, local copies, waits for them, and re-layouts  27.3 us
    all_to_all x1, waiting for transfers between devices, on_device(): lax.all_to_all(filtered, 'cuts', split_axis=1, concat_axis=3, tiled=True)  21.7 us
    ppermute x5, waiting for transfers between devices, extended(): lax.ppermute(head, axis, [((i + 1) % count, i) for i in range(ends)])  20.9 us
    convert_element_type x1, other arithmetic, on_device(): own_part.astype(jnp.float32)  13.8 us
    ppermute x5, starting transfers between devices, extended(): lax.ppermute(head, axis, [((i + 1) % count, i) for i in range(ends)])  13.4 us
    all_to_all x1, local copies, waits for them, and re-layouts, on_device(): lax.all_to_all(summed.astype(jnp.bfloat16), 'cuts', split_axis=3, concat_...  13.3 us
    convert_element_type x2, local copies, waits for them, and re-layouts, on_device(): summed.astype(jnp.bfloat16)  12.5 us
  transfers between devices with their start and end apart: 12, of which 7 were waited for; matrix products, arithmetic and copies ran while one was open for 0% of the time, Pallas kernels for 0%

commit v1 on v0

v1 whole, which is shorter than its diff:
```python
import jax
import jax.numpy as jnp
from jax import lax
from jax.experimental import pallas as pl
from jax.experimental.pallas import tpu as pltpu
from jax.sharding import PartitionSpec as P

ITERS = 5
SCALE = 32.0


def filter_kernel(grad_ref, weights_ref, classes_ref, out_ref, rows_in, rows_out):
    blocks, parts, depth, rows, lanes = grad_ref.shape
    total = blocks * depth
    kinds = weights_ref.shape[1] // total
    for part in range(parts):
        rows_in[part] = grad_ref[:, part].astype(jnp.float32).reshape(total * rows, lanes)
    weights = weights_ref[...]
    for row in range(rows):
        label = classes_ref[row : row + 1, :]
        label = jnp.concatenate([label] * parts, axis=1)
        values = jnp.concatenate(
            [rows_in[part, pl.ds(row, total, stride=rows), :] for part in range(parts)], axis=1
        )
        masked = jnp.concatenate(
            [jnp.where(label == kind, values, 0.0) for kind in range(kinds)], axis=0
        ).astype(jnp.bfloat16)
        found = jnp.dot(weights, masked, preferred_element_type=jnp.float32)
        for part in range(parts):
            rows_out[part, pl.ds(row, total, stride=rows), :] = found[:, part * lanes : (part + 1) * lanes]
    for part in range(parts):
        out_ref[:, part] = rows_out[part].reshape(blocks, depth, rows, lanes)


def tv_kernel(above_ref, own_ref, below_ref, out_ref, field, result):
    blocks, parts, depth, rows, lanes = own_ref.shape
    halo = ITERS
    step = parts * depth * rows
    first = (lax.axis_index("scan") == 0).astype(jnp.float32)
    last = (lax.axis_index("scan") == lax.axis_size("scan") - 1).astype(jnp.float32)
    lane = lax.broadcasted_iota(jnp.int32, (blocks, lanes), 1)
    block = lax.broadcasted_iota(jnp.int32, (blocks, lanes), 0)
    at_left = lane == 0
    at_right = lane == lanes - 1
    inner = jnp.where(at_right & (block == blocks - 1), 0.0, 1.0)

    def following(cells):
        near = pltpu.roll(cells, lanes - 1, 1)
        return jnp.where(at_right, pltpu.roll(near, blocks - 1, 0), near)

    def preceding(cells):
        near = pltpu.roll(cells, 1, 1)
        return jnp.where(at_left, pltpu.roll(near, 1, 0), near)

    def one_slice(s, carry):
        for row in range(-halo, rows + halo):
            source, at = (above_ref, row + rows) if row < 0 else (own_ref, row) if row < rows else (below_ref, row - rows)
            for part in range(parts):
                field[row + halo, part] = source[:, part, s, at, :]
        for sweep in range(1, ITERS + 1):
            low, high = sweep - ITERS, rows + ITERS - sweep
            before = None
            here = [field[low - 1 + halo, part] for part in range(parts)]
            for row in range(low - 1, high):
                below = [field[row + 1 + halo, part] for part in range(parts)]
                down = [b - h for b, h in zip(below, here)]
                if row == -1:
                    down = [d * (1.0 - first) for d in down]
                if row == rows - 1:
                    down = [d * (1.0 - last) for d in down]
                across = [(following(h) - h) * inner for h in here]
                power = sum(d * d for d in down) + sum(a * a for a in across)
                inverse = lax.rsqrt(power + 1.0)
                flux = [d * inverse for d in down]
                if before is not None:
                    for part in range(parts):
                        side = across[part] * inverse
                        spread = flux[part] - before[part] + side - preceding(side)
                        fresh = here[part] + 0.2 * spread
                        if sweep == ITERS:
                            out_ref[part, s, row, :, :] = fresh
                        else:
                            field[row + halo, part] = fresh
                before = flux
                here = below
        return carry

    lax.fori_loop(0, depth, one_slice, 0)


def on_device(partials, inverses, classes):
    _, parts, depth, rows_total, width = partials.shape
    scans = lax.axis_size("scan")
    cuts = lax.axis_size("cuts")
    rows = rows_total // scans
    lanes = width // cuts
    kinds, total, _ = inverses.shape
    core = lax.axis_index("scan") % 2

    split = partials.reshape(parts, depth, scans // 2, 2, rows, width)
    give = lax.dynamic_index_in_dim(split, 1 - core, 3, keepdims=False)
    keep = lax.dynamic_index_in_dim(split, core, 3, keepdims=False)
    got = lax.ppermute(give, "scan", [(i, i ^ 1) for i in range(scans)])
    pair = (keep.astype(jnp.float32) + got.astype(jnp.float32)).astype(jnp.bfloat16)
    pair = pair.transpose(2, 0, 1, 3, 4)
    groups = [list(range(c, scans, 2)) for c in range(2)]
    terms = lax.all_to_all(pair, "scan", 0, 0, axis_index_groups=groups, tiled=True)
    grad = jnp.sum(terms.astype(jnp.float32), axis=0).astype(jnp.bfloat16)

    grad = grad.reshape(parts, depth, rows, cuts, lanes).transpose(3, 0, 1, 2, 4)
    grad = lax.all_to_all(grad, "cuts", 0, 0, tiled=True)
    weights = inverses.transpose(1, 0, 2).reshape(total, kinds * total)
    filtered = pl.pallas_call(
        filter_kernel,
        out_shape=jax.ShapeDtypeStruct(grad.shape, jnp.float32),
        scratch_shapes=[
            pltpu.VMEM((parts, total * rows, lanes), jnp.float32),
            pltpu.VMEM((parts, total * rows, lanes), jnp.float32),
        ],
        compiler_params=pltpu.CompilerParams(vmem_limit_bytes=32 * 1024 * 1024),
    )(grad, weights, classes)
    coded = (filtered * SCALE).astype(jnp.float16)
    coded = lax.all_to_all(coded, "cuts", 0, 0, tiled=True)
    above = lax.ppermute(coded, "scan", [(i, i + 1) for i in range(scans - 1)])
    below = lax.ppermute(coded, "scan", [(i + 1, i) for i in range(scans - 1)])
    above, own, below = [c.astype(jnp.float32) * (1.0 / SCALE) for c in (above, coded, below)]
    result = pl.pallas_call(
        tv_kernel,
        out_shape=jax.ShapeDtypeStruct((parts, depth, rows, cuts, lanes), jnp.float32),
        scratch_shapes=[
            pltpu.VMEM((rows + 2 * ITERS, parts, cuts, lanes), jnp.float32),
            pltpu.VMEM((8, lanes), jnp.float32),
        ],
        compiler_params=pltpu.CompilerParams(vmem_limit_bytes=32 * 1024 * 1024),
    )(above, own, below)
    return result.reshape(parts, depth, rows, width)


def solution(mesh):
    placed = (P("scan", None, "cuts", None, None), P(), P("scan", "cuts"))
    return jax.shard_map(
        on_device,
        mesh=mesh,
        in_specs=placed,
        out_specs=P(None, "cuts", "scan", None),
        check_vma=False,
    )
```

time: 457 us -> 123 us (0.27)
  blocking collectives: 271 us -> 57.5 us
  local copies, waits for them, and re-layouts: 58.4 us -> 5.32 us
  waiting for transfers between devices: 54.8 us -> 21.8 us
  other arithmetic: 30.1 us -> 5.1 us
  starting transfers between devices: 38.9 us -> 22.9 us
  Pallas kernels: 0 us -> 9.88 us
    unnamed x1 -> x0, blocking collectives: 271 us -> none
    all_to_all x0 -> x2, blocking collectives: none -> 57.5 us  [the longest x1 39.8 us: on_device(): lax.all_to_all(pair, 'scan', 0, 0, axis_index_groups=groups, tiled=True)]
    unnamed x11 -> x2, local copies, waits for them, and re-layouts: 27.3 us -> 0.01 us
    all_to_all x2 -> x1, waiting for transfers between devices: 33.9 us -> 9.52 us  [on_device(): grad = lax.all_to_all(grad, 'cuts', 0, 0, tiled=True)]
    all_to_all x3 -> x0, local copies, waits for them, and re-layouts: 13.9 us -> none  [the longest x1 13.3 us: on_device(): lax.all_to_all(summed.astype(jnp.bfloat16), 'cuts', split_axis=3, concat_...]
    convert_element_type x3 -> x1, other arithmetic: 13.8 us -> 0.09 us  [on_device(): coded = (filtered * SCALE).astype(jnp.float16)]
    ppermute x10 -> x3, starting transfers between devices: 24.8 us -> 12.2 us  [the longest x1 5.96 us: on_device(): below = lax.ppermute(coded, 'scan', [(i + 1, i) for i in range(scans - 1)])]
    convert_element_type x2 -> x0, local copies, waits for them, and re-layouts: 12.5 us -> none  [on_device(): summed.astype(jnp.bfloat16)]
  transfers between devices with their start and end apart: 12 -> 4, of which waited for: 7 -> 4; matrix products, arithmetic and copies ran while one was open for 0% -> 1% of each run, Pallas kernels for 0% -> 0%
where the time goes in v1:
time: 123 us
  blocking collectives  57.5 us (47%)
  starting transfers between devices  22.9 us (19%)
  waiting for transfers between devices  21.8 us (18%)
  Pallas kernels  9.88 us (8%)
  local copies, waits for them, and re-layouts  5.32 us (4%)
  other arithmetic  5.1 us (4%)
    all_to_all x1, blocking collectives, on_device(): lax.all_to_all(pair, 'scan', 0, 0, axis_index_groups=groups, tiled=True)  39.8 us
    all_to_all x1, blocking collectives, on_device(): coded = lax.all_to_all(coded, 'cuts', 0, 0, tiled=True)  17.7 us
    all_to_all x1, starting transfers between devices, on_device(): grad = lax.all_to_all(grad, 'cuts', 0, 0, tiled=True)  10.6 us
    all_to_all x1, waiting for transfers between devices, on_device(): grad = lax.all_to_all(grad, 'cuts', 0, 0, tiled=True)  9.52 us
    pallas_call x1, Pallas kernels, on_device(): pl.pallas_call(tv_kernel, out_shape=jax.ShapeDtypeStruct((parts, depth, r...  9.13 us
    ppermute x1, starting transfers between devices, on_device(): below = lax.ppermute(coded, 'scan', [(i + 1, i) for i in range(scans - 1)])  5.96 us
    ppermute x1, waiting for transfers between devices, on_device(): got = lax.ppermute(give, 'scan', [(i, i ^ 1) for i in range(scans)])  5.42 us
    transpose x1, other arithmetic, on_device(): pair = pair.transpose(2, 0, 1, 3, 4)  4.18 us
  transfers between devices with their start and end apart: 4, of which 4 were waited for; matrix products, arithmetic and copies ran while one was open for 1% of the time, Pallas kernels for 0%

profile of v1, /device:TPU:1, one launch (start us, length us, event | category | flops | bytes accessed | tf_op | source)
XLA Modules:
  0.0 122.5 jit_solution(15609956049788035663)
XLA Ops:
  0.0 2.1 %dynamic-slice_bitcast_fusion = bf16[2,6,8,8,2048]{4,3,2,1,0:T(8,128)(2,1)S(1)} fusion(bf16[2,6,8,2,8,2048]{5,4,3,2,1,0:T(8,128)(2,1)} %bitcast.18, s32[]{:T(128)S(6)} %select_n.16), kind=kLoop, calls=%fused_computation.3 | loop fusion | bytes 6291460 | tf_op jit(solution)/shard_map/jit(dynamic_index_in_dim)/squeeze | solution.py:101
  2.1 3.3 %collective-permute-start = (bf16[2,6,8,8,2048]{4,3,2,1,0:T(8,128)(2,1)S(1)}, bf16[2,6,8,8,2048]{4,3,2,1,0:T(8,128)(2,1)}, u32[]{:S(2)}, u32[]{:S(2)}) collective-permute-start(bf16[2,6,8,8,2048]{4,3,2,1,0:T(8,128)(2,1)S(1)} %dynamic-slice_bitcast_fusion), channel_id=1, source_target_pairs={{0,16},{16,0},{32,48},{48,32},{64,80},{80,64},{96,112},{112,96},{1... | collective-permute-start | bytes 9437192 | tf_op jit(solution)/shard_map/ppermute | solution.py:103
  5.4 5.4 %collective-permute-done = bf16[2,6,8,8,2048]{4,3,2,1,0:T(8,128)(2,1)} collective-permute-done((bf16[2,6,8,8,2048]{4,3,2,1,0:T(8,128)(2,1)S(1)}, bf16[2,6,8,8,2048]{4,3,2,1,0:T(8,128)(2,1)}, u32[]{:S(2)}, u32[]{:S(2)}) %collective-permute-start) | collective-permute-done | bytes 3145760 | tf_op jit(solution)/shard_map/ppermute | solution.py:103
  10.9 4.2 %fusion.1 = bf16[8,2,6,8,2048]{4,3,0,2,1:T(8,128)(2,1)S(1)} fusion(bf16[2,6,8,8,2048]{4,3,2,1,0:T(8,128)(2,1)} %collective-permute-done, bf16[2,6,8,2,8,2048]{5,4,3,2,1,0:T(8,128)(2,1)} %bitcast.19, s32[]{:T(128)S(6)} %select_n.15), kind=kLoop, calls=%fused_computation.2 | loop fusion | flops 6291456 | bytes 9437188 | tf_op jit(solution)/shard_map/transpose | solution.py:105
  15.0 0.2 copy.9
  15.3 39.8 %all_to_all.15 = bf16[8,2,6,8,2048]{4,3,2,1,0:T(8,128)(2,1)S(1)} all-to-all(bf16[8,2,6,8,2048]{4,3,2,1,0:T(8,128)(2,1)S(1)} %copy.9), channel_id=1, replica_groups={{0,32,64,96,128,160,192,224},{16,48,80,112,144,176,208,240},{1,33,65,97..., dimensions={0} | all-to-all | bytes 6291456 | tf_op jit(solution)/shard_map/all_to_all | solution.py:107
  55.1 0.0 copy-start
  55.1 0.6 reduce_sum.12
  55.7 0.8 bitcast_bitcast_fusion
  56.5 10.6 %all-to-all-start.1 = ((bf16[16,2,6,8,128]{4,3,2,1,0:T(8,128)(2,1)}), bf16[16,2,6,8,128]{4,3,2,1,0:T(8,128)(2,1)S(1)}, u32[]{:S(2)}, u32[]{:S(2)}) async-start(bf16[16,2,6,8,128]{4,3,2,1,0:T(8,128)(2,1)} %bitcast_bitcast_fusion), calls=%async_computation.1 | async-start | bytes 786432 | tf_op jit(solution)/shard_map/all_to_all | solution.py:111
  67.1 1.0 copy.11
  68.1 0.2 reshape.16.weights_ref
  68.3 9.5 %all-to-all-done.1.grad_ref = bf16[16,2,6,8,128]{4,3,2,1,0:T(8,128)(2,1)S(1)} async-done(((bf16[16,2,6,8,128]{4,3,2,1,0:T(8,128)(2,1)}), bf16[16,2,6,8,128]{4,3,2,1,0:T(8,128)(2,1)S(1)}, u32[]{:S(2)}, u32[]{:S(2)}) %all-to-all-start.1) | async-done | bytes 393248 | tf_op jit(solution)/shard_map/all_to_all | solution.py:111
  77.8 0.0 copy-done
  77.8 0.8 shard_map.37
  78.6 0.1 multiply_convert_fusion
  78.7 17.7 %all_to_all.16 = f16[16,2,6,8,128]{4,3,2,1,0:T(8,128)(2,1)S(1)} all-to-all(f16[16,2,6,8,128]{4,3,2,1,0:T(8,128)(2,1)S(1)} %multiply_convert_fusion), channel_id=1, replica_groups=mesh['scan'=16,'cuts'=16] {'cuts'}, dimensions={0} | all-to-all | bytes 786432 | tf_op jit(solution)/shard_map/all_to_all | solution.py:123
  96.3 6.0 %collective-permute-start.2 = (f16[16,2,6,8,128]{4,3,2,1,0:T(8,128)(2,1)S(1)}, f16[16,2,6,8,128]{4,3,2,1,0:T(8,128)(2,1)S(1)}, u32[]{:S(2)}, u32[]{:S(2)}) collective-permute-start(f16[16,2,6,8,128]{4,3,2,1,0:T(8,128)(2,1)S(1)} %all_to_all.16), channel_id=1, source_target_pairs={{16,0},{32,16},{48,32},{64,48},{80,64},{96,80},{112,96},{128,112},... | collective-permute-start | bytes 1179656 | tf_op jit(solution)/shard_map/ppermute | solution.py:125
  102.3 3.0 %collective-permute-start.1 = (f16[16,2,6,8,128]{4,3,2,1,0:T(8,128)(2,1)S(1)}, f16[16,2,6,8,128]{4,3,2,1,0:T(8,128)(2,1)S(1)}, u32[]{:S(2)}, u32[]{:S(2)}) collective-permute-start(f16[16,2,6,8,128]{4,3,2,1,0:T(8,128)(2,1)S(1)} %all_to_all.16), channel_id=1, source_target_pairs={{0,16},{16,32},{32,48},{48,64},{64,80},{80,96},{96,112},{112,128},... | collective-permute-start | bytes 1179656 | tf_op jit(solution)/shard_map/ppermute | solution.py:124
  105.3 0.1 convert_multiply_fusion.1.own_ref
  105.4 3.4 %collective-permute-done.2 = f16[16,2,6,8,128]{4,3,2,1,0:T(8,128)(2,1)S(1)} collective-permute-done((f16[16,2,6,8,128]{4,3,2,1,0:T(8,128)(2,1)S(1)}, f16[16,2,6,8,128]{4,3,2,1,0:T(8,128)(2,1)S(1)}, u32[]{:S(2)}, u32[]{:S(2)}) %collective-permute-start.2) | collective-permute-done | bytes 393248 | tf_op jit(solution)/shard_map/ppermute | solution.py:125
  108.8 0.1 convert_multiply_fusion.below_ref
  108.9 3.4 %collective-permute-done.1 = f16[16,2,6,8,128]{4,3,2,1,0:T(8,128)(2,1)S(1)} collective-permute-done((f16[16,2,6,8,128]{4,3,2,1,0:T(8,128)(2,1)S(1)}, f16[16,2,6,8,128]{4,3,2,1,0:T(8,128)(2,1)S(1)}, u32[]{:S(2)}, u32[]{:S(2)}) %collective-permute-start.1) | collective-permute-done | bytes 393248 | tf_op jit(solution)/shard_map/ppermute | solution.py:124
  112.3 0.1 convert_multiply_fusion.2.above_ref
  112.4 9.1 %shard_map.38 = f32[2,6,8,16,128]{4,3,2,1,0:T(8,128)S(1)} custom-call(f32[16,2,6,8,128]{4,3,2,1,0:T(8,128)S(1)} %convert_multiply_fusion.2.above_ref, f32[16,2,6,8,128]{4,3,2,1,0:T(8,128)S(1)} %convert_multiply_fusion.1.own_ref, f32[16,2,6,8,128]{4,3,2,1,0:T(8,128)S(1)} %convert_multiply_fusion.below_ref), custom_call_target="tpu_custom_call" | custom-call | tf_op jit(solution)/shard_map/pallas_call | solution.py:127
  121.5 1.0 reshape.17
Async XLA Ops:
  2.1 8.7 %collective-permute-start = (bf16[2,6,8,8,2048]{4,3,2,1,0:T(8,128)(2,1)S(1)}, bf16[2,6,8,8,2048]{4,3,2,1,0:T(8,128)(2,1)}, u32[]{:S(2)}, u32[]{:S(2)}) collective-permute-start(bf16[2,6,8,8,2048]{4,3,2,1,0:T(8,128)(2,1)S(1)} %dynamic-slice_bitcast_fusion), channel_id=1, source_target_pairs={{0,16},{16,0},{32,48},{48,32},{64,80},{80,64},{96,112},{112,96},{1... | collective-permute-start | bytes 9437192 | tf_op jit(solution)/shard_map/ppermute | solution.py:103
  55.1 22.8 %copy-start = (s32[8,128]{1,0:T(8,128)S(1)}, s32[8,128]{1,0:T(8,128)}, u32[]{:S(2)}) copy-start(s32[8,128]{1,0:T(8,128)} %classes_ref.1) | copy-start | bytes 12292
  56.5 21.3 %all-to-all-start.1 = ((bf16[16,2,6,8,128]{4,3,2,1,0:T(8,128)(2,1)}), bf16[16,2,6,8,128]{4,3,2,1,0:T(8,128)(2,1)S(1)}, u32[]{:S(2)}, u32[]{:S(2)}) async-start(bf16[16,2,6,8,128]{4,3,2,1,0:T(8,128)(2,1)} %bitcast_bitcast_fusion), calls=%async_computation.1 | async-start | bytes 786432 | tf_op jit(solution)/shard_map/all_to_all | solution.py:111
  96.3 12.4 %collective-permute-start.2 = (f16[16,2,6,8,128]{4,3,2,1,0:T(8,128)(2,1)S(1)}, f16[16,2,6,8,128]{4,3,2,1,0:T(8,128)(2,1)S(1)}, u32[]{:S(2)}, u32[]{:S(2)}) collective-permute-start(f16[16,2,6,8,128]{4,3,2,1,0:T(8,128)(2,1)S(1)} %all_to_all.16), channel_id=1, source_target_pairs={{16,0},{32,16},{48,32},{64,48},{80,64},{96,80},{112,96},{128,112},... | collective-permute-start | bytes 1179656 | tf_op jit(solution)/shard_map/ppermute | solution.py:125
  102.3 10.0 %collective-permute-start.1 = (f16[16,2,6,8,128]{4,3,2,1,0:T(8,128)(2,1)S(1)}, f16[16,2,6,8,128]{4,3,2,1,0:T(8,128)(2,1)S(1)}, u32[]{:S(2)}, u32[]{:S(2)}) collective-permute-start(f16[16,2,6,8,128]{4,3,2,1,0:T(8,128)(2,1)S(1)} %all_to_all.16), channel_id=1, source_target_pairs={{0,16},{16,32},{32,48},{48,64},{64,80},{80,96},{96,112},{112,128},... | collective-permute-start | bytes 1179656 | tf_op jit(solution)/shard_map/ppermute | solution.py:124

commit v2 on v1

v2 whole, which is shorter than its diff:
```python
import jax
import jax.numpy as jnp
from jax import lax
from jax.experimental import pallas as pl
from jax.experimental.pallas import tpu as pltpu
from jax.sharding import PartitionSpec as P

ITERS = 5
TILE = 16
SUM_SCALE = 1024.0
SCALE = 32.0


def filter_kernel(grad_ref, weights_ref, classes_ref, out_ref, cells):
    blocks, parts, depth, rows, lanes = grad_ref.shape
    total = blocks * depth
    kinds = weights_ref.shape[1] // total
    for part in range(parts):
        cells[part] = grad_ref[:, part].astype(jnp.float32).reshape(total * rows, lanes)
    weights = weights_ref[...]
    for row in range(rows):
        label = classes_ref[row : row + 1, :]
        label = jnp.concatenate([label] * parts, axis=1)
        values = jnp.concatenate(
            [cells[part, pl.ds(row, total, stride=rows), :] for part in range(parts)], axis=1
        )
        masked = jnp.concatenate(
            [jnp.where(label == kind, values, 0.0) for kind in range(kinds)], axis=0
        ).astype(jnp.bfloat16)
        found = jnp.dot(weights, masked, preferred_element_type=jnp.float32)
        for part in range(parts):
            for s in range(depth):
                out_ref[pl.ds((row * parts + part) * depth + s, blocks, stride=rows * parts * depth), :] = found[
                    s * blocks : (s + 1) * blocks, part * lanes : (part + 1) * lanes
                ]


def tv_kernel(shape, skipped, above_ref, own_ref, below_ref, out_ref, field):
    blocks, parts, depth, rows, lanes = shape
    halo = ITERS
    half = blocks // 2
    first = (lax.axis_index("scan") == 0).astype(jnp.float32)
    last = (lax.axis_index("scan") == lax.axis_size("scan") - 1).astype(jnp.float32)
    lane = lax.broadcasted_iota(jnp.int32, (half, lanes), 1)
    line = lax.broadcasted_iota(jnp.int32, (half, lanes), 0)
    at_left = lane == 0
    at_right = lane == lanes - 1
    inner = jnp.where(at_right & (line == half - 1), 0.0, 1.0)

    def following(pair):
        near = [pltpu.roll(p, lanes - 1, 1) for p in pair]
        return jnp.where(at_right, near[1], near[0]), jnp.where(at_right, pltpu.roll(near[0], half - 1, 0), near[1])

    def preceding(pair):
        near = [pltpu.roll(p, 1, 1) for p in pair]
        return jnp.where(at_left, pltpu.roll(near[1], 1, 0), near[0]), jnp.where(at_left, near[0], near[1])

    def load(s, row, part, side):
        if row < 0:
            source, at = above_ref, (row + rows) * parts * depth - skipped
        elif row < rows:
            source, at = own_ref, row * parts * depth
        else:
            source, at = below_ref, (row - rows) * parts * depth
        per = source.shape[0] // blocks
        return source[pl.ds(side * per + at + part * depth + s, half, stride=2 * per), :]

    def one_slice(s, carry):
        for sweep in range(1, ITERS + 1):
            low, high = sweep - ITERS, rows + ITERS - sweep

            def read(row):
                if sweep == 1:
                    return [[load(s, row, part, side) for side in range(2)] for part in range(parts)]
                return [[field[row + halo, part, side] for side in range(2)] for part in range(parts)]

            before = None
            here = read(low - 1)
            for row in range(low - 1, high):
                below = read(row + 1)
                flux, across, inverse = [], [], []
                down = [[b - h for b, h in zip(bs, hs)] for bs, hs in zip(below, here)]
                if row == -1:
                    down = [[d * (1.0 - first) for d in ds] for ds in down]
                if row == rows - 1:
                    down = [[d * (1.0 - last) for d in ds] for ds in down]
                for part in range(parts):
                    after = following(here[part])
                    across.append([after[0] - here[part][0], (after[1] - here[part][1]) * inner])
                for side in range(2):
                    power = 1.0
                    for part in range(parts):
                        power = power + down[part][side] * down[part][side] + across[part][side] * across[part][side]
                    inverse.append(lax.rsqrt(power))
                flux = [[d * i for d, i in zip(ds, inverse)] for ds in down]
                if before is not None:
                    for part in range(parts):
                        sides = [a * i for a, i in zip(across[part], inverse)]
                        earlier = preceding(sides)
                        for side in range(2):
                            spread = flux[part][side] - before[part][side] + sides[side] - earlier[side]
                            fresh = here[part][side] + 0.2 * spread
                            if sweep == ITERS:
                                out_ref[part * depth + s, pl.ds(side * rows + row, half, stride=2 * rows), :] = fresh
                            else:
                                field[row + halo, part, side] = fresh
                before = flux
                here = below
        return carry

    lax.fori_loop(0, depth, one_slice, 0)


def on_device(partials, inverses, classes):
    _, parts, depth, rows_total, width = partials.shape
    scans = lax.axis_size("scan")
    cuts = lax.axis_size("cuts")
    rows = rows_total // scans
    lanes = width // cuts
    kinds, total, _ = inverses.shape
    me = lax.axis_index("scan")
    core, y, x = me % 2, (me // 2) % 2, me // 4
    chips = scans // 4
    f32, f16 = jnp.float32, jnp.float16

    def pick(array, index, axis):
        return lax.dynamic_index_in_dim(array, index, axis, keepdims=False)

    def send(array, target):
        return lax.ppermute(array, "scan", [(i, target(i)) for i in range(scans)])

    def other_core(i):
        return i ^ 1

    def other_y(i):
        return i ^ 2

    def along_x(k):
        return lambda i: (i + 4 * k) % scans

    def add(*terms):
        return sum(t.astype(f32) for t in terms)

    split = partials.reshape(parts, depth, chips, 2, 2, rows, width)

    give = pick(split, 1 - core, 4)
    mine = pick(split, core, 4)
    far = send(pick(give[1], 1 - y, 2), other_core)
    all_x = send(give[0], other_core)
    near = send(pick(give[1], y, 2), other_core)

    away = (add(pick(mine[1], 1 - y, 2), far) * SUM_SCALE).astype(f16)
    came = send(away, other_y)

    sums = [
        (add(pick(mine[0], (x + k) % chips, 1), pick(all_x, (x + k) % chips, 1)) * SUM_SCALE).astype(f16)
        for k in range(1, chips)
    ]
    order = sorted(range(1, chips), key=lambda k: abs(k - chips // 2))
    from_x = [send(sums[k - 1], along_x(k)) for k in order]
    kept = add(pick(mine[0], x, 1), pick(all_x, x, 1)) * SUM_SCALE
    over_x = kept + add(*from_x)
    from_y = send(pick(over_x, 1 - y, 1).astype(f16), other_y)
    part0 = pick(over_x, y, 1) + from_y.astype(f32)

    own = add(pick(mine[1], y, 2), near) * SUM_SCALE
    over_y = own + came.astype(f32)
    sent = [send(pick(over_y, (x + k) % chips, 1).astype(f16), along_x(k)) for k in order]
    part1 = pick(over_y, x, 1) + add(*sent)

    grad = (jnp.stack([part0, part1]) * (1.0 / SUM_SCALE)).astype(jnp.bfloat16)
    grad = grad.reshape(parts, depth, rows, cuts, lanes).transpose(3, 0, 1, 2, 4)
    grad = lax.all_to_all(grad, "cuts", 0, 0, tiled=True)
    weights = inverses.reshape(kinds, cuts, depth, total).transpose(2, 1, 0, 3).reshape(total, kinds * total)
    per = rows * parts * depth
    filtered = pl.pallas_call(
        filter_kernel,
        out_shape=jax.ShapeDtypeStruct((cuts * per, lanes), f32),
        scratch_shapes=[pltpu.VMEM((parts, total * rows, lanes), f32)],
        compiler_params=pltpu.CompilerParams(vmem_limit_bytes=32 * 1024 * 1024),
    )(grad, weights, classes)
    coded = (filtered * SCALE).astype(f16).reshape(cuts, per, lanes)
    coded = lax.all_to_all(coded, "cuts", 0, 0, tiled=True)
    skipped = (rows - ITERS) * parts * depth // TILE * TILE
    needed = -(-ITERS * parts * depth // TILE) * TILE
    above = lax.ppermute(coded[:, skipped:], "scan", [(i, i + 1) for i in range(scans - 1)])
    below = lax.ppermute(coded[:, :needed], "scan", [(i + 1, i) for i in range(scans - 1)])
    above, middle, below = [
        (c.astype(f32) * (1.0 / SCALE)).reshape(-1, lanes) for c in (above, coded, below)
    ]
    shape = (cuts, parts, depth, rows, lanes)
    result = pl.pallas_call(
        lambda *refs: tv_kernel(shape, skipped, *refs),
        out_shape=jax.ShapeDtypeStruct((parts * depth, cuts * rows, lanes), f32),
        scratch_shapes=[pltpu.VMEM((rows + 2 * ITERS, parts, 2, cuts // 2, lanes), f32)],
        compiler_params=pltpu.CompilerParams(vmem_limit_bytes=32 * 1024 * 1024),
    )(above, middle, below)
    result = result.reshape(parts, depth, cuts, rows, lanes).transpose(0, 1, 3, 2, 4)
    return result.reshape(parts, depth, rows, width)


def solution(mesh):
    placed = (P("scan", None, "cuts", None, None), P(), P("scan", "cuts"))
    return jax.shard_map(
        on_device,
        mesh=mesh,
        in_specs=placed,
        out_specs=P(None, "cuts", "scan", None),
        check_vma=False,
    )
```

time: 123 us -> 109 us (0.89)
  blocking collectives: 57.5 us -> 15.9 us
  waiting for transfers between devices: 21.8 us -> 36.6 us
  starting transfers between devices: 22.9 us -> 30.4 us
  other arithmetic: 5.1 us -> 7.24 us
  Pallas kernels: 9.88 us -> 11.6 us
    all_to_all x1 -> x0, blocking collectives: 39.8 us -> none  [on_device(): lax.all_to_all(pair, 'scan', 0, 0, axis_index_groups=groups, tiled=True)]
    ppermute x3 -> x13, waiting for transfers between devices: 12.2 us -> 26.2 us  [the longest x11 20.6 us: send(): return lax.ppermute(array, 'scan', [(i, target(i)) for i in range(scans)])]
    ppermute x3 -> x13, starting transfers between devices: 12.2 us -> 19.4 us  [the longest x11 10.4 us: send(): return lax.ppermute(array, 'scan', [(i, target(i)) for i in range(scans)])]
    transpose x1, other arithmetic: 4.18 us -> 0.82 us  [on_device(): grad.reshape(parts, depth, rows, cuts, lanes).transpose(3, 0, 1, 2, 4)]
    add x0 -> x2, other arithmetic: none -> 3.05 us  [the longest x1 1.75 us: on_device(): over_y = own + came.astype(f32)]
    convert_element_type x1 -> x5, other arithmetic: 0.09 us -> 3.03 us  [the longest x1 1.66 us: on_device(): (add(pick(mine[0], (x + k) % chips, 1), pick(all_x, (x + k) % chips, 1))...]
    dynamic_slice x0 -> x1, local copies, waits for them, and re-layouts: none -> 2.09 us  [pick(): return lax.dynamic_index_in_dim(array, index, axis, keepdims=False)]
    transpose x3 -> x1, local copies, waits for them, and re-layouts: 2.04 us -> 0.04 us  [on_device(): inverses.reshape(kinds, cuts, depth, total).transpose(2, 1, 0, 3)]
  transfers between devices with their start and end apart: 4 -> 14, of which waited for: 4 -> 8; matrix products, arithmetic and copies ran while one was open for 1% -> 9% of each run, Pallas kernels for 0% -> 0%
where the time goes in v2:
time: 109 us; the launch traced here: 108 us
  waiting for transfers between devices  36.6 us (34%)
  starting transfers between devices  30.4 us (28%)
  blocking collectives  15.9 us (15%)
  Pallas kernels  11.6 us (11%)
  other arithmetic  7.24 us (7%)
  local copies, waits for them, and re-layouts  5.8 us (5%)
    ppermute x11, waiting for transfers between devices, send(): return lax.ppermute(array, 'scan', [(i, target(i)) for i in range(scans)])  20.6 us
    all_to_all x1, blocking collectives, on_device(): coded = lax.all_to_all(coded, 'cuts', 0, 0, tiled=True)  15.9 us
    all_to_all x1, starting transfers between devices, on_device(): grad = lax.all_to_all(grad, 'cuts', 0, 0, tiled=True)  10.9 us
    pallas_call x1, Pallas kernels, on_device(): pl.pallas_call(lambda *refs: tv_kernel(shape, skipped, *refs), out_shape=...  10.7 us
    ppermute x11, starting transfers between devices, send(): return lax.ppermute(array, 'scan', [(i, target(i)) for i in range(scans)])  10.4 us
    all_to_all x1, waiting for transfers between devices, on_device(): grad = lax.all_to_all(grad, 'cuts', 0, 0, tiled=True)  10.4 us
    ppermute x1, starting transfers between devices, on_device(): lax.ppermute(coded[:, skipped:], 'scan', [(i, i + 1) for i in range(scans...  7.1 us
    ppermute x1, waiting for transfers between devices, on_device(): lax.ppermute(coded[:, :needed], 'scan', [(i + 1, i) for i in range(scans...  4.34 us
  transfers between devices with their start and end apart: 14, of which 8 were waited for; matrix products, arithmetic and copies ran while one was open for 9% of the time, Pallas kernels for 0%

profile of v2, /device:TPU:1, one launch (start us, length us, event | category | flops | bytes accessed | tf_op | source)
XLA Modules:
  0.0 107.7 jit_solution(16104508452329847603)
XLA Ops:
  0.0 2.1 %constant_dynamic-slice_fusion.1 = (bf16[1,6,4,1,1,8,2048]{6,5,4,3,2,1,0:T(8,128)(2,1)S(1)}, bf16[6,4,8,2048]{3,2,1,0:T(8,128)(2,1)S(1)}, bf16[6,4,8,2048]{3,2,1...) fusion(bf16[2,6,4,2,2,8,2048]{6,5,4,3,2,1,0:T(8,128)(2,1)} %bitcast.114, s32[]{:T(128)S(6)} %add.158, ...), kind=kLoop, calls=%fused_computation.49 | loop fusion | bytes 6291476 | tf_op jit(solution)/shard_map/jit(dynamic_index_in_dim)/dynamic_slice | solution.py:127
  2.2 3.3 %collective-permute-start.6 = (bf16[6,4,8,2048]{3,2,0,1:T(8,128)(2,1)S(1)}, bf16[6,4,8,2048]{3,2,0,1:T(8,128)(2,1)S(1)}, u32[]{:S(2)}, u32[]{:S(2)}) collective-permute-start(bf16[6,4,8,2048]{3,2,0,1:T(8,128)(2,1)S(1)} %copy.28), channel_id=1, source_target_pairs={{0,16},{16,0},{32,48},{48,32},{64,80},{80,64},{96,112},{112,96},{1... | collective-permute-start | bytes 2359304 | tf_op jit(solution)/shard_map/ppermute | solution.py:130
  5.5 2.8 %dynamic-slice_bitcast_fusion = bf16[6,4,2,8,2048]{4,3,2,1,0:T(8,128)(2,1)} fusion(bf16[2,6,4,2,2,8,2048]{6,5,4,3,2,1,0:T(8,128)(2,1)} %bitcast.115, s32[]{:T(128)S(6)} %select_n.87), kind=kLoop, calls=%fused_computation | loop fusion | bytes 3145732 | tf_op jit(solution)/shard_map/squeeze | solution.py:149
  8.3 0.6 collective-permute-start.5
  8.9 1.2 %fusion.1 = f16[6,4,8,2048]{3,2,0,1:T(8,128)(2,1)} fusion(bf16[6,4,8,2048]{3,2,0,1:T(8,128)(2,1)S(1)} %collective-permute-done.6, bf16[1,6,4,1,1,8,2048]{6,5,4,3,2,1,0:T(8,128)(2,1)S(1)} %get-tuple-element.11), kind=kLoop, calls=%fused_computation.3 | loop fusion | flops 1966080 | bytes 2359296 | tf_op jit(solution)/shard_map/convert_element_type | solution.py:152
  10.1 2.2 %collective-permute-done = bf16[6,4,2,8,2048]{4,3,2,1,0:T(8,128)(2,1)S(1)} collective-permute-done((bf16[6,4,2,8,2048]{4,3,2,1,0:T(8,128)(2,1)}, bf16[6,4,2,8,2048]{4,3,2,1,0:T(8,128)(2,1)S(1)}, u32[]{:S(2)}, u32[]{:S(2)}) %collective-permute-start) | collective-permute-done | bytes 1572896 | tf_op jit(solution)/shard_map/ppermute | solution.py:130
  12.3 1.7 %fusion.10 = (f16[6,2,8,2048]{3,2,1,0:T(8,128)(2,1)S(1)}, f16[6,2,8,2048]{3,2,1,0:T(8,128)(2,1)S(1)}, f16[6,2,8,2048]{3,2,1,0:T(8,128)(2,1)S(1)}) fusion(bf16[2,6,4,2,2,8,2048]{6,5,4,3,2,1,0:T(8,128)(2,1)} %bitcast.116, s32[]{:T(128)S(6)} %select_n.89, s32[]{:T(128)S(6)} %select_n.84, bf16[6,4,2,8,2048]{4,3,2,1,0:T(8,128)(2,1)S(1)} %collective-permute-done, ...), kind=kLoop, calls=%fused_computation.21 | loop fusion | flops 2949120 | bytes 3538960 | tf_op jit(solution)/shard_map/convert_element_type | solution.py:156
  14.0 0.8 collective-permute-start.3
  14.8 0.7 collective-permute-start.2
  15.5 1.0 collective-permute-start.1
  16.5 13.1 %collective-permute-done.7 = f16[6,4,8,2048]{3,2,0,1:T(8,128)(2,1)} collective-permute-done((f16[6,4,8,2048]{3,2,0,1:T(8,128)(2,1)}, f16[6,4,8,2048]{3,2,0,1:T(8,128)(2,1)}, u32[]{:S(2)}, u32[]{:S(2)}) %collective-permute-start.7) | collective-permute-done | bytes 786464 | tf_op jit(solution)/shard_map/ppermute | solution.py:130
  29.6 1.7 %fusion.3 = f32[6,4,8,2048]{3,2,0,1:T(8,128)S(1)} fusion(f16[6,4,8,2048]{3,2,0,1:T(8,128)(2,1)} %collective-permute-done.7, bf16[6,4,8,2048]{3,2,0,1:T(8,128)(2,1)} %collective-permute-done.5, bf16[1,6,4,1,1,8,2048]{6,5,4,3,2,1,0:T(8,128)(2,1)S(1)} %get-tuple-element.8), kind=kLoop, calls=%fused_computation.6 | loop fusion | flops 2359296 | bytes 3932160 | tf_op jit(solution)/shard_map/add | solution.py:167
  31.4 0.8 collective-permute-start.10
  32.2 0.7 collective-permute-start.9
  33.0 1.0 collective-permute-start.8
  34.0 1.3 %fusion.12 = f32[6,2,8,2048]{3,2,1,0:T(8,128)S(1)} fusion(f16[6,2,8,2048]{3,2,1,0:T(8,128)(2,1)S(1)} %collective-permute-done.3, f16[6,2,8,2048]{3,2,1,0:T(8,128)(2,1)S(1)} %collective-permute-done.2, f16[6,2,8,2048]{3,2,1,0:T(8,128)(2,1)S(1)} %collective-permute-done.1, bf16[2,6,4,2,2,8,2048]{6,5,4,3,2,1,0:T(8,128)(2,1)} %bitcast.117, s32[]{:T(128)S(6)} %select_n.86, ...), kind=kLoop, calls=%fused_computation.24 | loop fusion | flops 1966080 | bytes 2752520 | tf_op jit(solution)/shard_map/add | solution.py:162
  35.3 1.4 %collective-permute-start.4 = (f16[6,8,2048]{2,1,0:T(8,128)(2,1)S(1)}, f16[6,8,2048]{2,1,0:T(8,128)(2,1)S(1)}, u32[]{:S(2)}, u32[]{:S(2)}) collective-permute-start(f16[6,8,2048]{2,1,0:T(8,128)(2,1)S(1)} %fusion.16), channel_id=1, source_target_pairs={{0,32},{16,48},{32,0},{48,16},{64,96},{80,112},{96,64},{112,80},{1... | collective-permute-start | bytes 589832 | tf_op jit(solution)/shard_map/ppermute | solution.py:130
  36.7 0.4 collective-permute-done.10
  37.1 2.6 %collective-permute-done.9 = f16[6,8,2048]{2,1,0:T(8,128)(2,1)S(1)} collective-permute-done((f16[6,8,2048]{2,1,0:T(8,128)(2,1)S(1)}, f16[6,8,2048]{2,1,0:T(8,128)(2,1)S(1)}, u32[]{:S(2)}, u32[]{:S(2)}) %collective-permute-start.9) | collective-permute-done | bytes 196640 | tf_op jit(solution)/shard_map/ppermute | solution.py:130
  39.7 2.4 %collective-permute-done.8 = f16[6,8,2048]{2,1,0:T(8,128)(2,1)S(1)} collective-permute-done((f16[6,8,2048]{2,1,0:T(8,128)(2,1)S(1)}, f16[6,8,2048]{2,1,0:T(8,128)(2,1)S(1)}, u32[]{:S(2)}, u32[]{:S(2)}) %collective-permute-start.8) | collective-permute-done | bytes 196640 | tf_op jit(solution)/shard_map/ppermute | solution.py:130
  42.7 0.8 fusion.13
  43.5 10.9 %all-to-all-start = ((bf16[16,2,6,8,128]{4,3,2,1,0:T(8,128)(2,1)}), bf16[16,2,6,8,128]{4,3,2,1,0:T(8,128)(2,1)S(1)}, u32[]{:S(2)}, u32[]{:S(2)}) async-start(bf16[16,2,6,8,128]{4,3,2,1,0:T(8,128)(2,1)} %fusion.13), calls=%async_computation | async-start | bytes 786432 | tf_op jit(solution)/shard_map/all_to_all | solution.py:173
  54.6 0.2 reshape.82.weights_ref
  54.8 10.4 %all-to-all-done.grad_ref = bf16[16,2,6,8,128]{4,3,2,1,0:T(8,128)(2,1)S(1)} async-done(((bf16[16,2,6,8,128]{4,3,2,1,0:T(8,128)(2,1)}), bf16[16,2,6,8,128]{4,3,2,1,0:T(8,128)(2,1)S(1)}, u32[]{:S(2)}, u32[]{:S(2)}) %all-to-all-start) | async-done | bytes 393248 | tf_op jit(solution)/shard_map/all_to_all | solution.py:173
  65.1 0.9 shard_map.37
  66.1 15.9 %all_to_all.10 = f16[16,96,128]{2,1,0:T(8,128)(2,1)S(1)} all-to-all(f16[16,96,128]{2,1,0:T(8,128)(2,1)S(1)} %bitcast.120), channel_id=1, replica_groups=mesh['scan'=16,'cuts'=16] {'cuts'}, dimensions={0} | all-to-all | bytes 786432 | tf_op jit(solution)/shard_map/all_to_all | solution.py:183
  82.0 0.1 fusion.20
  82.1 7.1 %collective-permute-start.11 = (f16[16,64,128]{2,1,0:T(8,128)(2,1)S(1)}, f16[16,64,128]{2,1,0:T(8,128)(2,1)S(1)}, u32[]{:S(2)}, u32[]{:S(2)}) collective-permute-start(f16[16,64,128]{2,1,0:T(8,128)(2,1)S(1)} %get-tuple-element.16), channel_id=1, source_target_pairs={{0,16},{16,32},{32,48},{48,64},{64,80},{80,96},{96,112},{112,128},... | collective-permute-start | bytes 786440 | tf_op jit(solution)/shard_map/ppermute | solution.py:186
  89.3 1.9 %collective-permute-start.12 = (f16[16,64,128]{2,1,0:T(8,128)(2,1)S(1)}, f16[16,64,128]{2,1,0:T(8,128)(2,1)S(1)}, u32[]{:S(2)}, u32[]{:S(2)}) collective-permute-start(f16[16,64,128]{2,1,0:T(8,128)(2,1)S(1)} %get-tuple-element.15), channel_id=1, source_target_pairs={{16,0},{32,16},{48,32},{64,48},{80,64},{96,80},{112,96},{128,112},... | collective-permute-start | bytes 786440 | tf_op jit(solution)/shard_map/ppermute | solution.py:187
  91.3 1.3 %collective-permute-done.11 = f16[16,64,128]{2,1,0:T(8,128)(2,1)S(1)} collective-permute-done((f16[16,64,128]{2,1,0:T(8,128)(2,1)S(1)}, f16[16,64,128]{2,1,0:T(8,128)(2,1)S(1)}, u32[]{:S(2)}, u32[]{:S(2)}) %collective-permute-start.11) | collective-permute-done | bytes 262176 | tf_op jit(solution)/shard_map/ppermute | solution.py:186
  92.6 4.3 %collective-permute-done.12 = f16[16,64,128]{2,1,0:T(8,128)(2,1)S(1)} collective-permute-done((f16[16,64,128]{2,1,0:T(8,128)(2,1)S(1)}, f16[16,64,128]{2,1,0:T(8,128)(2,1)S(1)}, u32[]{:S(2)}, u32[]{:S(2)}) %collective-permute-start.12) | collective-permute-done | bytes 262176 | tf_op jit(solution)/shard_map/ppermute | solution.py:187
  97.0 10.7 %shard_map.38 = f32[12,128,128]{2,1,0:T(8,128)} custom-call(f32[1024,128]{1,0:T(8,128)S(1)} %bitcast.112, f32[1536,128]{1,0:T(8,128)S(1)} %bitcast.111, f32[1024,128]{1,0:T(8,128)S(1)} %bitcast.113), custom_call_target="tpu_custom_call" | custom-call | tf_op jit(solution)/shard_map/pallas_call | solution.py:192
  (28 shorter events, 1.2 us)
Async XLA Ops:
  2.2 6.8 %collective-permute-start.6 = (bf16[6,4,8,2048]{3,2,0,1:T(8,128)(2,1)S(1)}, bf16[6,4,8,2048]{3,2,0,1:T(8,128)(2,1)S(1)}, u32[]{:S(2)}, u32[]{:S(2)}) collective-permute-start(bf16[6,4,8,2048]{3,2,0,1:T(8,128)(2,1)S(1)} %copy.28), channel_id=1, source_target_pairs={{0,16},{16,0},{32,48},{48,32},{64,80},{80,64},{96,112},{112,96},{1... | collective-permute-start | bytes 2359304 | tf_op jit(solution)/shard_map/ppermute | solution.py:130
  8.2 4.0 %collective-permute-start = (bf16[6,4,2,8,2048]{4,3,2,1,0:T(8,128)(2,1)}, bf16[6,4,2,8,2048]{4,3,2,1,0:T(8,128)(2,1)S(1)}, u32[]{:S(2)}, u32[]{:S(2)}) collective-permute-start(bf16[6,4,2,8,2048]{4,3,2,1,0:T(8,128)(2,1)} %dynamic-slice_bitcast_fusion), channel_id=1, source_target_pairs={{0,16},{16,0},{32,48},{48,32},{64,80},{80,64},{96,112},{112,96},{1... | collective-permute-start | bytes 4718600 | tf_op jit(solution)/shard_map/ppermute | solution.py:130
  8.3 8.2 %collective-permute-start.5 = (bf16[6,4,8,2048]{3,2,0,1:T(8,128)(2,1)S(1)}, bf16[6,4,8,2048]{3,2,0,1:T(8,128)(2,1)}, u32[]{:S(2)}, u32[]{:S(2)}) collective-permute-start(bf16[6,4,8,2048]{3,2,0,1:T(8,128)(2,1)S(1)} %copy.27), channel_id=1, source_target_pairs={{0,16},{16,0},{32,48},{48,32},{64,80},{80,64},{96,112},{112,96},{1... | collective-permute-start | bytes 2359304 | tf_op jit(solution)/shard_map/ppermute | solution.py:130
  10.1 19.5 %collective-permute-start.7 = (f16[6,4,8,2048]{3,2,0,1:T(8,128)(2,1)}, f16[6,4,8,2048]{3,2,0,1:T(8,128)(2,1)}, u32[]{:S(2)}, u32[]{:S(2)}) collective-permute-start(f16[6,4,8,2048]{3,2,0,1:T(8,128)(2,1)} %fusion.1), channel_id=1, source_target_pairs={{0,32},{16,48},{32,0},{48,16},{64,96},{80,112},{96,64},{112,80},{1... | collective-permute-start | bytes 2359304 | tf_op jit(solution)/shard_map/ppermute | solution.py:130
  14.0 19.0 %collective-permute-start.3 = (f16[6,2,8,2048]{3,2,1,0:T(8,128)(2,1)S(1)}, f16[6,2,8,2048]{3,2,1,0:T(8,128)(2,1)S(1)}, u32[]{:S(2)}, u32[]{:S(2)}) collective-permute-start(f16[6,2,8,2048]{3,2,1,0:T(8,128)(2,1)S(1)} %get-tuple-element.7), channel_id=1, source_target_pairs={{0,192},{16,208},{32,224},{48,240},{64,0},{80,16},{96,32},{112,48}... | collective-permute-start | bytes 1179656 | tf_op jit(solution)/shard_map/ppermute | solution.py:130
  14.8 19.2 %collective-permute-start.2 = (f16[6,2,8,2048]{3,2,1,0:T(8,128)(2,1)S(1)}, f16[6,2,8,2048]{3,2,1,0:T(8,128)(2,1)S(1)}, u32[]{:S(2)}, u32[]{:S(2)}) collective-permute-start(f16[6,2,8,2048]{3,2,1,0:T(8,128)(2,1)S(1)} %get-tuple-element.6), channel_id=1, source_target_pairs={{0,64},{16,80},{32,96},{48,112},{64,128},{80,144},{96,160},{112,17... | collective-permute-start | bytes 1179656 | tf_op jit(solution)/shard_map/ppermute | solution.py:130
  15.5 18.5 %collective-permute-start.1 = (f16[6,2,8,2048]{3,2,1,0:T(8,128)(2,1)S(1)}, f16[6,2,8,2048]{3,2,1,0:T(8,128)(2,1)S(1)}, u32[]{:S(2)}, u32[]{:S(2)}) collective-permute-start(f16[6,2,8,2048]{3,2,1,0:T(8,128)(2,1)S(1)} %get-tuple-element.5), channel_id=1, source_target_pairs={{0,128},{16,144},{32,160},{48,176},{64,192},{80,208},{96,224},{112... | collective-permute-start | bytes 1179656 | tf_op jit(solution)/shard_map/ppermute | solution.py:130
  31.4 5.7 %collective-permute-start.10 = (f16[6,8,2048]{2,1,0:T(8,128)(2,1)S(1)}, f16[6,8,2048]{2,1,0:T(8,128)(2,1)S(1)}, u32[]{:S(2)}, u32[]{:S(2)}) collective-permute-start(f16[6,8,2048]{2,1,0:T(8,128)(2,1)S(1)} %get-tuple-element.13), channel_id=1, source_target_pairs={{0,192},{16,208},{32,224},{48,240},{64,0},{80,16},{96,32},{112,48}... | collective-permute-start | bytes 589832 | tf_op jit(solution)/shard_map/ppermute | solution.py:130
  32.2 7.5 %collective-permute-start.9 = (f16[6,8,2048]{2,1,0:T(8,128)(2,1)S(1)}, f16[6,8,2048]{2,1,0:T(8,128)(2,1)S(1)}, u32[]{:S(2)}, u32[]{:S(2)}) collective-permute-start(f16[6,8,2048]{2,1,0:T(8,128)(2,1)S(1)} %get-tuple-element.14), channel_id=1, source_target_pairs={{0,64},{16,80},{32,96},{48,112},{64,128},{80,144},{96,160},{112,17... | collective-permute-start | bytes 589832 | tf_op jit(solution)/shard_map/ppermute | solution.py:130
  33.0 9.1 %collective-permute-start.8 = (f16[6,8,2048]{2,1,0:T(8,128)(2,1)S(1)}, f16[6,8,2048]{2,1,0:T(8,128)(2,1)S(1)}, u32[]{:S(2)}, u32[]{:S(2)}) collective-permute-start(f16[6,8,2048]{2,1,0:T(8,128)(2,1)S(1)} %get-tuple-element.12), channel_id=1, source_target_pairs={{0,128},{16,144},{32,160},{48,176},{64,192},{80,208},{96,224},{112... | collective-permute-start | bytes 589832 | tf_op jit(solution)/shard_map/ppermute | solution.py:130
  35.3 7.1 %collective-permute-start.4 = (f16[6,8,2048]{2,1,0:T(8,128)(2,1)S(1)}, f16[6,8,2048]{2,1,0:T(8,128)(2,1)S(1)}, u32[]{:S(2)}, u32[]{:S(2)}) collective-permute-start(f16[6,8,2048]{2,1,0:T(8,128)(2,1)S(1)} %fusion.16), channel_id=1, source_target_pairs={{0,32},{16,48},{32,0},{48,16},{64,96},{80,112},{96,64},{112,80},{1... | collective-permute-start | bytes 589832 | tf_op jit(solution)/shard_map/ppermute | solution.py:130
  42.5 11.9 %copy-start.1 = (bf16[8,96,96]{2,1,0:T(8,128)(2,1)S(1)}, bf16[8,96,96]{2,1,0:T(8,128)(2,1)}, u32[]{:S(2)}) copy-start(bf16[8,96,96]{2,1,0:T(8,128)(2,1)} %param.4) | copy-start | bytes 442372
  42.7 22.4 %copy-start = (s32[8,128]{1,0:T(8,128)S(1)}, s32[8,128]{1,0:T(8,128)}, u32[]{:S(2)}) copy-start(s32[8,128]{1,0:T(8,128)} %classes_ref.1) | copy-start | bytes 12292
  43.5 21.6 %all-to-all-start = ((bf16[16,2,6,8,128]{4,3,2,1,0:T(8,128)(2,1)}), bf16[16,2,6,8,128]{4,3,2,1,0:T(8,128)(2,1)S(1)}, u32[]{:S(2)}, u32[]{:S(2)}) async-start(bf16[16,2,6,8,128]{4,3,2,1,0:T(8,128)(2,1)} %fusion.13), calls=%async_computation | async-start | bytes 786432 | tf_op jit(solution)/shard_map/all_to_all | solution.py:173
  82.1 10.4 %collective-permute-start.11 = (f16[16,64,128]{2,1,0:T(8,128)(2,1)S(1)}, f16[16,64,128]{2,1,0:T(8,128)(2,1)S(1)}, u32[]{:S(2)}, u32[]{:S(2)}) collective-permute-start(f16[16,64,128]{2,1,0:T(8,128)(2,1)S(1)} %get-tuple-element.16), channel_id=1, source_target_pairs={{0,16},{16,32},{32,48},{48,64},{64,80},{80,96},{96,112},{112,128},... | collective-permute-start | bytes 786440 | tf_op jit(solution)/shard_map/ppermute | solution.py:186
  89.3 7.7 %collective-permute-start.12 = (f16[16,64,128]{2,1,0:T(8,128)(2,1)S(1)}, f16[16,64,128]{2,1,0:T(8,128)(2,1)S(1)}, u32[]{:S(2)}, u32[]{:S(2)}) collective-permute-start(f16[16,64,128]{2,1,0:T(8,128)(2,1)S(1)} %get-tuple-element.15), channel_id=1, source_target_pairs={{16,0},{32,16},{48,32},{64,48},{80,64},{96,80},{112,96},{128,112},... | collective-permute-start | bytes 786440 | tf_op jit(solution)/shard_map/ppermute | solution.py:187

commit v3 on v2

--- a/solution.py
+++ b/solution.py
@@ -111,6 +111,41 @@
     lax.fori_loop(0, depth, one_slice, 0)
 
 
+def copy_kernel(plan, source_ref, *refs):
+    count = len(plan)
+    sems = refs[count]
+    me = lax.axis_index("scan")
+    core, y, x = lax.rem(me, 2), lax.rem(me // 2, 2), me // 4
+    chips = source_ref.shape[2]
+    copies = []
+    for out, (theirs, pieces) in zip(refs, plan):
+        whose = 1 - core if theirs else core
+        for slot, (part, k, e) in enumerate(pieces):
+            copies.append(
+                pltpu.make_async_copy(
+                    source_ref.at[part, :, lax.rem(x + k, chips), 1 - y if e else y, whose],
+                    out.at[slot],
+                    sems.at[len(copies)],
+                )
+            )
+    for copy in copies:
+        copy.start()
+    for copy in copies:
+        copy.wait()
+
+
+def copied(split, *plan):
+    _, depth, _, _, _, rows, width = split.shape
+    return pl.pallas_call(
+        lambda *refs: copy_kernel(plan, *refs),
+        out_shape=[jax.ShapeDtypeStruct((len(pieces), depth, rows, width), split.dtype) for _, pieces in plan],
+        in_specs=[pl.BlockSpec(memory_space=pltpu.HBM)],
+        out_specs=[pl.BlockSpec(memory_space=pl.ANY if theirs else pltpu.VMEM) for theirs, _ in plan],
+        scratch_shapes=[pltpu.SemaphoreType.DMA((sum(len(pieces) for _, pieces in plan),))],
+        compiler_params=pltpu.CompilerParams(vmem_limit_bytes=24 * 1024 * 1024),
+    )(split)
+
+
 def on_device(partials, inverses, classes):
     _, parts, depth, rows_total, width = partials.shape
     scans = lax.axis_size("scan")
@@ -118,16 +153,11 @@
     rows = rows_total // scans
     lanes = width // cuts
     kinds, total, _ = inverses.shape
-    me = lax.axis_index("scan")
-    core, y, x = me % 2, (me // 2) % 2, me // 4
     chips = scans // 4
     f32, f16 = jnp.float32, jnp.float16
 
-    def pick(array, index, axis):
-        return lax.dynamic_index_in_dim(array, index, axis, keepdims=False)
-
-    def send(array, target):
-        return lax.ppermute(array, "scan", [(i, target(i)) for i in range(scans)])
+    def send(array, target, order=1):
+        return lax.ppermute(array, "scan", [(i, target(i)) for i in range(scans)][::order])
 
     def other_core(i):
         return i ^ 1
@@ -138,40 +168,68 @@
     def along_x(k):
         return lambda i: (i + 4 * k) % scans
 
-    def add(*terms):
-        return sum(t.astype(f32) for t in terms)
+    def paired(own, got):
+        return (own.astype(f32) + got.astype(f32)) * SUM_SCALE
+
+    weights = inverses.reshape(kinds, cuts, depth, total).transpose(2, 1, 0, 3).reshape(total, kinds * total)
 
     split = partials.reshape(parts, depth, chips, 2, 2, rows, width)
-
-    give = pick(split, 1 - core, 4)
-    mine = pick(split, core, 4)
-    far = send(pick(give[1], 1 - y, 2), other_core)
-    all_x = send(give[0], other_core)
-    near = send(pick(give[1], y, 2), other_core)
-
-    away = (add(pick(mine[1], 1 - y, 2), far) * SUM_SCALE).astype(f16)
-    came = send(away, other_y)
-
-    sums = [
-        (add(pick(mine[0], (x + k) % chips, 1), pick(all_x, (x + k) % chips, 1)) * SUM_SCALE).astype(f16)
-        for k in range(1, chips)
+    split = pltpu.with_memory_space_constraint(split, pltpu.HBM)
+    odd = list(range(1, chips, 2))
+    even = list(range(2, chips, 2)) + [0]
+    along = [(0, k, e) for k in range(1, chips) for e in range(2)]
+    across_odd = [(1, k, 1) for k in odd]
+    across_even = [(1, k, 1) for k in even]
+    kept_along = [(0, 0, 0), (0, 0, 1)]
+    kept_odd = [(1, k, 0) for k in odd]
+    kept_even = [(1, k, 0) for k in even]
+    rest = across_even + kept_odd + kept_even + kept_along
+    give_odd, give_along = copied(split, (True, across_odd), (True, along))
+    got_odd = send(give_odd, other_core)
+    got_along = send(give_along, other_core, -1)
+    own_odd, own_along, own_even, own_kept_odd, own_kept_even, own_kept_along, give_rest = copied(
+        split,
+        (False, across_odd),
+        (False, along),
+        (False, across_even),
+        (False, kept_odd),
+        (False, kept_even),
+        (False, kept_along),
+        (True, rest),
+    )
+    got_rest = send(give_rest, other_core)
+    got_even, got_kept_odd, got_kept_even, got_kept_along = [
+        got_rest[2 * i : 2 * i + 2] for i in range(4)
     ]
-    order = sorted(range(1, chips), key=lambda k: abs(k - chips // 2))
-    from_x = [send(sums[k - 1], along_x(k)) for k in order]
-    kept = add(pick(mine[0], x, 1), pick(all_x, x, 1)) * SUM_SCALE
-    over_x = kept + add(*from_x)
-    from_y = send(pick(over_x, 1 - y, 1).astype(f16), other_y)
-    part0 = pick(over_x, y, 1) + from_y.astype(f32)
-
-    own = add(pick(mine[1], y, 2), near) * SUM_SCALE
-    over_y = own + came.astype(f32)
-    sent = [send(pick(over_y, (x + k) % chips, 1).astype(f16), along_x(k)) for k in order]
-    part1 = pick(over_y, x, 1) + add(*sent)
+
+    def after(value, made):
+        return lax.optimization_barrier((value, made))[0]
+
+    sums = paired(own_along, got_along).astype(f16)
+    from_x = [send(sums[2 * k - 2 : 2 * k], along_x(k)) for k in range(1, chips)]
+    odd_code = paired(own_odd, got_odd).astype(f16)
+    came_odd = send(odd_code, other_y)
+    even_code = paired(own_even, got_even).astype(f16)
+    came_even = send(even_code, other_y, -1)
+
+    came_odd = after(came_odd, even_code)
+    odd_sums = (paired(own_kept_odd, got_kept_odd) + came_odd.astype(f32)).astype(f16)
+    sent = [send(odd_sums[i], along_x(k), -1) for i, k in enumerate(odd)]
+
+    from_x = after(from_x, odd_sums)
+    over_x = paired(own_kept_along, got_kept_along) + sum(c.astype(f32) for c in from_x)
+    last = over_x[1].astype(f16)
+    part0 = over_x[0] + send(last, other_y).astype(f32)
+
+    came_even = after(came_even, last)
+    even_sums = paired(own_kept_even, got_kept_even) + came_even.astype(f32)
+    sent += [send(even_sums[i].astype(f16), along_x(k), -1) for i, k in enumerate(even[:-1])]
+    part1 = even_sums[len(even) - 1] + sum(c.astype(f32) for c in sent)
 
     grad = (jnp.stack([part0, part1]) * (1.0 / SUM_SCALE)).astype(jnp.bfloat16)
     grad = grad.reshape(parts, depth, rows, cuts, lanes).transpose(3, 0, 1, 2, 4)
+    grad, weights = lax.optimization_barrier((grad, weights))
     grad = lax.all_to_all(grad, "cuts", 0, 0, tiled=True)
-    weights = inverses.reshape(kinds, cuts, depth, total).transpose(2, 1, 0, 3).reshape(total, kinds * total)
     per = rows * parts * depth
     filtered = pl.pallas_call(
         filter_kernel,

time: 109 us -> 206 us (1.89)
  Pallas kernels: 11.6 us -> 109 us
  blocking collectives: 15.9 us -> 35.2 us
  waiting for transfers between devices: 36.6 us -> 26.3 us
  starting transfers between devices: 30.4 us -> 24.1 us
  local copies, waits for them, and re-layouts: 5.8 us -> 1.16 us
    pallas_call x0 -> x2, Pallas kernels: none -> 97.8 us  [copied(): pl.pallas_call(lambda *refs: copy_kernel(plan, *refs), out_shape=[jax.Sha...]
    all_to_all x0 -> x1, blocking collectives: none -> 19.5 us  [on_device(): grad = lax.all_to_all(grad, 'cuts', 0, 0, tiled=True)]
    all_to_all x1 -> x0, starting transfers between devices: 10.9 us -> none  [on_device(): grad = lax.all_to_all(grad, 'cuts', 0, 0, tiled=True)]
    all_to_all x1 -> x0, waiting for transfers between devices: 10.4 us -> none  [on_device(): grad = lax.all_to_all(grad, 'cuts', 0, 0, tiled=True)]
    ppermute x11 -> x12, starting transfers between devices: 10.4 us -> 14.7 us  [send(): lax.ppermute(array, 'scan', [(i, target(i)) for i in range(scans)][::order])]
    squeeze x3 -> x1, local copies, waits for them, and re-layouts: 2.88 us -> 0.07 us  [on_device(): sent = [send(odd_sums[i], along_x(k), -1) for i, k in enumerate(odd)]]
    convert_element_type x4 -> x6, other arithmetic: 2.95 us -> 5.23 us  [the longest x1 1.71 us: on_device(): sums = paired(own_along, got_along).astype(f16)]
    dynamic_slice x1 -> x0, local copies, waits for them, and re-layouts: 2.09 us -> none  [pick(): return lax.dynamic_index_in_dim(array, index, axis, keepdims=False)]
  transfers between devices with their start and end apart: 14 -> 14, of which waited for: 8 -> 9; matrix products, arithmetic and copies ran while one was open for 9% -> 4% of each run, Pallas kernels for 0% -> 24%
where the time goes in v3:
time: 206 us; the launch traced here: 205 us
  Pallas kernels  109 us (53%)
  blocking collectives  35.2 us (17%)
  waiting for transfers between devices  26.3 us (13%)
  starting transfers between devices  24.1 us (12%)
  other arithmetic  8.15 us (4%)
    pallas_call x2, Pallas kernels, copied(): pl.pallas_call(lambda *refs: copy_kernel(plan, *refs), out_shape=[jax.Sha...  97.8 us
    ppermute x12, waiting for transfers between devices, send(): lax.ppermute(array, 'scan', [(i, target(i)) for i in range(scans)][::order])  20.7 us
    all_to_all x1, blocking collectives, on_device(): grad = lax.all_to_all(grad, 'cuts', 0, 0, tiled=True)  19.5 us
    all_to_all x1, blocking collectives, on_device(): coded = lax.all_to_all(coded, 'cuts', 0, 0, tiled=True)  15.7 us
    ppermute x12, starting transfers between devices, send(): lax.ppermute(array, 'scan', [(i, target(i)) for i in range(scans)][::order])  14.7 us
    pallas_call x1, Pallas kernels, on_device(): pl.pallas_call(lambda *refs: tv_kernel(shape, skipped, *refs), out_shape=...  10.7 us
    ppermute x1, starting transfers between devices, on_device(): lax.ppermute(coded[:, skipped:], 'scan', [(i, i + 1) for i in range(scans...  7.42 us
    ppermute x1, waiting for transfers between devices, on_device(): lax.ppermute(coded[:, :needed], 'scan', [(i + 1, i) for i in range(scans...  4.34 us
  transfers between devices with their start and end apart: 14, of which 9 were waited for; matrix products, arithmetic and copies ran while one was open for 4% of the time, Pallas kernels for 24%

profile of v3, /device:TPU:1, one launch (start us, length us, event | category | flops | bytes accessed | tf_op | source)
XLA Modules:
  0.0 204.5 jit_solution(1945604325966855463)
XLA Ops:
  0.0 48.8 %shard_map.38 = (bf16[2,6,8,2048]{3,2,1,0:T(8,128)(2,1)}, bf16[6,6,8,2048]{3,2,1,0:T(8,128)(2,1)}) custom-call(bf16[2,6,4,2,2,8,2048]{6,5,4,3,2,1,0:T(8,128)(2,1)} %bitcast.54), custom_call_target="tpu_custom_call" | custom-call | tf_op jit(solution)/shard_map/pallas_call | solution.py:139
  48.8 3.3 %collective-permute-start.1 = (bf16[6,6,8,2048]{3,2,1,0:T(8,128)(2,1)}, bf16[6,6,8,2048]{3,2,1,0:T(8,128)(2,1)}, u32[]{:S(2)}, u32[]{:S(2)}) collective-permute-start(bf16[6,6,8,2048]{3,2,1,0:T(8,128)(2,1)} %get-tuple-element.24), channel_id=1, source_target_pairs={{240,224},{224,240},{208,192},{192,208},{176,160},{160,176},{144,1... | collective-permute-start | bytes 3538952 | tf_op jit(solution)/shard_map/ppermute | solution.py:160
  52.3 49.0 %shard_map.37 = (bf16[2,6,8,2048]{3,2,1,0:T(8,128)(2,1)S(1)}, bf16[6,6,8,2048]{3,2,1,0:T(8,128)(2,1)S(1)}, bf16[2,6,8,2048]{3,2,1,0:T(8,128)(2,1)S(1)}, bf16[2,6...) custom-call(bf16[2,6,4,2,2,8,2048]{6,5,4,3,2,1,0:T(8,128)(2,1)} %bit, ...), custom_call_target="tpu_custom_call" | custom-call | tf_op jit(solution)/shard_map/pallas_call | solution.py:139
  101.2 0.5 collective-permute-start
  102.0 1.1 multiply_convert_fusion.3
  103.3 1.7 multiply_convert_fusion
  105.0 0.3 fusion.8
  105.3 0.9 collective-permute-start.2
  106.1 2.5 %collective-permute-start.3 = (f16[2,6,8,2048]{3,2,1,0:T(8,128)(2,1)S(1)}, f16[2,6,8,2048]{3,2,1,0:T(8,128)(2,1)S(1)}, u32[]{:S(2)}, u32[]{:S(2)}) collective-permute-start(f16[2,6,8,2048]{3,2,1,0:T(8,128)(2,1)S(1)} %get-tuple-element.38), channel_id=1, source_target_pairs={{0,128},{16,144},{32,160},{48,176},{64,192},{80,208},{96,224},{112... | collective-permute-start | bytes 1179656 | tf_op jit(solution)/shard_map/ppermute | solution.py:160
  108.6 1.2 collective-permute-start.4
  109.7 1.1 multiply_convert_fusion.2
  110.9 0.3 collective-permute-start.8
  111.1 2.8 %collective-permute-done.6 = f16[2,6,8,2048]{3,2,1,0:T(8,128)(2,1)S(1)} collective-permute-done((f16[2,6,8,2048]{3,2,1,0:T(8,128)(2,1)S(1)}, f16[2,6,8,2048]{3,2,1,0:T(8,128)(2,1)S(1)}, u32[]{:S(2)}, u32[]{:S(2)}) %collective-permute-start.6) | collective-permute-done | bytes 393248 | tf_op jit(solution)/shard_map/ppermute | solution.py:160
  114.0 1.2 add_convert_fusion
  115.2 2.1 %collective-permute-done.2 = f16[2,6,8,2048]{3,2,1,0:T(8,128)(2,1)S(1)} collective-permute-done((f16[2,6,8,2048]{3,2,1,0:T(8,128)(2,1)S(1)}, f16[2,6,8,2048]{3,2,1,0:T(8,128)(2,1)S(1)}, u32[]{:S(2)}, u32[]{:S(2)}) %collective-permute-start.2) | collective-permute-done | bytes 393248 | tf_op jit(solution)/shard_map/ppermute | solution.py:160
  117.3 8.6 %collective-permute-done.3 = f16[2,6,8,2048]{3,2,1,0:T(8,128)(2,1)S(1)} collective-permute-done((f16[2,6,8,2048]{3,2,1,0:T(8,128)(2,1)S(1)}, f16[2,6,8,2048]{3,2,1,0:T(8,128)(2,1)S(1)}, u32[]{:S(2)}, u32[]{:S(2)}) %collective-permute-start.3) | collective-permute-done | bytes 393248 | tf_op jit(solution)/shard_map/ppermute | solution.py:160
  126.0 1.3 add_add_fusion
  127.3 1.2 collective-permute-start.7
  128.6 3.4 %collective-permute-start.10 = (f16[6,8,2048]{2,1,0:T(8,128)(2,1)S(1)}, f16[6,8,2048]{2,1,0:T(8,128)(2,1)S(1)}, u32[]{:S(2)}, u32[]{:S(2)}) collective-permute-start(f16[6,8,2048]{2,1,0:T(8,128)(2,1)S(1)} %get-tuple-element.43), channel_id=1, source_target_pairs={{240,176},{224,160},{208,144},{192,128},{176,112},{160,96},{144,80... | collective-permute-start | bytes 589832 | tf_op jit(solution)/shard_map/ppermute | solution.py:160
  132.1 1.2 convert_add_fusion
  133.2 1.4 collective-permute-start.11
  134.9 0.6 collective-permute-done.10
  135.5 4.1 %collective-permute-done.9 = f16[6,8,2048]{2,1,0:T(8,128)(2,1)S(1)} collective-permute-done((f16[6,8,2048]{2,1,0:T(8,128)(2,1)S(1)}, f16[6,8,2048]{2,1,0:T(8,128)(2,1)S(1)}, u32[]{:S(2)}, u32[]{:S(2)}) %collective-permute-start.9) | collective-permute-done | bytes 196640 | tf_op jit(solution)/shard_map/ppermute | solution.py:160
  139.6 2.3 %collective-permute-done.11 = f16[6,8,2048]{2,1,0:T(8,128)(2,1)S(1)} collective-permute-done((f16[6,8,2048]{2,1,0:T(8,128)(2,1)S(1)}, f16[6,8,2048]{2,1,0:T(8,128)(2,1)S(1)}, u32[]{:S(2)}, u32[]{:S(2)}) %collective-permute-start.11) | collective-permute-done | bytes 196640 | tf_op jit(solution)/shard_map/ppermute | solution.py:160
  142.3 19.5 %all_to_all.10.grad_ref = bf16[16,2,6,8,128]{4,3,2,1,0:T(8,128)(2,1)S(1)} all-to-all(bf16[16,2,6,8,128]{4,3,2,1,0:T(8,128)(2,1)S(1)} %fusion.1), channel_id=1, replica_groups=mesh['scan'=16,'cuts'=16] {'cuts'}, dimensions={0} | all-to-all | bytes 786432 | tf_op jit(solution)/shard_map/all_to_all | solution.py:232
  161.8 0.9 shard_map.39
  162.8 15.7 %all_to_all.11 = f16[16,96,128]{2,1,0:T(8,128)(2,1)S(1)} all-to-all(f16[16,96,128]{2,1,0:T(8,128)(2,1)S(1)} %bitcast.58), channel_id=1, replica_groups=mesh['scan'=16,'cuts'=16] {'cuts'}, dimensions={0} | all-to-all | bytes 786432 | tf_op jit(solution)/shard_map/all_to_all | solution.py:241
  178.6 7.4 %collective-permute-start.12 = (f16[16,64,128]{2,1,0:T(8,128)(2,1)S(1)}, f16[16,64,128]{2,1,0:T(8,128)(2,1)S(1)}, u32[]{:S(2)}, u32[]{:S(2)}) collective-permute-start(f16[16,64,128]{2,1,0:T(8,128)(2,1)S(1)} %get-tuple-element.41), channel_id=1, source_target_pairs={{0,16},{16,32},{32,48},{48,64},{64,80},{80,96},{96,112},{112,128},... | collective-permute-start | bytes 786440 | tf_op jit(solution)/shard_map/ppermute | solution.py:244
  186.1 1.9 collective-permute-start.13
  188.1 1.3 collective-permute-done.12
  189.4 4.3 %collective-permute-done.13 = f16[16,64,128]{2,1,0:T(8,128)(2,1)S(1)} collective-permute-done((f16[16,64,128]{2,1,0:T(8,128)(2,1)S(1)}, f16[16,64,128]{2,1,0:T(8,128)(2,1)S(1)}, u32[]{:S(2)}, u32[]{:S(2)}) %collective-permute-start.13) | collective-permute-done | bytes 262176 | tf_op jit(solution)/shard_map/ppermute | solution.py:245
  193.8 10.7 %shard_map.40 = f32[12,128,128]{2,1,0:T(8,128)} custom-call(f32[1024,128]{1,0:T(8,128)S(1)} %bitcast.52, f32[1536,128]{1,0:T(8,128)S(1)} %bitcast.51, f32[1024,128]{1,0:T(8,128)S(1)} %bitcast.53), custom_call_target="tpu_custom_call" | custom-call | tf_op jit(solution)/shard_map/pallas_call | solution.py:250
  (31 shorter events, 1.7 us)
Async XLA Ops:
  48.8 54.5 %collective-permute-start.1 = (bf16[6,6,8,2048]{3,2,1,0:T(8,128)(2,1)}, bf16[6,6,8,2048]{3,2,1,0:T(8,128)(2,1)}, u32[]{:S(2)}, u32[]{:S(2)}) collective-permute-start(bf16[6,6,8,2048]{3,2,1,0:T(8,128)(2,1)} %get-tuple-element.24), channel_id=1, source_target_pairs={{240,224},{224,240},{208,192},{192,208},{176,160},{160,176},{144,1... | collective-permute-start | bytes 3538952 | tf_op jit(solution)/shard_map/ppermute | solution.py:160
  52.2 49.6 %copy-start.1 = (bf16[8,96,96]{2,1,0:T(8,128)(2,1)S(1)}, bf16[8,96,96]{2,1,0:T(8,128)(2,1)}, u32[]{:S(2)}) copy-start(bf16[8,96,96]{2,1,0:T(8,128)(2,1)} %param.4) | copy-start | bytes 442372
  52.2 49.9 %collective-permute-start.5 = (bf16[2,6,8,2048]{3,2,1,0:T(8,128)(2,1)}, bf16[2,6,8,2048]{3,2,1,0:T(8,128)(2,1)}, u32[]{:S(2)}, u32[]{:S(2)}) collective-permute-start(bf16[2,6,8,2048]{3,2,1,0:T(8,128)(2,1)} %get-tuple-element.27), channel_id=1, source_target_pairs={{0,16},{16,0},{32,48},{48,32},{64,80},{80,64},{96,112},{112,96},{1... | collective-permute-start | bytes 1179656 | tf_op jit(solution)/shard_map/ppermute | solution.py:160
  101.2 8.5 %collective-permute-start = (bf16[8,6,8,2048]{3,2,1,0:T(8,128)(2,1)}, bf16[8,6,8,2048]{3,2,1,0:T(8,128)(2,1)}, u32[]{:S(2)}, u32[]{:S(2)}) collective-permute-start(bf16[8,6,8,2048]{3,2,1,0:T(8,128)(2,1)} %get-tuple-element.22), channel_id=1, source_target_pairs={{0,16},{16,0},{32,48},{48,32},{64,80},{80,64},{96,112},{112,96},{1... | collective-permute-start | bytes 4718600 | tf_op jit(solution)/shard_map/ppermute | solution.py:160
  103.2 10.8 %collective-permute-start.6 = (f16[2,6,8,2048]{3,2,1,0:T(8,128)(2,1)S(1)}, f16[2,6,8,2048]{3,2,1,0:T(8,128)(2,1)S(1)}, u32[]{:S(2)}, u32[]{:S(2)}) collective-permute-start(f16[2,6,8,2048]{3,2,1,0:T(8,128)(2,1)S(1)} %multiply_convert_fusion.3), channel_id=1, source_target_pairs={{0,32},{16,48},{32,0},{48,16},{64,96},{80,112},{96,64},{112,80},{1... | collective-permute-start | bytes 1179656 | tf_op jit(solution)/shard_map/ppermute | solution.py:160
  105.3 12.0 %collective-permute-start.2 = (f16[2,6,8,2048]{3,2,1,0:T(8,128)(2,1)S(1)}, f16[2,6,8,2048]{3,2,1,0:T(8,128)(2,1)S(1)}, u32[]{:S(2)}, u32[]{:S(2)}) collective-permute-start(f16[2,6,8,2048]{3,2,1,0:T(8,128)(2,1)S(1)} %get-tuple-element.39), channel_id=1, source_target_pairs={{0,64},{16,80},{32,96},{48,112},{64,128},{80,144},{96,160},{112,17... | collective-permute-start | bytes 1179656 | tf_op jit(solution)/shard_map/ppermute | solution.py:160
  106.1 19.8 %collective-permute-start.3 = (f16[2,6,8,2048]{3,2,1,0:T(8,128)(2,1)S(1)}, f16[2,6,8,2048]{3,2,1,0:T(8,128)(2,1)S(1)}, u32[]{:S(2)}, u32[]{:S(2)}) collective-permute-start(f16[2,6,8,2048]{3,2,1,0:T(8,128)(2,1)S(1)} %get-tuple-element.38), channel_id=1, source_target_pairs={{0,128},{16,144},{32,160},{48,176},{64,192},{80,208},{96,224},{112... | collective-permute-start | bytes 1179656 | tf_op jit(solution)/shard_map/ppermute | solution.py:160
  108.6 17.4 %collective-permute-start.4 = (f16[2,6,8,2048]{3,2,1,0:T(8,128)(2,1)S(1)}, f16[2,6,8,2048]{3,2,1,0:T(8,128)(2,1)S(1)}, u32[]{:S(2)}, u32[]{:S(2)}) collective-permute-start(f16[2,6,8,2048]{3,2,1,0:T(8,128)(2,1)S(1)} %get-tuple-element.37), channel_id=1, source_target_pairs={{0,192},{16,208},{32,224},{48,240},{64,0},{80,16},{96,32},{112,48}... | collective-permute-start | bytes 1179656 | tf_op jit(solution)/shard_map/ppermute | solution.py:160
  110.9 21.2 %collective-permute-start.8 = (f16[2,6,8,2048]{3,2,1,0:T(8,128)(2,1)S(1)}, f16[2,6,8,2048]{3,2,1,0:T(8,128)(2,1)S(1)}, u32[]{:S(2)}, u32[]{:S(2)}) collective-permute-start(f16[2,6,8,2048]{3,2,1,0:T(8,128)(2,1)S(1)} %multiply_convert_fusion.2), channel_id=1, source_target_pairs={{240,208},{224,192},{208,240},{192,224},{176,144},{160,128},{144,1... | collective-permute-start | bytes 1179656 | tf_op jit(solution)/shard_map/ppermute | solution.py:160
  127.3 7.3 %collective-permute-start.7 = (f16[6,8,2048]{2,1,0:T(8,128)(2,1)S(1)}, f16[6,8,2048]{2,1,0:T(8,128)(2,1)S(1)}, u32[]{:S(2)}, u32[]{:S(2)}) collective-permute-start(f16[6,8,2048]{2,1,0:T(8,128)(2,1)S(1)} %fusion.6), channel_id=1, source_target_pairs={{0,32},{16,48},{32,0},{48,16},{64,96},{80,112},{96,64},{112,80},{1... | collective-permute-start | bytes 589832 | tf_op jit(solution)/shard_map/ppermute | solution.py:160
  128.6 6.9 %collective-permute-start.10 = (f16[6,8,2048]{2,1,0:T(8,128)(2,1)S(1)}, f16[6,8,2048]{2,1,0:T(8,128)(2,1)S(1)}, u32[]{:S(2)}, u32[]{:S(2)}) collective-permute-start(f16[6,8,2048]{2,1,0:T(8,128)(2,1)S(1)} %get-tuple-element.43), channel_id=1, source_target_pairs={{240,176},{224,160},{208,144},{192,128},{176,112},{160,96},{144,80... | collective-permute-start | bytes 589832 | tf_op jit(solution)/shard_map/ppermute | solution.py:160
  132.0 7.5 %collective-permute-start.9 = (f16[6,8,2048]{2,1,0:T(8,128)(2,1)S(1)}, f16[6,8,2048]{2,1,0:T(8,128)(2,1)S(1)}, u32[]{:S(2)}, u32[]{:S(2)}) collective-permute-start(f16[6,8,2048]{2,1,0:T(8,128)(2,1)S(1)} %get-tuple-element.42), channel_id=1, source_target_pairs={{240,48},{224,32},{208,16},{192,0},{176,240},{160,224},{144,208},{... | collective-permute-start | bytes 589832 | tf_op jit(solution)/shard_map/ppermute | solution.py:160
  133.2 8.6 %collective-permute-start.11 = (f16[6,8,2048]{2,1,0:T(8,128)(2,1)S(1)}, f16[6,8,2048]{2,1,0:T(8,128)(2,1)S(1)}, u32[]{:S(2)}, u32[]{:S(2)}) collective-permute-start(f16[6,8,2048]{2,1,0:T(8,128)(2,1)S(1)} %fusion.7), channel_id=1, source_target_pairs={{240,112},{224,96},{208,80},{192,64},{176,48},{160,32},{144,16},{1... | collective-permute-start | bytes 589832 | tf_op jit(solution)/shard_map/ppermute | solution.py:160
  142.0 19.8 %copy-start = (s32[8,128]{1,0:T(8,128)S(1)}, s32[8,128]{1,0:T(8,128)}, u32[]{:S(2)}) copy-start(s32[8,128]{1,0:T(8,128)} %classes_ref.1) | copy-start | bytes 12292
  178.6 10.7 %collective-permute-start.12 = (f16[16,64,128]{2,1,0:T(8,128)(2,1)S(1)}, f16[16,64,128]{2,1,0:T(8,128)(2,1)S(1)}, u32[]{:S(2)}, u32[]{:S(2)}) collective-permute-start(f16[16,64,128]{2,1,0:T(8,128)(2,1)S(1)} %get-tuple-element.41), channel_id=1, source_target_pairs={{0,16},{16,32},{32,48},{48,64},{64,80},{80,96},{96,112},{112,128},... | collective-permute-start | bytes 786440 | tf_op jit(solution)/shard_map/ppermute | solution.py:244
  186.1 7.7 %collective-permute-start.13 = (f16[16,64,128]{2,1,0:T(8,128)(2,1)S(1)}, f16[16,64,128]{2,1,0:T(8,128)(2,1)S(1)}, u32[]{:S(2)}, u32[]{:S(2)}) collective-permute-start(f16[16,64,128]{2,1,0:T(8,128)(2,1)S(1)} %get-tuple-element.40), channel_id=1, source_target_pairs={{16,0},{32,16},{48,32},{64,48},{80,64},{96,80},{112,96},{128,112},... | collective-permute-start | bytes 786440 | tf_op jit(solution)/shard_map/ppermute | solution.py:245

commit v4 on v3

v4 whole, which is shorter than its diff:
```python
import jax
import jax.numpy as jnp
from jax import lax
from jax.experimental import pallas as pl
from jax.experimental.pallas import tpu as pltpu
from jax.sharding import PartitionSpec as P

ITERS = 5
WAYS = 4
TILE = 16
SUM_SCALE = 1024.0
SCALE = 32.0


def home(lane, shift, lanes):
    return lanes // WAYS * lax.rem(lax.rem(lane, WAYS) + shift, WAYS) + lane // WAYS


def filter_kernel(grad_ref, weights_ref, classes_ref, out_ref, cells):
    blocks, parts, depth, rows, lanes = grad_ref.shape
    total = blocks * depth
    kinds = weights_ref.shape[1] // total
    shift = lax.rem(lax.axis_index("cuts"), WAYS)
    source = lax.broadcasted_iota(jnp.int32, (lanes, lanes), 0)
    target = lax.broadcasted_iota(jnp.int32, (lanes, lanes), 1)
    turn = jnp.where(home(source, shift, lanes) == target, 1.0, 0.0).astype(jnp.bfloat16)
    for part in range(parts):
        flat = grad_ref[:, part].astype(jnp.float32).reshape(total * rows, lanes).astype(jnp.bfloat16)
        cells[part] = jnp.dot(flat, turn, preferred_element_type=jnp.float32)
    labels = jnp.dot(
        classes_ref[...].astype(jnp.float32).astype(jnp.bfloat16), turn, preferred_element_type=jnp.float32
    )
    weights = weights_ref[...]
    for row in range(rows):
        label = jnp.concatenate([labels[row : row + 1, :]] * parts, axis=1)
        values = jnp.concatenate(
            [cells[part, pl.ds(row, total, stride=rows), :] for part in range(parts)], axis=1
        )
        masked = jnp.concatenate(
            [jnp.where(label == float(kind), values, 0.0) for kind in range(kinds)], axis=0
        ).astype(jnp.bfloat16)
        found = jnp.dot(weights, masked, preferred_element_type=jnp.float32)
        for part in range(parts):
            for s in range(depth):
                out_ref[pl.ds((part * rows + row) * depth + s, blocks, stride=rows * parts * depth), :] = found[
                    s * blocks : (s + 1) * blocks, part * lanes : (part + 1) * lanes
                ]


def tv_kernel(shape, skipped, above_ref, own_ref, below_ref, out_ref, field):
    blocks, parts, depth, rows, lanes = shape
    halo = ITERS
    tiles = range(WAYS)
    groups = blocks // WAYS
    lines = parts * groups
    size = lanes // WAYS
    first = (lax.axis_index("scan") == 0).astype(jnp.float32)
    last = (lax.axis_index("scan") == lax.axis_size("scan") - 1).astype(jnp.float32)
    lane = lax.broadcasted_iota(jnp.int32, (lines, lanes), 1)
    line = lax.broadcasted_iota(jnp.int32, (lines, lanes), 0)
    at_left = lane == 0
    at_right = lane == lanes - 1
    inner = jnp.where(at_right & (lax.rem(line, groups) == groups - 1), 0.0, 1.0)
    homes = [home(lane, b, lanes) for b in tiles]

    def skewed(values):
        found = []
        for m in tiles:
            pick = values[-m % WAYS]
            for group in range(1, WAYS):
                pick = jnp.where(lane // size == group, values[(group - m) % WAYS], pick)
            found.append(pick)
        return found

    def load(s, row):
        if row < 0:
            source, at = above_ref, (row + rows) * depth - skipped
        elif row < rows:
            source, at = own_ref, row * depth
        else:
            source, at = below_ref, (row - rows) * depth
        per = source.shape[0] // (blocks * parts)
        found = skewed([source[pl.ds(b * per + at + s, lines, stride=WAYS * per), :] for b in tiles])
        return [pltpu.roll(f, (lanes - size * m) % lanes, 1) for m, f in enumerate(found)]

    def store(s, row, values):
        values = skewed([pltpu.roll(v, size * m, 1) for m, v in enumerate(values)])
        for b in tiles:
            value = jnp.take_along_axis(values[b], homes[b], axis=1)
            for part in range(parts):
                out_ref[part * depth + s, pl.ds(b * rows + row, groups, stride=WAYS * rows), :] = value[
                    part * groups : (part + 1) * groups
                ]

    def one_slice(s, carry):
        for sweep in range(1, ITERS + 1):
            low, high = sweep - ITERS, rows + ITERS - sweep

            def read(row):
                return load(s, row) if sweep == 1 else [field[row + halo, m] for m in tiles]

            before = None
            here = read(low - 1)
            for row in range(low - 1, high):
                below = read(row + 1)
                down = [b - h for b, h in zip(below, here)]
                if row == -1:
                    down = [d * (1.0 - first) for d in down]
                if row == rows - 1:
                    down = [d * (1.0 - last) for d in down]
                near = pltpu.roll(here[0], lanes - 1, 1)
                near = jnp.where(at_right, pltpu.roll(near, lines - 1, 0), near)
                across = [n - h for n, h in zip(here[1:] + [near], here)]
                across[-1] = across[-1] * inner
                power = [d * d + a * a for d, a in zip(down, across)]
                inverse = [lax.rsqrt(p + pltpu.roll(p, groups, 0) + 1.0) for p in power]
                flux = [d * i for d, i in zip(down, inverse)]
                if before is not None:
                    sides = [a * i for a, i in zip(across, inverse)]
                    near = pltpu.roll(sides[-1], 1, 1)
                    near = jnp.where(at_left, pltpu.roll(near, 1, 0), near)
                    fresh = [
                        h + 0.2 * (f - b + s1 - s0)
                        for h, f, b, s1, s0 in zip(here, flux, before, sides, [near] + sides[:-1])
                    ]
                    if sweep == ITERS:
                        store(s, row, fresh)
                    else:
                        for m in tiles:
                            field[row + halo, m] = fresh[m]
                before = flux
                here = below
        return carry

    lax.fori_loop(0, depth, one_slice, 0)


def copy_kernel(plan, source_ref, *refs):
    count = len(plan)
    sems = refs[count]
    me = lax.axis_index("scan")
    core, y, x = lax.rem(me, 2), lax.rem(me // 2, 2), me // 4
    chips = source_ref.shape[2]
    copies = []
    for out, (theirs, pieces) in zip(refs, plan):
        whose = 1 - core if theirs else core
        for slot, (part, k, e) in enumerate(pieces):
            copies.append(
                pltpu.make_async_copy(
                    source_ref.at[part, :, lax.rem(x + k, chips), 1 - y if e else y, whose],
                    out.at[slot],
                    sems.at[len(copies)],
                )
            )
    for copy in copies:
        copy.start()
    for copy in copies:
        copy.wait()


def copied(split, *plan):
    _, depth, _, _, _, rows, width = split.shape
    moved = 4 * sum(len(pieces) for _, pieces in plan) * depth * rows * width
    return pl.pallas_call(
        lambda *refs: copy_kernel(plan, *refs),
        out_shape=[jax.ShapeDtypeStruct((len(pieces), depth, rows, width), split.dtype) for _, pieces in plan],
        in_specs=[pl.BlockSpec(memory_space=pltpu.HBM)],
        out_specs=[pl.BlockSpec(memory_space=pltpu.VMEM)] * len(plan),
        scratch_shapes=[pltpu.SemaphoreType.DMA((sum(len(pieces) for _, pieces in plan),))],
        cost_estimate=pl.CostEstimate(flops=0, bytes_accessed=moved, transcendentals=0),
        compiler_params=pltpu.CompilerParams(vmem_limit_bytes=24 * 1024 * 1024),
    )(split)


def on_device(partials, inverses, classes):
    _, parts, depth, rows_total, width = partials.shape
    scans = lax.axis_size("scan")
    cuts = lax.axis_size("cuts")
    rows = rows_total // scans
    lanes = width // cuts
    kinds, total, _ = inverses.shape
    chips = scans // 4
    f32, f16 = jnp.float32, jnp.float16

    def send(array, target, order=1):
        return lax.ppermute(array, "scan", [(i, target(i)) for i in range(scans)][::order])

    def other_core(i):
        return i ^ 1

    def other_y(i):
        return i ^ 2

    def along_x(k):
        return lambda i: (i + 4 * k) % scans

    def paired(own, got):
        return (own.astype(f32) + got.astype(f32)) * SUM_SCALE

    weights = inverses.reshape(kinds, cuts, depth, total).transpose(2, 1, 0, 3).reshape(total, kinds * total)

    def after(value, made):
        return lax.optimization_barrier((value, made))[0]

    split = partials.reshape(parts, depth, chips, 2, 2, rows, width)
    split = pltpu.with_memory_space_constraint(split, pltpu.HBM)
    early = [(0, 2, 0), (0, 2, 1), (1, 2, 1), (1, 0, 1)]
    late = [(1, 1, 1), (1, 3, 1)] + [(0, k, e) for k in (1, 3, 0) for e in range(2)] + [(1, k, 0) for k in (2, 0, 1, 3)]
    give_early, own_early = copied(split, (True, early), (False, early))
    got_early = send(give_early, other_core)
    give_late, own_late = copied(split, (True, late), (False, late))
    got_late = send(after(give_late, got_early), other_core, -1)

    two_steps = paired(own_early[:2], got_early[:2]).astype(f16)
    y_far = paired(own_early[2:], got_early[2:]).astype(f16)
    came_far = send(y_far, other_y)
    from_left = send(two_steps[0], along_x(1))
    from_right = send(two_steps[1], along_x(3))

    y_near = paired(own_late[:2], got_late[:2]).astype(f16)
    came_near = send(y_near, other_y, -1)
    one_step = paired(own_late[2:6], got_late[2:6])
    mine0 = paired(own_late[6:8], got_late[6:8])
    mine1 = paired(own_late[8:], got_late[8:])

    from_left, from_right = after((from_left, from_right), y_near)
    to_right = jnp.stack([one_step[0] + from_left.astype(f32), one_step[1]]).astype(f16)
    to_left = jnp.stack([one_step[2], one_step[3] + from_right.astype(f32)]).astype(f16)
    x_left = send(to_right, along_x(1))
    x_right = send(to_left, along_x(3))

    came_far = after(came_far, (to_right, to_left))
    far1 = mine1[:2] + came_far.astype(f32)
    two_steps1 = far1[0].astype(f16)
    half = depth // 2
    from_left1 = send(two_steps1[:half], along_x(1), -1)
    from_right1 = send(two_steps1[half:], along_x(3), -1)

    x_left, x_right = after((x_left, x_right), two_steps1)
    over_x = mine0 + x_left.astype(f32) + x_right.astype(f32)
    last = over_x[1].astype(f16)
    part0 = over_x[0] + send(last, other_y).astype(f32)

    came_near, from_left1, from_right1 = after((came_near, from_left1, from_right1), last)
    near1 = mine1[2:] + came_near.astype(f32)
    to_right1 = jnp.concatenate([near1[0, :half] + from_left1.astype(f32), near1[0, half:]]).astype(f16)
    to_left1 = jnp.concatenate([near1[1, :half], near1[1, half:] + from_right1.astype(f32)]).astype(f16)
    x_left1 = send(to_right1, along_x(1))
    x_right1 = send(to_left1, along_x(3))
    part1 = far1[1] + x_left1.astype(f32) + x_right1.astype(f32)

    grad = (jnp.stack([part0, part1]) * (1.0 / SUM_SCALE)).astype(jnp.bfloat16)
    grad = grad.reshape(parts, depth, rows, cuts, lanes).transpose(3, 0, 1, 2, 4)
    grad, weights = lax.optimization_barrier((grad, weights))
    grad = lax.all_to_all(grad, "cuts", 0, 0, tiled=True)
    per = rows * parts * depth
    filtered = pl.pallas_call(
        filter_kernel,
        out_shape=jax.ShapeDtypeStruct((cuts * per, lanes), f32),
        scratch_shapes=[pltpu.VMEM((parts, total * rows, lanes), f32)],
        compiler_params=pltpu.CompilerParams(vmem_limit_bytes=32 * 1024 * 1024),
    )(grad, weights, classes)
    coded = (filtered * SCALE).astype(f16).reshape(cuts, per, lanes)
    coded = lax.all_to_all(coded, "cuts", 0, 0, tiled=True)
    coded = coded.reshape(cuts, parts, rows * depth, lanes)
    skipped = (rows - ITERS) * depth // TILE * TILE
    needed = -(-ITERS * depth // TILE) * TILE
    above = lax.ppermute(coded[:, :, skipped:], "scan", [(i, i + 1) for i in range(scans - 1)])
    below = lax.ppermute(coded[:, :, :needed], "scan", [(i + 1, i) for i in range(scans - 1)])
    above, middle, below = [
        (c.astype(f32) * (1.0 / SCALE)).transpose(1, 0, 2, 3).reshape(-1, lanes) for c in (above, coded, below)
    ]
    shape = (cuts, parts, depth, rows, lanes)
    result = pl.pallas_call(
        lambda *refs: tv_kernel(shape, skipped, *refs),
        out_shape=jax.ShapeDtypeStruct((parts * depth, cuts * rows, lanes), f32),
        scratch_shapes=[pltpu.VMEM((rows + 2 * ITERS, WAYS, parts * cuts // WAYS, lanes), f32)],
        compiler_params=pltpu.CompilerParams(vmem_limit_bytes=32 * 1024 * 1024),
    )(above, middle, below)
    result = result.reshape(parts, depth, cuts, rows, lanes).transpose(0, 1, 3, 2, 4)
    return result.reshape(parts, depth, rows, width)


def solution(mesh):
    placed = (P("scan", None, "cuts", None, None), P(), P("scan", "cuts"))
    return jax.shard_map(
        on_device,
        mesh=mesh,
        in_specs=placed,
        out_specs=P(None, "cuts", "scan", None),
        check_vma=False,
    )
```

time: 206 us -> 98.3 us (0.48)
  Pallas kernels: 109 us -> 12.5 us
  waiting for transfers between devices: 26.3 us -> 19.8 us
  other arithmetic: 8.15 us -> 2.54 us
  starting transfers between devices: 24.1 us -> 26.4 us
    pallas_call x2, Pallas kernels: 97.8 us -> 4.15 us  [copied(): pl.pallas_call(lambda *refs: copy_kernel(plan, *refs), out_shape=[jax.Sha...]
    ppermute x12 -> x13, waiting for transfers between devices: 20.7 us -> 14.3 us  [send(): lax.ppermute(array, 'scan', [(i, target(i)) for i in range(scans)][::order])]
    convert_element_type x5 -> x2, other arithmetic: 5.21 us -> 0.44 us  [the longest x1 0.29 us: on_device(): two_steps = paired(own_early[:2], got_early[:2]).astype(f16)]
    pallas_call x1, Pallas kernels: 10.7 us -> 7.3 us  [on_device(): pl.pallas_call(lambda *refs: tv_kernel(shape, skipped, *refs), out_shape=...]
    add x2 -> x1, other arithmetic: 2.46 us -> 0.24 us  [on_device(): over_x = mine0 + x_left.astype(f32) + x_right.astype(f32)]
    ppermute x12 -> x13, starting transfers between devices: 14.7 us -> 16 us  [send(): lax.ppermute(array, 'scan', [(i, target(i)) for i in range(scans)][::order])]
  transfers between devices with their start and end apart: 14 -> 15, of which waited for: 9 -> 8; matrix products, arithmetic and copies ran while one was open for 4% -> 3% of each run, Pallas kernels for 24% -> 3%
where the time goes in v4:
time: 98.3 us; the launch traced here: 97.5 us
  blocking collectives  34.8 us (35%)
  starting transfers between devices  26.4 us (27%)
  waiting for transfers between devices  19.8 us (20%)
  Pallas kernels  12.5 us (13%)
  other arithmetic  2.54 us (3%)
  local copies, waits for them, and re-layouts  1.16 us (1%)
    all_to_all x1, blocking collectives, on_device(): grad = lax.all_to_all(grad, 'cuts', 0, 0, tiled=True)  20 us
    ppermute x13, starting transfers between devices, send(): lax.ppermute(array, 'scan', [(i, target(i)) for i in range(scans)][::order])  16 us
    all_to_all x1, blocking collectives, on_device(): coded = lax.all_to_all(coded, 'cuts', 0, 0, tiled=True)  14.8 us
    ppermute x13, waiting for transfers between devices, send(): lax.ppermute(array, 'scan', [(i, target(i)) for i in range(scans)][::order])  14.3 us
    ppermute x1, starting transfers between devices, on_device(): lax.ppermute(coded[:, :, skipped:], 'scan', [(i, i + 1) for i in range(sc...  8.47 us
    pallas_call x1, Pallas kernels, on_device(): pl.pallas_call(lambda *refs: tv_kernel(shape, skipped, *refs), out_shape=...  7.3 us
    ppermute x1, waiting for transfers between devices, on_device(): lax.ppermute(coded[:, :, :needed], 'scan', [(i + 1, i) for i in range(sca...  4.28 us
    pallas_call x2, Pallas kernels, copied(): pl.pallas_call(lambda *refs: copy_kernel(plan, *refs), out_shape=[jax.Sha...  4.15 us
  transfers between devices with their start and end apart: 15, of which 8 were waited for; matrix products, arithmetic and copies ran while one was open for 3% of the time, Pallas kernels for 3%

profile of v4, /device:TPU:1, one launch (start us, length us, event | category | flops | bytes accessed | tf_op | source)
XLA Modules:
  0.0 97.5 jit_solution(2592319534135920287)
XLA Ops:
  0.0 1.5 %shard_map.38 = (bf16[4,6,8,2048]{3,2,1,0:T(8,128)(2,1)S(1)}, bf16[4,6,8,2048]{3,2,1,0:T(8,128)(2,1)S(1)}) custom-call(bf16[2,6,4,2,2,8,2048]{6,5,4,3,2,1,0:T(8,128)(2,1)} %bitcast.101), custom_call_target="tpu_custom_call" | custom-call | bytes 3145728 | tf_op jit(solution)/shard_map/pallas_call | solution.py:164
  1.5 3.3 %collective-permute-start = (bf16[4,6,8,2048]{3,2,1,0:T(8,128)(2,1)S(1)}, bf16[4,6,8,2048]{3,2,1,0:T(8,128)(2,1)S(1)}, u32[]{:S(2)}, u32[]{:S(2)}) collective-permute-start(bf16[4,6,8,2048]{3,2,1,0:T(8,128)(2,1)S(1)} %get-tuple-element.22), channel_id=1, source_target_pairs={{0,16},{16,0},{32,48},{48,32},{64,80},{80,64},{96,112},{112,96},{1... | collective-permute-start | bytes 2359304 | tf_op jit(solution)/shard_map/ppermute | solution.py:186
  4.9 2.6 %shard_map.37 = (bf16[12,6,8,2048]{3,2,1,0:T(8,128)(2,1)S(1)}, bf16[12,6,8,2048]{3,2,1,0:T(8,128)(2,1)S(1)}) custom-call(bf16[2,6,4,2,2,8,2048]{6,5,4,3,2,1,0:T(8,128)(2,1)} %bitcast.102), custom_call_target="tpu_custom_call" | custom-call | bytes 9437184 | tf_op jit(solution)/shard_map/pallas_call | solution.py:164
  7.6 0.3 multiply_convert_fusion.3
  8.1 0.8 collective-permute-start.2
  8.9 1.9 %collective-permute-start.3 = (f16[6,8,2048]{2,1,0:T(8,128)(2,1)S(1)}, f16[6,8,2048]{2,1,0:T(8,128)(2,1)S(1)}, u32[]{:S(2)}, u32[]{:S(2)}) collective-permute-start(f16[6,8,2048]{2,1,0:T(8,128)(2,1)S(1)} %get-tuple-element.56), channel_id=1, source_target_pairs={{0,192},{16,208},{32,224},{48,240},{64,0},{80,16},{96,32},{112,48}... | collective-permute-start | bytes 589832 | tf_op jit(solution)/shard_map/ppermute | solution.py:186
  10.9 1.3 %collective-permute-done.1 = bf16[12,6,8,2048]{3,2,1,0:T(8,128)(2,1)S(1)} collective-permute-done((bf16[12,6,8,2048]{3,2,1,0:T(8,128)(2,1)S(1)}, bf16[12,6,8,2048]{3,2,1,0:T(8,128)(2,1)S(1)}, u32[]{:S(2)}, u32[]{:S(2)}) %collective-permute-start.1) | collective-permute-done | bytes 2359328 | tf_op jit(solution)/shard_map/ppermute | solution.py:186
  12.1 0.6 add_multiply_fusion
  12.8 0.1 multiply_convert_fusion.2
  13.0 0.3 collective-permute-start.8
  13.3 2.1 %collective-permute-done.2 = f16[6,8,2048]{2,1,0:T(8,128)(2,1)S(1)} collective-permute-done((f16[6,8,2048]{2,1,0:T(8,128)(2,1)S(1)}, f16[6,8,2048]{2,1,0:T(8,128)(2,1)S(1)}, u32[]{:S(2)}, u32[]{:S(2)}) %collective-permute-start.2) | collective-permute-done | bytes 196640 | tf_op jit(solution)/shard_map/ppermute | solution.py:186
  15.6 0.2 collective-permute-start.4
  15.9 2.6 %collective-permute-start.5 = (f16[2,6,8,2048]{3,2,1,0:T(8,128)(2,1)S(1)}, f16[2,6,8,2048]{3,2,1,0:T(8,128)(2,1)S(1)}, u32[]{:S(2)}, u32[]{:S(2)}) collective-permute-start(f16[2,6,8,2048]{3,2,1,0:T(8,128)(2,1)S(1)} %pad_maximum_fusion.1), channel_id=1, source_target_pairs={{0,192},{16,208},{32,224},{48,240},{64,0},{80,16},{96,32},{112,48}... | collective-permute-start | bytes 1179656 | tf_op jit(solution)/shard_map/ppermute | solution.py:186
  18.8 2.7 %collective-permute-start.10 = (f16[3,8,2048]{2,1,0:T(8,128)(2,1)S(1)}, f16[3,8,2048]{2,1,0:T(8,128)(2,1)S(1)}, u32[]{:S(2)}, u32[]{:S(2)}) collective-permute-start(f16[3,8,2048]{2,1,0:T(8,128)(2,1)S(1)} %get-tuple-element.54), channel_id=1, source_target_pairs={{240,176},{224,160},{208,144},{192,128},{176,112},{160,96},{144,80... | collective-permute-start | bytes 294920 | tf_op jit(solution)/shard_map/ppermute | solution.py:186
  21.5 4.7 %collective-permute-done.4 = f16[2,6,8,2048]{3,2,1,0:T(8,128)(2,1)S(1)} collective-permute-done((f16[2,6,8,2048]{3,2,1,0:T(8,128)(2,1)S(1)}, f16[2,6,8,2048]{3,2,1,0:T(8,128)(2,1)S(1)}, u32[]{:S(2)}, u32[]{:S(2)}) %collective-permute-start.4) | collective-permute-done | bytes 393248 | tf_op jit(solution)/shard_map/ppermute | solution.py:186
  26.2 0.2 convert_add_fusion
  26.5 1.8 %collective-permute-done.9 = f16[3,8,2048]{2,1,0:T(8,128)(2,1)S(1)} collective-permute-done((f16[3,8,2048]{2,1,0:T(8,128)(2,1)S(1)}, f16[3,8,2048]{2,1,0:T(8,128)(2,1)S(1)}, u32[]{:S(2)}, u32[]{:S(2)}) %collective-permute-start.9) | collective-permute-done | bytes 98336 | tf_op jit(solution)/shard_map/ppermute | solution.py:186
  28.3 0.1 fusion.19
  28.7 2.6 %collective-permute-start.12 = (f16[6,8,2048]{2,1,0:T(8,128)(2,1)S(1)}, f16[6,8,2048]{2,1,0:T(8,128)(2,1)S(1)}, u32[]{:S(2)}, u32[]{:S(2)}) collective-permute-start(f16[6,8,2048]{2,1,0:T(8,128)(2,1)S(1)} %pad_maximum_fusion.3), channel_id=1, source_target_pairs={{0,192},{16,208},{32,224},{48,240},{64,0},{80,16},{96,32},{112,48}... | collective-permute-start | bytes 589832 | tf_op jit(solution)/shard_map/ppermute | solution.py:186
  31.6 0.2 reshape.41.weights_ref
  31.8 1.1 %collective-permute-start.6 = (f16[6,8,2048]{2,1,0:T(8,128)(2,1)S(1)}, f16[6,8,2048]{2,1,0:T(8,128)(2,1)S(1)}, u32[]{:S(2)}, u32[]{:S(2)}) collective-permute-start(f16[6,8,2048]{2,1,0:T(8,128)(2,1)S(1)} %fusion.13), channel_id=1, source_target_pairs={{0,32},{16,48},{32,0},{48,16},{64,96},{80,112},{96,64},{112,80},{1... | collective-permute-start | bytes 589832 | tf_op jit(solution)/shard_map/ppermute | solution.py:186
  32.8 1.1 %collective-permute-done.12 = f16[6,8,2048]{2,1,0:T(8,128)(2,1)S(1)} collective-permute-done((f16[6,8,2048]{2,1,0:T(8,128)(2,1)S(1)}, f16[6,8,2048]{2,1,0:T(8,128)(2,1)S(1)}, u32[]{:S(2)}, u32[]{:S(2)}) %collective-permute-start.12) | collective-permute-done | bytes 196640 | tf_op jit(solution)/shard_map/ppermute | solution.py:186
  33.9 3.2 %collective-permute-done.11 = f16[6,8,2048]{2,1,0:T(8,128)(2,1)S(1)} collective-permute-done((f16[6,8,2048]{2,1,0:T(8,128)(2,1)S(1)}, f16[6,8,2048]{2,1,0:T(8,128)(2,1)S(1)}, u32[]{:S(2)}, u32[]{:S(2)}) %collective-permute-start.11) | collective-permute-done | bytes 196640 | tf_op jit(solution)/shard_map/ppermute | solution.py:186
  37.8 20.0 %all_to_all.10.grad_ref = bf16[16,2,6,8,128]{4,3,2,1,0:T(8,128)(2,1)S(1)} all-to-all(bf16[16,2,6,8,128]{4,3,2,1,0:T(8,128)(2,1)S(1)} %fusion.1), channel_id=1, replica_groups=mesh['scan'=16,'cuts'=16] {'cuts'}, dimensions={0} | all-to-all | bytes 786432 | tf_op jit(solution)/shard_map/all_to_all | solution.py:255
  57.8 1.1 %shard_map.39 = f32[1536,128]{1,0:T(8,128)S(1)} custom-call(bf16[16,2,6,8,128]{4,3,2,1,0:T(8,128)(2,1)S(1)} %all_to_all.10.grad_ref, bf16[96,768]{1,0:T(8,128)(2,1)S(1)} %reshape.41.weights_ref, s32[8,128]{1,0:T(8,128)S(1)} %copy-done), custom_call_target="tpu_custom_call" | custom-call | tf_op jit(solution)/shard_map/pallas_call | solution.py:257
  59.0 14.8 %all_to_all.11 = f16[16,96,128]{2,1,0:T(8,128)(2,1)S(1)} all-to-all(f16[16,96,128]{2,1,0:T(8,128)(2,1)S(1)} %bitcast.107), channel_id=1, replica_groups=mesh['scan'=16,'cuts'=16] {'cuts'}, dimensions={0} | all-to-all | bytes 786432 | tf_op jit(solution)/shard_map/all_to_all | solution.py:264
  73.8 0.1 fusion.22
  74.0 8.5 %collective-permute-start.13 = (f16[16,2,32,128]{3,2,1,0:T(8,128)(2,1)S(1)}, f16[16,2,32,128]{3,2,1,0:T(8,128)(2,1)S(1)}, u32[]{:S(2)}, u32[]{:S(2)}) collective-permute-start(f16[16,2,32,128]{3,2,1,0:T(8,128)(2,1)S(1)} %get-tuple-element.51), channel_id=1, source_target_pairs={{0,16},{16,32},{32,48},{48,64},{64,80},{80,96},{96,112},{112,128},... | collective-permute-start | bytes 786440 | tf_op jit(solution)/shard_map/ppermute | solution.py:268
  82.4 1.9 %collective-permute-start.14 = (f16[16,2,32,128]{3,2,1,0:T(8,128)(2,1)S(1)}, f16[16,2,32,128]{3,2,1,0:T(8,128)(2,1)S(1)}, u32[]{:S(2)}, u32[]{:S(2)}) collective-permute-start(f16[16,2,32,128]{3,2,1,0:T(8,128)(2,1)S(1)} %get-tuple-element.50), channel_id=1, source_target_pairs={{16,0},{32,16},{48,32},{64,48},{80,64},{96,80},{112,96},{128,112},... | collective-permute-start | bytes 786440 | tf_op jit(solution)/shard_map/ppermute | solution.py:269
  84.5 1.2 %collective-permute-done.13 = f16[16,2,32,128]{3,2,1,0:T(8,128)(2,1)S(1)} collective-permute-done((f16[16,2,32,128]{3,2,1,0:T(8,128)(2,1)S(1)}, f16[16,2,32,128]{3,2,1,0:T(8,128)(2,1)S(1)}, u32[]{:S(2)}, u32[]{:S(2)}) %collective-permute-start.13) | collective-permute-done | bytes 262176 | tf_op jit(solution)/shard_map/ppermute | solution.py:268
  85.8 4.3 %collective-permute-done.14 = f16[16,2,32,128]{3,2,1,0:T(8,128)(2,1)S(1)} collective-permute-done((f16[16,2,32,128]{3,2,1,0:T(8,128)(2,1)S(1)}, f16[16,2,32,128]{3,2,1,0:T(8,128)(2,1)S(1)}, u32[]{:S(2)}, u32[]{:S(2)}) %collective-permute-start.14) | collective-permute-done | bytes 262176 | tf_op jit(solution)/shard_map/ppermute | solution.py:269
  90.2 7.3 %shard_map.40 = f32[12,128,128]{2,1,0:T(8,128)} custom-call(f32[1024,128]{1,0:T(8,128)S(1)} %bitcast.99, f32[1536,128]{1,0:T(8,128)S(1)} %bitcast.98, f32[1024,128]{1,0:T(8,128)S(1)} %bitcast.100), custom_call_target="tpu_custom_call" | custom-call | tf_op jit(solution)/shard_map/pallas_call | solution.py:274
  (43 shorter events, 2.4 us)
Async XLA Ops:
  1.5 6.0 %collective-permute-start = (bf16[4,6,8,2048]{3,2,1,0:T(8,128)(2,1)S(1)}, bf16[4,6,8,2048]{3,2,1,0:T(8,128)(2,1)S(1)}, u32[]{:S(2)}, u32[]{:S(2)}) collective-permute-start(bf16[4,6,8,2048]{3,2,1,0:T(8,128)(2,1)S(1)} %get-tuple-element.22), channel_id=1, source_target_pairs={{0,16},{16,0},{32,48},{48,32},{64,80},{80,64},{96,112},{112,96},{1... | collective-permute-start | bytes 2359304 | tf_op jit(solution)/shard_map/ppermute | solution.py:186
  7.5 4.6 %collective-permute-start.1 = (bf16[12,6,8,2048]{3,2,1,0:T(8,128)(2,1)S(1)}, bf16[12,6,8,2048]{3,2,1,0:T(8,128)(2,1)S(1)}, u32[]{:S(2)}, u32[]{:S(2)}) collective-permute-start(bf16[12,6,8,2048]{3,2,1,0:T(8,128)(2,1)S(1)} %get-tuple-element.23), channel_id=1, source_target_pairs={{240,224},{224,240},{208,192},{192,208},{176,160},{160,176},{144,1... | collective-permute-start | bytes 7077896 | tf_op jit(solution)/shard_map/ppermute | solution.py:186
  7.9 10.6 %collective-permute-start.7 = (f16[2,6,8,2048]{3,2,1,0:T(8,128)(2,1)S(1)}, f16[2,6,8,2048]{3,2,1,0:T(8,128)(2,1)S(1)}, u32[]{:S(2)}, u32[]{:S(2)}) collective-permute-start(f16[2,6,8,2048]{3,2,1,0:T(8,128)(2,1)S(1)} %get-tuple-element.45), channel_id=1, source_target_pairs={{0,32},{16,48},{32,0},{48,16},{64,96},{80,112},{96,64},{112,80},{1... | collective-permute-start | bytes 1179656 | tf_op jit(solution)/shard_map/ppermute | solution.py:186
  8.1 7.3 %collective-permute-start.2 = (f16[6,8,2048]{2,1,0:T(8,128)(2,1)S(1)}, f16[6,8,2048]{2,1,0:T(8,128)(2,1)S(1)}, u32[]{:S(2)}, u32[]{:S(2)}) collective-permute-start(f16[6,8,2048]{2,1,0:T(8,128)(2,1)S(1)} %get-tuple-element.57), channel_id=1, source_target_pairs={{0,64},{16,80},{32,96},{48,112},{64,128},{80,144},{96,160},{112,17... | collective-permute-start | bytes 589832 | tf_op jit(solution)/shard_map/ppermute | solution.py:186
  8.9 6.5 %collective-permute-start.3 = (f16[6,8,2048]{2,1,0:T(8,128)(2,1)S(1)}, f16[6,8,2048]{2,1,0:T(8,128)(2,1)S(1)}, u32[]{:S(2)}, u32[]{:S(2)}) collective-permute-start(f16[6,8,2048]{2,1,0:T(8,128)(2,1)S(1)} %get-tuple-element.56), channel_id=1, source_target_pairs={{0,192},{16,208},{32,224},{48,240},{64,0},{80,16},{96,32},{112,48}... | collective-permute-start | bytes 589832 | tf_op jit(solution)/shard_map/ppermute | solution.py:186
  13.0 15.3 %collective-permute-start.8 = (f16[2,6,8,2048]{3,2,1,0:T(8,128)(2,1)S(1)}, f16[2,6,8,2048]{3,2,1,0:T(8,128)(2,1)S(1)}, u32[]{:S(2)}, u32[]{:S(2)}) collective-permute-start(f16[2,6,8,2048]{3,2,1,0:T(8,128)(2,1)S(1)} %multiply_convert_fusion.2), channel_id=1, source_target_pairs={{240,208},{224,192},{208,240},{192,224},{176,144},{160,128},{144,1... | collective-permute-start | bytes 1179656 | tf_op jit(solution)/shard_map/ppermute | solution.py:186
  15.6 10.6 %collective-permute-start.4 = (f16[2,6,8,2048]{3,2,1,0:T(8,128)(2,1)S(1)}, f16[2,6,8,2048]{3,2,1,0:T(8,128)(2,1)S(1)}, u32[]{:S(2)}, u32[]{:S(2)}) collective-permute-start(f16[2,6,8,2048]{3,2,1,0:T(8,128)(2,1)S(1)} %pad_maximum_fusion), channel_id=1, source_target_pairs={{0,64},{16,80},{32,96},{48,112},{64,128},{80,144},{96,160},{112,17... | collective-permute-start | bytes 1179656 | tf_op jit(solution)/shard_map/ppermute | solution.py:186
  15.9 10.3 %collective-permute-start.5 = (f16[2,6,8,2048]{3,2,1,0:T(8,128)(2,1)S(1)}, f16[2,6,8,2048]{3,2,1,0:T(8,128)(2,1)S(1)}, u32[]{:S(2)}, u32[]{:S(2)}) collective-permute-start(f16[2,6,8,2048]{3,2,1,0:T(8,128)(2,1)S(1)} %pad_maximum_fusion.1), channel_id=1, source_target_pairs={{0,192},{16,208},{32,224},{48,240},{64,0},{80,16},{96,32},{112,48}... | collective-permute-start | bytes 1179656 | tf_op jit(solution)/shard_map/ppermute | solution.py:186
  18.8 9.6 %collective-permute-start.9 = (f16[3,8,2048]{2,1,0:T(8,128)(2,1)S(1)}, f16[3,8,2048]{2,1,0:T(8,128)(2,1)S(1)}, u32[]{:S(2)}, u32[]{:S(2)}) collective-permute-start(f16[3,8,2048]{2,1,0:T(8,128)(2,1)S(1)} %get-tuple-element.55), channel_id=1, source_target_pairs={{240,48},{224,32},{208,16},{192,0},{176,240},{160,224},{144,208},{... | collective-permute-start | bytes 294920 | tf_op jit(solution)/shard_map/ppermute | solution.py:186
  18.8 9.5 %collective-permute-start.10 = (f16[3,8,2048]{2,1,0:T(8,128)(2,1)S(1)}, f16[3,8,2048]{2,1,0:T(8,128)(2,1)S(1)}, u32[]{:S(2)}, u32[]{:S(2)}) collective-permute-start(f16[3,8,2048]{2,1,0:T(8,128)(2,1)S(1)} %get-tuple-element.54), channel_id=1, source_target_pairs={{240,176},{224,160},{208,144},{192,128},{176,112},{160,96},{144,80... | collective-permute-start | bytes 294920 | tf_op jit(solution)/shard_map/ppermute | solution.py:186
  28.5 3.0 %copy-start.1 = (bf16[8,96,96]{2,1,0:T(8,128)(2,1)S(1)}, bf16[8,96,96]{2,1,0:T(8,128)(2,1)}, u32[]{:S(2)}) copy-start(bf16[8,96,96]{2,1,0:T(8,128)(2,1)} %param.4) | copy-start | bytes 442372
  28.7 5.3 %collective-permute-start.12 = (f16[6,8,2048]{2,1,0:T(8,128)(2,1)S(1)}, f16[6,8,2048]{2,1,0:T(8,128)(2,1)S(1)}, u32[]{:S(2)}, u32[]{:S(2)}) collective-permute-start(f16[6,8,2048]{2,1,0:T(8,128)(2,1)S(1)} %pad_maximum_fusion.3), channel_id=1, source_target_pairs={{0,192},{16,208},{32,224},{48,240},{64,0},{80,16},{96,32},{112,48}... | collective-permute-start | bytes 589832 | tf_op jit(solution)/shard_map/ppermute | solution.py:186
  31.4 5.8 %collective-permute-start.11 = (f16[6,8,2048]{2,1,0:T(8,128)(2,1)S(1)}, f16[6,8,2048]{2,1,0:T(8,128)(2,1)S(1)}, u32[]{:S(2)}, u32[]{:S(2)}) collective-permute-start(f16[6,8,2048]{2,1,0:T(8,128)(2,1)S(1)} %pad_maximum_fusion.2), channel_id=1, source_target_pairs={{0,64},{16,80},{32,96},{48,112},{64,128},{80,144},{96,160},{112,17... | collective-permute-start | bytes 589832 | tf_op jit(solution)/shard_map/ppermute | solution.py:186
  31.8 5.7 %collective-permute-start.6 = (f16[6,8,2048]{2,1,0:T(8,128)(2,1)S(1)}, f16[6,8,2048]{2,1,0:T(8,128)(2,1)S(1)}, u32[]{:S(2)}, u32[]{:S(2)}) collective-permute-start(f16[6,8,2048]{2,1,0:T(8,128)(2,1)S(1)} %fusion.13), channel_id=1, source_target_pairs={{0,32},{16,48},{32,0},{48,16},{64,96},{80,112},{96,64},{112,80},{1... | collective-permute-start | bytes 589832 | tf_op jit(solution)/shard_map/ppermute | solution.py:186
  37.6 20.2 %copy-start = (s32[8,128]{1,0:T(8,128)S(1)}, s32[8,128]{1,0:T(8,128)}, u32[]{:S(2)}) copy-start(s32[8,128]{1,0:T(8,128)} %classes_ref.1) | copy-start | bytes 12292
  74.0 11.8 %collective-permute-start.13 = (f16[16,2,32,128]{3,2,1,0:T(8,128)(2,1)S(1)}, f16[16,2,32,128]{3,2,1,0:T(8,128)(2,1)S(1)}, u32[]{:S(2)}, u32[]{:S(2)}) collective-permute-start(f16[16,2,32,128]{3,2,1,0:T(8,128)(2,1)S(1)} %get-tuple-element.51), channel_id=1, source_target_pairs={{0,16},{16,32},{32,48},{48,64},{64,80},{80,96},{96,112},{112,128},... | collective-permute-start | bytes 786440 | tf_op jit(solution)/shard_map/ppermute | solution.py:268
  82.4 7.7 %collective-permute-start.14 = (f16[16,2,32,128]{3,2,1,0:T(8,128)(2,1)S(1)}, f16[16,2,32,128]{3,2,1,0:T(8,128)(2,1)S(1)}, u32[]{:S(2)}, u32[]{:S(2)}) collective-permute-start(f16[16,2,32,128]{3,2,1,0:T(8,128)(2,1)S(1)} %get-tuple-element.50), channel_id=1, source_target_pairs={{16,0},{32,16},{48,32},{64,48},{80,64},{96,80},{112,96},{128,112},... | collective-permute-start | bytes 786440 | tf_op jit(solution)/shard_map/ppermute | solution.py:269

commit v5 on v4

--- a/solution.py
+++ b/solution.py
@@ -182,8 +182,9 @@
     chips = scans // 4
     f32, f16 = jnp.float32, jnp.float16
 
-    def send(array, target, order=1):
-        return lax.ppermute(array, "scan", [(i, target(i)) for i in range(scans)][::order])
+    def send(array, target, turn=0):
+        pairs = [(i, target(i)) for i in range(scans)]
+        return lax.ppermute(array, "scan", pairs[turn:] + pairs[:turn])
 
     def other_core(i):
         return i ^ 1
@@ -209,7 +210,7 @@
     give_early, own_early = copied(split, (True, early), (False, early))
     got_early = send(give_early, other_core)
     give_late, own_late = copied(split, (True, late), (False, late))
-    got_late = send(after(give_late, got_early), other_core, -1)
+    got_late = send(after(give_late, got_early), other_core, 1)
 
     two_steps = paired(own_early[:2], got_early[:2]).astype(f16)
     y_far = paired(own_early[2:], got_early[2:]).astype(f16)
@@ -218,7 +219,7 @@
     from_right = send(two_steps[1], along_x(3))
 
     y_near = paired(own_late[:2], got_late[:2]).astype(f16)
-    came_near = send(y_near, other_y, -1)
+    came_near = send(y_near, other_y, 1)
     one_step = paired(own_late[2:6], got_late[2:6])
     mine0 = paired(own_late[6:8], got_late[6:8])
     mine1 = paired(own_late[8:], got_late[8:])
@@ -233,25 +234,27 @@
     far1 = mine1[:2] + came_far.astype(f32)
     two_steps1 = far1[0].astype(f16)
     half = depth // 2
-    from_left1 = send(two_steps1[:half], along_x(1), -1)
-    from_right1 = send(two_steps1[half:], along_x(3), -1)
+    from_left1 = send(two_steps1[:half], along_x(1), 1)
+    from_right1 = send(two_steps1[half:], along_x(3), 1)
 
     x_left, x_right = after((x_left, x_right), two_steps1)
     over_x = mine0 + x_left.astype(f32) + x_right.astype(f32)
     last = over_x[1].astype(f16)
-    part0 = over_x[0] + send(last, other_y).astype(f32)
+    part0 = over_x[0] + send(last, other_y, 2).astype(f32)
 
     came_near, from_left1, from_right1 = after((came_near, from_left1, from_right1), last)
     near1 = mine1[2:] + came_near.astype(f32)
     to_right1 = jnp.concatenate([near1[0, :half] + from_left1.astype(f32), near1[0, half:]]).astype(f16)
     to_left1 = jnp.concatenate([near1[1, :half], near1[1, half:] + from_right1.astype(f32)]).astype(f16)
-    x_left1 = send(to_right1, along_x(1))
-    x_right1 = send(to_left1, along_x(3))
+    x_left1 = send(to_right1, along_x(1), 2)
+    x_right1 = send(to_left1, along_x(3), 2)
+    x_left1, x_right1 = after((x_left1, x_right1), part0)
     part1 = far1[1] + x_left1.astype(f32) + x_right1.astype(f32)
 
     grad = (jnp.stack([part0, part1]) * (1.0 / SUM_SCALE)).astype(jnp.bfloat16)
     grad = grad.reshape(parts, depth, rows, cuts, lanes).transpose(3, 0, 1, 2, 4)
-    grad, weights = lax.optimization_barrier((grad, weights))
+    upper = lax.axis_index("scan") & 1 == 0
+    grad, weights, upper = lax.optimization_barrier((grad, weights, upper))
     grad = lax.all_to_all(grad, "cuts", 0, 0, tiled=True)
     per = rows * parts * depth
     filtered = pl.pallas_call(
@@ -265,8 +268,13 @@
     coded = coded.reshape(cuts, parts, rows * depth, lanes)
     skipped = (rows - ITERS) * depth // TILE * TILE
     needed = -(-ITERS * depth // TILE) * TILE
-    above = lax.ppermute(coded[:, :, skipped:], "scan", [(i, i + 1) for i in range(scans - 1)])
-    below = lax.ppermute(coded[:, :, :needed], "scan", [(i + 1, i) for i in range(scans - 1)])
+    top, bottom = coded[:, :, :needed], coded[:, :, skipped:]
+    odds = range(1, scans - 1, 2)
+    chip = lax.ppermute(
+        jnp.where(upper, top, bottom), "scan", [(i, i + 1) for i in odds] + [(i + 1, i) for i in odds]
+    )
+    core = send(jnp.where(upper, bottom, top), other_core)
+    above, below = jnp.where(upper, chip, core), jnp.where(upper, core, chip)
     above, middle, below = [
         (c.astype(f32) * (1.0 / SCALE)).transpose(1, 0, 2, 3).reshape(-1, lanes) for c in (above, coded, below)
     ]

time: 98.3 us -> 101 us (1.027)
  the two profiles are of different devices: /device:TPU:1 before, /device:TPU:7 now
where the time goes in v5:
time: 101 us
  blocking collectives  34.8 us (34%)
  waiting for transfers between devices  22.7 us (22%)
  starting transfers between devices  20 us (20%)
  Pallas kernels  14 us (14%)
  other arithmetic  7.11 us (7%)
  local copies, waits for them, and re-layouts  1.68 us (2%)
    all_to_all x1, blocking collectives, on_device(): grad = lax.all_to_all(grad, 'cuts', 0, 0, tiled=True)  19.9 us
    ppermute x14, starting transfers between devices, send(): return lax.ppermute(array, 'scan', pairs[turn:] + pairs[:turn])  17.8 us
    all_to_all x1, blocking collectives, on_device(): coded = lax.all_to_all(coded, 'cuts', 0, 0, tiled=True)  14.9 us
    ppermute x14, waiting for transfers between devices, send(): return lax.ppermute(array, 'scan', pairs[turn:] + pairs[:turn])  14.5 us
    ppermute x1, waiting for transfers between devices, on_device(): lax.ppermute(jnp.where(upper, top, bottom), 'scan', [(i, i + 1) for i in...  8.12 us
    pallas_call x1, Pallas kernels, on_device(): pl.pallas_call(lambda *refs: tv_kernel(shape, skipped, *refs), out_shape=...  7.3 us
    pallas_call x2, Pallas kernels, copied(): pl.pallas_call(lambda *refs: copy_kernel(plan, *refs), out_shape=[jax.Sha...  5.57 us
    ppermute x1, starting transfers between devices, on_device(): lax.ppermute(jnp.where(upper, top, bottom), 'scan', [(i, i + 1) for i in...  2.2 us
  transfers between devices with their start and end apart: 15, of which 8 were waited for; matrix products, arithmetic and copies ran while one was open for 7% of the time, Pallas kernels for 4%

profile of v5, /device:TPU:7, one launch (start us, length us, event | category | flops | bytes accessed | tf_op | source)
XLA Modules:
  0.0 100.6 jit_solution(7020632121253963804)
XLA Ops:
  0.0 1.5 %shard_map.38 = (bf16[4,6,8,2048]{3,2,1,0:T(8,128)(2,1)S(1)}, bf16[4,6,8,2048]{3,2,1,0:T(8,128)(2,1)S(1)}) custom-call(bf16[2,6,4,2,2,8,2048]{6,5,4,3,2,1,0:T(8,128)(2,1)} %bitcast.98), custom_call_target="tpu_custom_call" | custom-call | bytes 3145728 | tf_op jit(solution)/shard_map/pallas_call | solution.py:164
  1.5 0.8 collective-permute-start
  2.3 4.0 %shard_map.37 = (bf16[12,6,8,2048]{3,2,1,0:T(8,128)(2,1)}, bf16[12,6,8,2048]{3,2,1,0:T(8,128)(2,1)S(1)}) custom-call(bf16[2,6,4,2,2,8,2048]{6,5,4,3,2,1,0:T(8,128)(2,1)} %bitcast.99), custom_call_target="tpu_custom_call" | custom-call | bytes 9437184 | tf_op jit(solution)/shard_map/pallas_call | solution.py:164
  6.6 0.7 copy-done.1
  7.5 1.4 %multiply_convert_fusion.3 = (f16[2,6,8,2048]{3,2,1,0:T(8,128)(2,1)S(1)}, f16[2,6,8,2048]{3,2,1,0:T(8,128)(2,1)S(1)}) fusion(bf16[4,6,8,2048]{3,2,1,0:T(8,128)(2,1)} %copy-done.1, bf16[4,6,8,2048]{3,2,1,0:T(8,128)(2,1)S(1)} %get-tuple-element.27), kind=kLoop, calls=%fused_computation.11 | loop fusion | flops 1966080 | bytes 2359296 | tf_op jit(solution)/shard_map/convert_element_type | solution.py:215
  8.9 1.4 %collective-permute-start.7 = (f16[2,6,8,2048]{3,2,1,0:T(8,128)(2,1)S(1)}, f16[2,6,8,2048]{3,2,1,0:T(8,128)(2,1)S(1)}, u32[]{:S(2)}, u32[]{:S(2)}) collective-permute-start(f16[2,6,8,2048]{3,2,1,0:T(8,128)(2,1)S(1)} %get-tuple-element.51), channel_id=1, source_target_pairs={{0,32},{16,48},{32,0},{48,16},{64,96},{80,112},{96,64},{112,80},{1... | collective-permute-start | bytes 1179656 | tf_op jit(solution)/shard_map/ppermute | solution.py:187
  10.3 0.7 collective-permute-start.2
  11.1 0.8 collective-permute-start.3
  11.9 2.0 %add_multiply_fusion = (f32[4,6,8,2048]{3,2,1,0:T(8,128)S(1)}, f16[4,6,8,2048]{3,2,1,0:T(8,128)(2,1)S(1)}, f32[4,6,8,2048]{3,2,1,0:T(8,128)S(1)}) fusion(bf16[12,6,8,2048]{3,2,1,0:T(8,128)(2,1)} %collective-permute-done.1, bf16[12,6,8,2048]{3,2,1,0:T(8,128)(2,1)S(1)} %get-tuple-element.23), kind=kLoop, calls=%fused_computation | loop fusion | flops 3538944 | bytes 7077888 | tf_op jit(solution)/shard_map/mul | solution.py:199
  13.9 1.1 %multiply_convert_fusion.2 = f16[2,6,8,2048]{3,2,1,0:T(8,128)(2,1)S(1)} fusion(bf16[12,6,8,2048]{3,2,1,0:T(8,128)(2,1)} %collective-permute-done.1, bf16[12,6,8,2048]{3,2,1,0:T(8,128)(2,1)S(1)} %get-tuple-element.23), kind=kLoop, calls=%fused_computation.10 | loop fusion | flops 983040 | bytes 1179648 | tf_op jit(solution)/shard_map/convert_element_type | solution.py:221
  15.1 0.8 collective-permute-start.8
  15.9 0.6 collective-permute-done.2
  16.6 1.9 %collective-permute-done.3 = f16[6,8,2048]{2,1,0:T(8,128)(2,1)S(1)} collective-permute-done((f16[6,8,2048]{2,1,0:T(8,128)(2,1)S(1)}, f16[6,8,2048]{2,1,0:T(8,128)(2,1)S(1)}, u32[]{:S(2)}, u32[]{:S(2)}) %collective-permute-start.3) | collective-permute-done | bytes 196640 | tf_op jit(solution)/shard_map/ppermute | solution.py:187
  18.7 0.4 collective-permute-start.4
  19.1 1.2 %collective-permute-start.5 = (f16[2,6,8,2048]{3,2,1,0:T(8,128)(2,1)S(1)}, f16[2,6,8,2048]{3,2,1,0:T(8,128)(2,1)S(1)}, u32[]{:S(2)}, u32[]{:S(2)}) collective-permute-start(f16[2,6,8,2048]{3,2,1,0:T(8,128)(2,1)S(1)} %pad_maximum_fusion.1), channel_id=1, source_target_pairs={{0,192},{16,208},{32,224},{48,240},{64,0},{80,16},{96,32},{112,48}... | collective-permute-start | bytes 1179656 | tf_op jit(solution)/shard_map/ppermute | solution.py:187
  20.5 1.6 %collective-permute-start.9 = (f16[3,8,2048]{2,1,0:T(8,128)(2,1)S(1)}, f16[3,8,2048]{2,1,0:T(8,128)(2,1)S(1)}, u32[]{:S(2)}, u32[]{:S(2)}) collective-permute-start(f16[3,8,2048]{2,1,0:T(8,128)(2,1)S(1)} %get-tuple-element.63), channel_id=1, source_target_pairs={{16,80},{32,96},{48,112},{64,128},{80,144},{96,160},{112,176},{128... | collective-permute-start | bytes 294920 | tf_op jit(solution)/shard_map/ppermute | solution.py:187
  22.2 6.0 %collective-permute-done.4 = f16[2,6,8,2048]{3,2,1,0:T(8,128)(2,1)S(1)} collective-permute-done((f16[2,6,8,2048]{3,2,1,0:T(8,128)(2,1)S(1)}, f16[2,6,8,2048]{3,2,1,0:T(8,128)(2,1)S(1)}, u32[]{:S(2)}, u32[]{:S(2)}) %collective-permute-start.4) | collective-permute-done | bytes 393248 | tf_op jit(solution)/shard_map/ppermute | solution.py:187
  28.2 1.7 %collective-permute-done.5 = f16[2,6,8,2048]{3,2,1,0:T(8,128)(2,1)S(1)} collective-permute-done((f16[2,6,8,2048]{3,2,1,0:T(8,128)(2,1)S(1)}, f16[2,6,8,2048]{3,2,1,0:T(8,128)(2,1)S(1)}, u32[]{:S(2)}, u32[]{:S(2)}) %collective-permute-start.5) | collective-permute-done | bytes 393248 | tf_op jit(solution)/shard_map/ppermute | solution.py:187
  29.9 1.2 %convert_add_fusion = f32[2,6,8,2048]{3,2,1,0:T(8,128)S(1)} fusion(f16[2,6,8,2048]{3,2,1,0:T(8,128)(2,1)S(1)} %collective-permute-done.5, f16[2,6,8,2048]{3,2,1,0:T(8,128)(2,1)S(1)} %collective-permute-done.4, bf16[12,6,8,2048]{3,2,1,0:T(8,128)(2,1)} %collective-permute-done.1, bf16[12,6,8,2048]{3,2,1,0:T(8,128)(2,1)S(1)} %get-tuple-element.23), kind=kLoop, calls=%fused_computation.9 | loop fusion | flops 1572864 | bytes 2359296 | tf_op jit(solution)/shard_map/add | solution.py:241
  31.1 1.0 collective-permute-start.6
  32.4 0.2 collective-permute-start.11
  32.6 1.6 %collective-permute-start.12 = (f16[6,8,2048]{2,1,0:T(8,128)(2,1)S(1)}, f16[6,8,2048]{2,1,0:T(8,128)(2,1)S(1)}, u32[]{:S(2)}, u32[]{:S(2)}) collective-permute-start(f16[6,8,2048]{2,1,0:T(8,128)(2,1)S(1)} %pad_maximum_fusion.3), channel_id=1, source_target_pairs={{32,224},{48,240},{64,0},{80,16},{96,32},{112,48},{128,64},{144,80... | collective-permute-start | bytes 589832 | tf_op jit(solution)/shard_map/ppermute | solution.py:187
  34.2 1.5 %collective-permute-done.6 = f16[6,8,2048]{2,1,0:T(8,128)(2,1)S(1)} collective-permute-done((f16[6,8,2048]{2,1,0:T(8,128)(2,1)S(1)}, f16[6,8,2048]{2,1,0:T(8,128)(2,1)S(1)}, u32[]{:S(2)}, u32[]{:S(2)}) %collective-permute-start.6) | collective-permute-done | bytes 196640 | tf_op jit(solution)/shard_map/ppermute | solution.py:187
  35.8 1.2 %collective-permute-done.11 = f16[6,8,2048]{2,1,0:T(8,128)(2,1)S(1)} collective-permute-done((f16[6,8,2048]{2,1,0:T(8,128)(2,1)S(1)}, f16[6,8,2048]{2,1,0:T(8,128)(2,1)S(1)}, u32[]{:S(2)}, u32[]{:S(2)}) %collective-permute-start.11) | collective-permute-done | bytes 196640 | tf_op jit(solution)/shard_map/ppermute | solution.py:187
  37.0 1.6 %collective-permute-done.12 = f16[6,8,2048]{2,1,0:T(8,128)(2,1)S(1)} collective-permute-done((f16[6,8,2048]{2,1,0:T(8,128)(2,1)S(1)}, f16[6,8,2048]{2,1,0:T(8,128)(2,1)S(1)}, u32[]{:S(2)}, u32[]{:S(2)}) %collective-permute-start.12) | collective-permute-done | bytes 196640 | tf_op jit(solution)/shard_map/ppermute | solution.py:187
  39.2 19.9 %all_to_all.10.grad_ref = bf16[16,2,6,8,128]{4,3,2,1,0:T(8,128)(2,1)S(1)} all-to-all(bf16[16,2,6,8,128]{4,3,2,1,0:T(8,128)(2,1)S(1)} %fusion.1), channel_id=1, replica_groups=mesh['scan'=16,'cuts'=16] {'cuts'}, dimensions={0} | all-to-all | bytes 786432 | tf_op jit(solution)/shard_map/all_to_all | solution.py:258
  59.2 1.1 %shard_map.39 = f32[1536,128]{1,0:T(8,128)S(1)} custom-call(bf16[16,2,6,8,128]{4,3,2,1,0:T(8,128)(2,1)S(1)} %all_to_all.10.grad_ref, bf16[96,768]{1,0:T(8,128)(2,1)S(1)} %reshape.41.weights_ref, s32[8,128]{1,0:T(8,128)S(1)} %copy-done), custom_call_target="tpu_custom_call" | custom-call | tf_op jit(solution)/shard_map/pallas_call | solution.py:260
  60.4 14.9 %all_to_all.11 = f16[16,96,128]{2,1,0:T(8,128)(2,1)S(1)} all-to-all(f16[16,96,128]{2,1,0:T(8,128)(2,1)S(1)} %bitcast.105), channel_id=1, replica_groups=mesh['scan'=16,'cuts'=16] {'cuts'}, dimensions={0} | all-to-all | bytes 786432 | tf_op jit(solution)/shard_map/all_to_all | solution.py:267
  75.4 7.1 %collective-permute-start.14 = (f16[16,2,32,128]{3,2,1,0:T(8,128)(2,1)S(1)}, f16[16,2,32,128]{3,2,1,0:T(8,128)(2,1)S(1)}, u32[]{:S(2)}, u32[]{:S(2)}) collective-permute-start(f16[16,2,32,128]{3,2,1,0:T(8,128)(2,1)S(1)} %get-tuple-element.58), channel_id=1, source_target_pairs={{0,16},{16,0},{32,48},{48,32},{64,80},{80,64},{96,112},{112,96},{1... | collective-permute-start | bytes 786440 | tf_op jit(solution)/shard_map/ppermute | solution.py:187
  82.5 2.2 %collective-permute-start.13 = (f16[16,2,32,128]{3,2,1,0:T(8,128)(2,1)S(1)}, f16[16,2,32,128]{3,2,1,0:T(8,128)(2,1)S(1)}, u32[]{:S(2)}, u32[]{:S(2)}) collective-permute-start(f16[16,2,32,128]{3,2,1,0:T(8,128)(2,1)S(1)} %get-tuple-element.59), channel_id=1, source_target_pairs={{16,32},{48,64},{80,96},{112,128},{144,160},{176,192},{208,224},{3... | collective-permute-start | bytes 786440 | tf_op jit(solution)/shard_map/ppermute | solution.py:273
  84.9 8.1 %collective-permute-done.13 = f16[16,2,32,128]{3,2,1,0:T(8,128)(2,1)S(1)} collective-permute-done((f16[16,2,32,128]{3,2,1,0:T(8,128)(2,1)S(1)}, f16[16,2,32,128]{3,2,1,0:T(8,128)(2,1)S(1)}, u32[]{:S(2)}, u32[]{:S(2)}) %collective-permute-start.13) | collective-permute-done | bytes 262176 | tf_op jit(solution)/shard_map/ppermute | solution.py:273
  93.3 7.3 %shard_map.40 = f32[12,128,128]{2,1,0:T(8,128)} custom-call(f32[1024,128]{1,0:T(8,128)S(1)} %bitcast.96, f32[1536,128]{1,0:T(8,128)S(1)} %bitcast.95, f32[1024,128]{1,0:T(8,128)S(1)} %bitcast.97), custom_call_target="tpu_custom_call" | custom-call | tf_op jit(solution)/shard_map/pallas_call | solution.py:282
  (44 shorter events, 2.5 us)
Async XLA Ops:
  1.5 5.0 %copy-start.2 = (bf16[8,96,96]{2,1,0:T(8,128)(2,1)S(1)}, bf16[8,96,96]{2,1,0:T(8,128)(2,1)}, u32[]{:S(2)}) copy-start(bf16[8,96,96]{2,1,0:T(8,128)(2,1)} %param.4) | copy-start | bytes 442372
  1.5 4.8 %collective-permute-start = (bf16[4,6,8,2048]{3,2,1,0:T(8,128)(2,1)S(1)}, bf16[4,6,8,2048]{3,2,1,0:T(8,128)(2,1)S(1)}, u32[]{:S(2)}, u32[]{:S(2)}) collective-permute-start(bf16[4,6,8,2048]{3,2,1,0:T(8,128)(2,1)S(1)} %get-tuple-element.25), channel_id=1, source_target_pairs={{0,16},{16,0},{32,48},{48,32},{64,80},{80,64},{96,112},{112,96},{1... | collective-permute-start | bytes 2359304 | tf_op jit(solution)/shard_map/ppermute | solution.py:187
  6.4 0.9 copy-start.1
  6.4 5.5 %collective-permute-start.1 = (bf16[12,6,8,2048]{3,2,1,0:T(8,128)(2,1)}, bf16[12,6,8,2048]{3,2,1,0:T(8,128)(2,1)}, u32[]{:S(2)}, u32[]{:S(2)}) collective-permute-start(bf16[12,6,8,2048]{3,2,1,0:T(8,128)(2,1)} %get-tuple-element.26), channel_id=1, source_target_pairs={{16,0},{32,48},{48,32},{64,80},{80,64},{96,112},{112,96},{128,144}... | collective-permute-start | bytes 7077896 | tf_op jit(solution)/shard_map/ppermute | solution.py:187
  8.9 11.5 %collective-permute-start.7 = (f16[2,6,8,2048]{3,2,1,0:T(8,128)(2,1)S(1)}, f16[2,6,8,2048]{3,2,1,0:T(8,128)(2,1)S(1)}, u32[]{:S(2)}, u32[]{:S(2)}) collective-permute-start(f16[2,6,8,2048]{3,2,1,0:T(8,128)(2,1)S(1)} %get-tuple-element.51), channel_id=1, source_target_pairs={{0,32},{16,48},{32,0},{48,16},{64,96},{80,112},{96,64},{112,80},{1... | collective-permute-start | bytes 1179656 | tf_op jit(solution)/shard_map/ppermute | solution.py:187
  10.3 6.2 %collective-permute-start.2 = (f16[6,8,2048]{2,1,0:T(8,128)(2,1)S(1)}, f16[6,8,2048]{2,1,0:T(8,128)(2,1)S(1)}, u32[]{:S(2)}, u32[]{:S(2)}) collective-permute-start(f16[6,8,2048]{2,1,0:T(8,128)(2,1)S(1)} %get-tuple-element.65), channel_id=1, source_target_pairs={{0,64},{16,80},{32,96},{48,112},{64,128},{80,144},{96,160},{112,17... | collective-permute-start | bytes 589832 | tf_op jit(solution)/shard_map/ppermute | solution.py:187
  11.1 7.4 %collective-permute-start.3 = (f16[6,8,2048]{2,1,0:T(8,128)(2,1)S(1)}, f16[6,8,2048]{2,1,0:T(8,128)(2,1)S(1)}, u32[]{:S(2)}, u32[]{:S(2)}) collective-permute-start(f16[6,8,2048]{2,1,0:T(8,128)(2,1)S(1)} %get-tuple-element.64), channel_id=1, source_target_pairs={{0,192},{16,208},{32,224},{48,240},{64,0},{80,16},{96,32},{112,48}... | collective-permute-start | bytes 589832 | tf_op jit(solution)/shard_map/ppermute | solution.py:187
  15.1 17.0 %collective-permute-start.8 = (f16[2,6,8,2048]{3,2,1,0:T(8,128)(2,1)S(1)}, f16[2,6,8,2048]{3,2,1,0:T(8,128)(2,1)S(1)}, u32[]{:S(2)}, u32[]{:S(2)}) collective-permute-start(f16[2,6,8,2048]{3,2,1,0:T(8,128)(2,1)S(1)} %multiply_convert_fusion.2), channel_id=1, source_target_pairs={{16,48},{32,0},{48,16},{64,96},{80,112},{96,64},{112,80},{128,160}... | collective-permute-start | bytes 1179656 | tf_op jit(solution)/shard_map/ppermute | solution.py:187
  18.7 9.5 %collective-permute-start.4 = (f16[2,6,8,2048]{3,2,1,0:T(8,128)(2,1)S(1)}, f16[2,6,8,2048]{3,2,1,0:T(8,128)(2,1)S(1)}, u32[]{:S(2)}, u32[]{:S(2)}) collective-permute-start(f16[2,6,8,2048]{3,2,1,0:T(8,128)(2,1)S(1)} %pad_maximum_fusion), channel_id=1, source_target_pairs={{0,64},{16,80},{32,96},{48,112},{64,128},{80,144},{96,160},{112,17... | collective-permute-start | bytes 1179656 | tf_op jit(solution)/shard_map/ppermute | solution.py:187
  19.1 10.7 %collective-permute-start.5 = (f16[2,6,8,2048]{3,2,1,0:T(8,128)(2,1)S(1)}, f16[2,6,8,2048]{3,2,1,0:T(8,128)(2,1)S(1)}, u32[]{:S(2)}, u32[]{:S(2)}) collective-permute-start(f16[2,6,8,2048]{3,2,1,0:T(8,128)(2,1)S(1)} %pad_maximum_fusion.1), channel_id=1, source_target_pairs={{0,192},{16,208},{32,224},{48,240},{64,0},{80,16},{96,32},{112,48}... | collective-permute-start | bytes 1179656 | tf_op jit(solution)/shard_map/ppermute | solution.py:187
  20.5 11.5 %collective-permute-start.9 = (f16[3,8,2048]{2,1,0:T(8,128)(2,1)S(1)}, f16[3,8,2048]{2,1,0:T(8,128)(2,1)S(1)}, u32[]{:S(2)}, u32[]{:S(2)}) collective-permute-start(f16[3,8,2048]{2,1,0:T(8,128)(2,1)S(1)} %get-tuple-element.63), channel_id=1, source_target_pairs={{16,80},{32,96},{48,112},{64,128},{80,144},{96,160},{112,176},{128... | collective-permute-start | bytes 294920 | tf_op jit(solution)/shard_map/ppermute | solution.py:187
  22.2 9.9 %collective-permute-start.10 = (f16[3,8,2048]{2,1,0:T(8,128)(2,1)S(1)}, f16[3,8,2048]{2,1,0:T(8,128)(2,1)S(1)}, u32[]{:S(2)}, u32[]{:S(2)}) collective-permute-start(f16[3,8,2048]{2,1,0:T(8,128)(2,1)S(1)} %get-tuple-element.62), channel_id=1, source_target_pairs={{16,208},{32,224},{48,240},{64,0},{80,16},{96,32},{112,48},{128,64... | collective-permute-start | bytes 294920 | tf_op jit(solution)/shard_map/ppermute | solution.py:187
  31.1 4.6 %collective-permute-start.6 = (f16[6,8,2048]{2,1,0:T(8,128)(2,1)S(1)}, f16[6,8,2048]{2,1,0:T(8,128)(2,1)S(1)}, u32[]{:S(2)}, u32[]{:S(2)}) collective-permute-start(f16[6,8,2048]{2,1,0:T(8,128)(2,1)S(1)} %fusion.12), channel_id=1, source_target_pairs={{32,0},{48,16},{64,96},{80,112},{96,64},{112,80},{128,160},{144,17... | collective-permute-start | bytes 589832 | tf_op jit(solution)/shard_map/ppermute | solution.py:187
  32.4 4.6 %collective-permute-start.11 = (f16[6,8,2048]{2,1,0:T(8,128)(2,1)S(1)}, f16[6,8,2048]{2,1,0:T(8,128)(2,1)S(1)}, u32[]{:S(2)}, u32[]{:S(2)}) collective-permute-start(f16[6,8,2048]{2,1,0:T(8,128)(2,1)S(1)} %pad_maximum_fusion.2), channel_id=1, source_target_pairs={{32,96},{48,112},{64,128},{80,144},{96,160},{112,176},{128,192},{1... | collective-permute-start | bytes 589832 | tf_op jit(solution)/shard_map/ppermute | solution.py:187
  32.6 6.0 %collective-permute-start.12 = (f16[6,8,2048]{2,1,0:T(8,128)(2,1)S(1)}, f16[6,8,2048]{2,1,0:T(8,128)(2,1)S(1)}, u32[]{:S(2)}, u32[]{:S(2)}) collective-permute-start(f16[6,8,2048]{2,1,0:T(8,128)(2,1)S(1)} %pad_maximum_fusion.3), channel_id=1, source_target_pairs={{32,224},{48,240},{64,0},{80,16},{96,32},{112,48},{128,64},{144,80... | collective-permute-start | bytes 589832 | tf_op jit(solution)/shard_map/ppermute | solution.py:187
  39.0 20.2 %copy-start = (s32[8,128]{1,0:T(8,128)S(1)}, s32[8,128]{1,0:T(8,128)}, u32[]{:S(2)}) copy-start(s32[8,128]{1,0:T(8,128)} %classes_ref.1) | copy-start | bytes 12292
  75.4 9.5 %collective-permute-start.14 = (f16[16,2,32,128]{3,2,1,0:T(8,128)(2,1)S(1)}, f16[16,2,32,128]{3,2,1,0:T(8,128)(2,1)S(1)}, u32[]{:S(2)}, u32[]{:S(2)}) collective-permute-start(f16[16,2,32,128]{3,2,1,0:T(8,128)(2,1)S(1)} %get-tuple-element.58), channel_id=1, source_target_pairs={{0,16},{16,0},{32,48},{48,32},{64,80},{80,64},{96,112},{112,96},{1... | collective-permute-start | bytes 786440 | tf_op jit(solution)/shard_map/ppermute | solution.py:187
  82.5 10.5 %collective-permute-start.13 = (f16[16,2,32,128]{3,2,1,0:T(8,128)(2,1)S(1)}, f16[16,2,32,128]{3,2,1,0:T(8,128)(2,1)S(1)}, u32[]{:S(2)}, u32[]{:S(2)}) collective-permute-start(f16[16,2,32,128]{3,2,1,0:T(8,128)(2,1)S(1)} %get-tuple-element.59), channel_id=1, source_target_pairs={{16,32},{48,64},{80,96},{112,128},{144,160},{176,192},{208,224},{3... | collective-permute-start | bytes 786440 | tf_op jit(solution)/shard_map/ppermute | solution.py:273

commit v6 on v5

--- a/solution.py
+++ b/solution.py
@@ -47,92 +47,155 @@
                 ]
 
 
-def tv_kernel(shape, skipped, above_ref, own_ref, below_ref, out_ref, field):
-    blocks, parts, depth, rows, lanes = shape
-    halo = ITERS
-    tiles = range(WAYS)
-    groups = blocks // WAYS
-    lines = parts * groups
-    size = lanes // WAYS
-    first = (lax.axis_index("scan") == 0).astype(jnp.float32)
-    last = (lax.axis_index("scan") == lax.axis_size("scan") - 1).astype(jnp.float32)
-    lane = lax.broadcasted_iota(jnp.int32, (lines, lanes), 1)
-    line = lax.broadcasted_iota(jnp.int32, (lines, lanes), 0)
-    at_left = lane == 0
-    at_right = lane == lanes - 1
-    inner = jnp.where(at_right & (lax.rem(line, groups) == groups - 1), 0.0, 1.0)
-    homes = [home(lane, b, lanes) for b in tiles]
-
-    def skewed(values):
+class Tiles:
+    def __init__(self, shape):
+        self.blocks, self.parts, self.depth, self.rows, self.lanes = shape
+        self.groups = self.blocks // WAYS
+        self.lines = self.parts * self.groups
+        self.size = self.lanes // WAYS
+        self.lane = lax.broadcasted_iota(jnp.int32, (self.lines, self.lanes), 1)
+        line = lax.broadcasted_iota(jnp.int32, (self.lines, self.lanes), 0)
+        self.at_left = self.lane == 0
+        self.at_right = self.lane == self.lanes - 1
+        self.inner = jnp.where(self.at_right & (lax.rem(line, self.groups) == self.groups - 1), 0.0, 1.0)
+
+    def skewed(self, values):
         found = []
-        for m in tiles:
+        for m in range(WAYS):
             pick = values[-m % WAYS]
             for group in range(1, WAYS):
-                pick = jnp.where(lane // size == group, values[(group - m) % WAYS], pick)
+                pick = jnp.where(self.lane // self.size == group, values[(group - m) % WAYS], pick)
             found.append(pick)
         return found
 
-    def load(s, row):
-        if row < 0:
-            source, at = above_ref, (row + rows) * depth - skipped
-        elif row < rows:
-            source, at = own_ref, row * depth
-        else:
-            source, at = below_ref, (row - rows) * depth
-        per = source.shape[0] // (blocks * parts)
-        found = skewed([source[pl.ds(b * per + at + s, lines, stride=WAYS * per), :] for b in tiles])
-        return [pltpu.roll(f, (lanes - size * m) % lanes, 1) for m, f in enumerate(found)]
-
-    def store(s, row, values):
-        values = skewed([pltpu.roll(v, size * m, 1) for m, v in enumerate(values)])
-        for b in tiles:
-            value = jnp.take_along_axis(values[b], homes[b], axis=1)
-            for part in range(parts):
-                out_ref[part * depth + s, pl.ds(b * rows + row, groups, stride=WAYS * rows), :] = value[
-                    part * groups : (part + 1) * groups
+    def load(self, source, at):
+        per = source.shape[0] // (self.blocks * self.parts)
+        found = [source[pl.ds(b * per + at, self.lines, stride=WAYS * per), :] for b in range(WAYS)]
+        return [
+            pltpu.roll(f, (self.lanes - self.size * m) % self.lanes, 1) for m, f in enumerate(self.skewed(found))
+        ]
+
+    def store(self, out_ref, s, row, values):
+        values = self.skewed([pltpu.roll(v, self.size * m, 1) for m, v in enumerate(values)])
+        for b in range(WAYS):
+            value = jnp.take_along_axis(values[b], home(self.lane, b, self.lanes), axis=1)
+            for part in range(self.parts):
+                out_ref[part * self.depth + s, pl.ds(b * self.rows + row, self.groups, stride=WAYS * self.rows), :] = (
+                    value[part * self.groups : (part + 1) * self.groups]
+                )
+
+    def sweep(self, low, high, read, write, edges=()):
+        before = None
+        here = read(low - 1)
+        for row in range(low - 1, high):
+            below = read(row + 1)
+            down = [b - h for b, h in zip(below, here)]
+            for edge, factor in edges:
+                if row == edge:
+                    down = [d * factor for d in down]
+            near = pltpu.roll(here[0], self.lanes - 1, 1)
+            near = jnp.where(self.at_right, pltpu.roll(near, self.lines - 1, 0), near)
+            across = [n - h for n, h in zip(here[1:] + [near], here)]
+            across[-1] = across[-1] * self.inner
+            power = [d * d + a * a for d, a in zip(down, across)]
+            inverse = [lax.rsqrt(p + pltpu.roll(p, self.groups, 0) + 1.0) for p in power]
+            flux = [d * i for d, i in zip(down, inverse)]
+            if before is not None:
+                sides = [a * i for a, i in zip(across, inverse)]
+                near = pltpu.roll(sides[-1], 1, 1)
+                near = jnp.where(self.at_left, pltpu.roll(near, 1, 0), near)
+                fresh = [
+                    h + 0.2 * (f - b + s1 - s0)
+                    for h, f, b, s1, s0 in zip(here, flux, before, sides, [near] + sides[:-1])
                 ]
-
-    def one_slice(s, carry):
-        for sweep in range(1, ITERS + 1):
-            low, high = sweep - ITERS, rows + ITERS - sweep
-
-            def read(row):
-                return load(s, row) if sweep == 1 else [field[row + halo, m] for m in tiles]
-
-            before = None
-            here = read(low - 1)
-            for row in range(low - 1, high):
-                below = read(row + 1)
-                down = [b - h for b, h in zip(below, here)]
-                if row == -1:
-                    down = [d * (1.0 - first) for d in down]
-                if row == rows - 1:
-                    down = [d * (1.0 - last) for d in down]
-                near = pltpu.roll(here[0], lanes - 1, 1)
-                near = jnp.where(at_right, pltpu.roll(near, lines - 1, 0), near)
-                across = [n - h for n, h in zip(here[1:] + [near], here)]
-                across[-1] = across[-1] * inner
-                power = [d * d + a * a for d, a in zip(down, across)]
-                inverse = [lax.rsqrt(p + pltpu.roll(p, groups, 0) + 1.0) for p in power]
-                flux = [d * i for d, i in zip(down, inverse)]
-                if before is not None:
-                    sides = [a * i for a, i in zip(across, inverse)]
-                    near = pltpu.roll(sides[-1], 1, 1)
-                    near = jnp.where(at_left, pltpu.roll(near, 1, 0), near)
-                    fresh = [
-                        h + 0.2 * (f - b + s1 - s0)
-                        for h, f, b, s1, s0 in zip(here, flux, before, sides, [near] + sides[:-1])
-                    ]
-                    if sweep == ITERS:
-                        store(s, row, fresh)
+                write(row, here, fresh)
+            before = flux
+            here = below
+
+
+def near_kernel(shape, skipped, own_ref, core_ref, out_ref, edge_ref, field):
+    tiles = Tiles(shape)
+    rows, depth, halo = tiles.rows, tiles.depth, ITERS
+    out_ref[...] = jnp.zeros_like(out_ref)
+
+    def on(upper):
+        def one_slice(s, carry):
+            for step in range(1, ITERS + 1):
+                low, high = (step, rows + ITERS - step) if upper else (step - ITERS, rows - step)
+                side, kept = (low - 1, low) if upper else (high, high - 1)
+
+                def read(row):
+                    if step > 1:
+                        return [field[row + halo, m] for m in range(WAYS)]
+                    if 0 <= row < rows:
+                        return tiles.load(own_ref, row * depth + s)
+                    return tiles.load(core_ref, ((row - rows) if upper else (row + rows)) * depth - (0 if upper else skipped) + s)
+
+                def seen(row):
+                    values = read(row)
+                    if row == side:
+                        for m in range(WAYS):
+                            edge_ref[s, step - 1, 0, m] = values[m]
+                    return values
+
+                def write(row, here, fresh):
+                    if row == kept:
+                        for m in range(WAYS):
+                            edge_ref[s, step - 1, 1, m] = here[m]
+                    if step == ITERS:
+                        tiles.store(out_ref, s, row, fresh)
                     else:
-                        for m in tiles:
+                        for m in range(WAYS):
                             field[row + halo, m] = fresh[m]
-                before = flux
-                here = below
-        return carry
-
-    lax.fori_loop(0, depth, one_slice, 0)
+
+                tiles.sweep(low, high, seen, write)
+            return carry
+
+        lax.fori_loop(0, depth, one_slice, 0)
+
+    core = lax.rem(lax.axis_index("scan"), 2)
+    pl.when(core == 0)(lambda: on(True))
+    pl.when(core == 1)(lambda: on(False))
+
+
+def far_kernel(shape, skipped, chip_ref, edge_ref, done_ref, out_ref, field):
+    tiles = Tiles(shape)
+    rows, depth, halo = tiles.rows, tiles.depth, ITERS
+    out_ref[...] = done_ref[...]
+    me = lax.axis_index("scan")
+    first = jnp.where(me == 0, 0.0, 1.0)
+    last = jnp.where(me == lax.axis_size("scan") - 1, 0.0, 1.0)
+
+    def on(upper):
+        def one_slice(s, carry):
+            for step in range(1, ITERS + 1):
+                low, high = (step - ITERS, step) if upper else (rows - step, rows + ITERS - step)
+                side, kept = (high - 1, high) if upper else (low, low - 1)
+
+                def read(row):
+                    if row == side:
+                        return [edge_ref[s, step - 1, 0, m] for m in range(WAYS)]
+                    if row == kept:
+                        return [edge_ref[s, step - 1, 1, m] for m in range(WAYS)]
+                    if step > 1:
+                        return [field[row + halo, m] for m in range(WAYS)]
+                    return tiles.load(chip_ref, ((row + rows) if upper else (row - rows)) * depth - (skipped if upper else 0) + s)
+
+                def write(row, here, fresh):
+                    if step == ITERS:
+                        tiles.store(out_ref, s, row, fresh)
+                    else:
+                        for m in range(WAYS):
+                            field[row + halo, m] = fresh[m]
+
+                tiles.sweep(low, high, read, write, [(-1, first)] if upper else [(rows - 1, last)])
+            return carry
+
+        lax.fori_loop(0, depth, one_slice, 0)
+
+    core = lax.rem(me, 2)
+    pl.when(core == 0)(lambda: on(True))
+    pl.when(core == 1)(lambda: on(False))
 
 
 def copy_kernel(plan, source_ref, *refs):
@@ -168,7 +231,7 @@
         out_specs=[pl.BlockSpec(memory_space=pltpu.VMEM)] * len(plan),
         scratch_shapes=[pltpu.SemaphoreType.DMA((sum(len(pieces) for _, pieces in plan),))],
         cost_estimate=pl.CostEstimate(flops=0, bytes_accessed=moved, transcendentals=0),
-        compiler_params=pltpu.CompilerParams(vmem_limit_bytes=24 * 1024 * 1024),
+        compiler_params=pltpu.CompilerParams(vmem_limit_bytes=moved + 2 * 1024 * 1024),
     )(split)
 
 
@@ -198,8 +261,6 @@
     def paired(own, got):
         return (own.astype(f32) + got.astype(f32)) * SUM_SCALE
 
-    weights = inverses.reshape(kinds, cuts, depth, total).transpose(2, 1, 0, 3).reshape(total, kinds * total)
-
     def after(value, made):
         return lax.optimization_barrier((value, made))[0]
 
@@ -248,11 +309,11 @@
     to_left1 = jnp.concatenate([near1[1, :half], near1[1, half:] + from_right1.astype(f32)]).astype(f16)
     x_left1 = send(to_right1, along_x(1), 2)
     x_right1 = send(to_left1, along_x(3), 2)
-    x_left1, x_right1 = after((x_left1, x_right1), part0)
     part1 = far1[1] + x_left1.astype(f32) + x_right1.astype(f32)
 
     grad = (jnp.stack([part0, part1]) * (1.0 / SUM_SCALE)).astype(jnp.bfloat16)
     grad = grad.reshape(parts, depth, rows, cuts, lanes).transpose(3, 0, 1, 2, 4)
+    weights = after(inverses, last).reshape(kinds, cuts, depth, total).transpose(2, 1, 0, 3).reshape(total, kinds * total)
     upper = lax.axis_index("scan") & 1 == 0
     grad, weights, upper = lax.optimization_barrier((grad, weights, upper))
     grad = lax.all_to_all(grad, "cuts", 0, 0, tiled=True)
@@ -261,7 +322,7 @@
         filter_kernel,
         out_shape=jax.ShapeDtypeStruct((cuts * per, lanes), f32),
         scratch_shapes=[pltpu.VMEM((parts, total * rows, lanes), f32)],
-        compiler_params=pltpu.CompilerParams(vmem_limit_bytes=32 * 1024 * 1024),
+        compiler_params=pltpu.CompilerParams(vmem_limit_bytes=16 * 1024 * 1024),
     )(grad, weights, classes)
     coded = (filtered * SCALE).astype(f16).reshape(cuts, per, lanes)
     coded = lax.all_to_all(coded, "cuts", 0, 0, tiled=True)
@@ -273,18 +334,31 @@
     chip = lax.ppermute(
         jnp.where(upper, top, bottom), "scan", [(i, i + 1) for i in odds] + [(i + 1, i) for i in odds]
     )
-    core = send(jnp.where(upper, bottom, top), other_core)
-    above, below = jnp.where(upper, chip, core), jnp.where(upper, core, chip)
-    above, middle, below = [
-        (c.astype(f32) * (1.0 / SCALE)).transpose(1, 0, 2, 3).reshape(-1, lanes) for c in (above, coded, below)
-    ]
+
+    def plain(array):
+        return (array.astype(f32) * (1.0 / SCALE)).transpose(1, 0, 2, 3).reshape(-1, lanes)
+
+    middle = plain(coded)
+    core = send(after(jnp.where(upper, bottom, top), middle), other_core)
     shape = (cuts, parts, depth, rows, lanes)
+    lines = parts * cuts // WAYS
+    out = jax.ShapeDtypeStruct((parts * depth, cuts * rows, lanes), f32)
+    field = pltpu.VMEM((rows + 2 * ITERS, WAYS, lines, lanes), f32)
+    work = cuts * rows * parts * depth * lanes
+    done, edges = pl.pallas_call(
+        lambda *refs: near_kernel(shape, skipped, *refs),
+        out_shape=[out, jax.ShapeDtypeStruct((depth, ITERS, 2, WAYS, lines, lanes), f32)],
+        scratch_shapes=[field],
+        cost_estimate=pl.CostEstimate(flops=0, bytes_accessed=16 * work, transcendentals=0),
+        compiler_params=pltpu.CompilerParams(vmem_limit_bytes=12 * 1024 * 1024),
+    )(middle, plain(core))
+    chip, edges, done = lax.optimization_barrier((chip, edges, done))
     result = pl.pallas_call(
-        lambda *refs: tv_kernel(shape, skipped, *refs),
-        out_shape=jax.ShapeDtypeStruct((parts * depth, cuts * rows, lanes), f32),
-        scratch_shapes=[pltpu.VMEM((rows + 2 * ITERS, WAYS, parts * cuts // WAYS, lanes), f32)],
-        compiler_params=pltpu.CompilerParams(vmem_limit_bytes=32 * 1024 * 1024),
-    )(above, middle, below)
+        lambda *refs: far_kernel(shape, skipped, *refs),
+        out_shape=out,
+        scratch_shapes=[field],
+        compiler_params=pltpu.CompilerParams(vmem_limit_bytes=12 * 1024 * 1024),
+    )(plain(chip), edges, done)
     result = result.reshape(parts, depth, cuts, rows, lanes).transpose(0, 1, 3, 2, 4)
     return result.reshape(parts, depth, rows, width)
 

time: 101 us -> 96.3 us (0.953)
  the two profiles are of different devices: /device:TPU:7 before, /device:TPU:1 now
where the time goes in v6:
time: 96.3 us; the launch traced here: 95.4 us
  blocking collectives  34.8 us (36%)
  starting transfers between devices  24.8 us (26%)
  Pallas kernels  17.2 us (18%)
  waiting for transfers between devices  14.6 us (15%)
  other arithmetic  2.63 us (3%)
  local copies, waits for them, and re-layouts  1.03 us (1%)
    ppermute x14, starting transfers between devices, send(): return lax.ppermute(array, 'scan', pairs[turn:] + pairs[:turn])  22.9 us
    all_to_all x1, blocking collectives, on_device(): grad = lax.all_to_all(grad, 'cuts', 0, 0, tiled=True)  20 us
    all_to_all x1, blocking collectives, on_device(): coded = lax.all_to_all(coded, 'cuts', 0, 0, tiled=True)  14.8 us
    ppermute x14, waiting for transfers between devices, send(): return lax.ppermute(array, 'scan', pairs[turn:] + pairs[:turn])  14.3 us
    pallas_call x1, Pallas kernels, on_device(): pl.pallas_call(lambda *refs: far_kernel(shape, skipped, *refs), out_shape...  6.28 us
    pallas_call x1, Pallas kernels, on_device(): pl.pallas_call(lambda *refs: near_kernel(shape, skipped, *refs), out_shap...  5.71 us
    pallas_call x2, Pallas kernels, copied(): pl.pallas_call(lambda *refs: copy_kernel(plan, *refs), out_shape=[jax.Sha...  4.15 us
  transfers between devices with their start and end apart: 15, of which 7 were waited for; matrix products, arithmetic and copies ran while one was open for 3% of the time, Pallas kernels for 9%

profile of v6, /device:TPU:1, one launch (start us, length us, event | category | flops | bytes accessed | tf_op | source)
XLA Modules:
  0.0 95.4 jit_solution(8431955599170734408)
XLA Ops:
  0.0 1.5 %shard_map.38 = (bf16[4,6,8,2048]{3,2,1,0:T(8,128)(2,1)S(1)}, bf16[4,6,8,2048]{3,2,1,0:T(8,128)(2,1)S(1)}) custom-call(bf16[2,6,4,2,2,8,2048]{6,5,4,3,2,1,0:T(8,128)(2,1)} %bitcast.101), custom_call_target="tpu_custom_call" | custom-call | bytes 3145728 | tf_op jit(solution)/shard_map/pallas_call | solution.py:227
  1.5 3.3 %collective-permute-start = (bf16[4,6,8,2048]{3,2,1,0:T(8,128)(2,1)S(1)}, bf16[4,6,8,2048]{3,2,1,0:T(8,128)(2,1)S(1)}, u32[]{:S(2)}, u32[]{:S(2)}) collective-permute-start(bf16[4,6,8,2048]{3,2,1,0:T(8,128)(2,1)S(1)} %get-tuple-element.30), channel_id=1, source_target_pairs={{0,16},{16,0},{32,48},{48,32},{64,80},{80,64},{96,112},{112,96},{1... | collective-permute-start | bytes 2359304 | tf_op jit(solution)/shard_map/ppermute | solution.py:250
  4.9 2.6 %shard_map.37 = (bf16[12,6,8,2048]{3,2,1,0:T(8,128)(2,1)S(1)}, bf16[12,6,8,2048]{3,2,1,0:T(8,128)(2,1)S(1)}) custom-call(bf16[2,6,4,2,2,8,2048]{6,5,4,3,2,1,0:T(8,128)(2,1)} %bitcast.102), custom_call_target="tpu_custom_call" | custom-call | bytes 9437184 | tf_op jit(solution)/shard_map/pallas_call | solution.py:227
  7.6 0.3 multiply_convert_fusion.3
  8.1 0.8 collective-permute-start.2
  8.9 1.9 %collective-permute-start.3 = (f16[6,8,2048]{2,1,0:T(8,128)(2,1)S(1)}, f16[6,8,2048]{2,1,0:T(8,128)(2,1)S(1)}, u32[]{:S(2)}, u32[]{:S(2)}) collective-permute-start(f16[6,8,2048]{2,1,0:T(8,128)(2,1)S(1)} %get-tuple-element.72), channel_id=1, source_target_pairs={{0,192},{16,208},{32,224},{48,240},{64,0},{80,16},{96,32},{112,48}... | collective-permute-start | bytes 589832 | tf_op jit(solution)/shard_map/ppermute | solution.py:250
  10.9 1.3 %collective-permute-done.1 = bf16[12,6,8,2048]{3,2,1,0:T(8,128)(2,1)S(1)} collective-permute-done((bf16[12,6,8,2048]{3,2,1,0:T(8,128)(2,1)S(1)}, bf16[12,6,8,2048]{3,2,1,0:T(8,128)(2,1)S(1)}, u32[]{:S(2)}, u32[]{:S(2)}) %collective-permute-start.1) | collective-permute-done | bytes 2359328 | tf_op jit(solution)/shard_map/ppermute | solution.py:250
  12.1 0.6 add_multiply_fusion
  12.8 0.1 multiply_convert_fusion.2
  13.0 0.3 collective-permute-start.8
  13.3 2.1 %collective-permute-done.2 = f16[6,8,2048]{2,1,0:T(8,128)(2,1)S(1)} collective-permute-done((f16[6,8,2048]{2,1,0:T(8,128)(2,1)S(1)}, f16[6,8,2048]{2,1,0:T(8,128)(2,1)S(1)}, u32[]{:S(2)}, u32[]{:S(2)}) %collective-permute-start.2) | collective-permute-done | bytes 196640 | tf_op jit(solution)/shard_map/ppermute | solution.py:250
  15.6 0.2 collective-permute-start.4
  15.9 2.6 %collective-permute-start.5 = (f16[2,6,8,2048]{3,2,1,0:T(8,128)(2,1)S(1)}, f16[2,6,8,2048]{3,2,1,0:T(8,128)(2,1)S(1)}, u32[]{:S(2)}, u32[]{:S(2)}) collective-permute-start(f16[2,6,8,2048]{3,2,1,0:T(8,128)(2,1)S(1)} %pad_maximum_fusion.1), channel_id=1, source_target_pairs={{0,192},{16,208},{32,224},{48,240},{64,0},{80,16},{96,32},{112,48}... | collective-permute-start | bytes 1179656 | tf_op jit(solution)/shard_map/ppermute | solution.py:250
  18.8 2.7 %collective-permute-start.10 = (f16[3,8,2048]{2,1,0:T(8,128)(2,1)S(1)}, f16[3,8,2048]{2,1,0:T(8,128)(2,1)S(1)}, u32[]{:S(2)}, u32[]{:S(2)}) collective-permute-start(f16[3,8,2048]{2,1,0:T(8,128)(2,1)S(1)} %get-tuple-element.70), channel_id=1, source_target_pairs={{16,208},{32,224},{48,240},{64,0},{80,16},{96,32},{112,48},{128,64... | collective-permute-start | bytes 294920 | tf_op jit(solution)/shard_map/ppermute | solution.py:250
  21.5 4.7 %collective-permute-done.4 = f16[2,6,8,2048]{3,2,1,0:T(8,128)(2,1)S(1)} collective-permute-done((f16[2,6,8,2048]{3,2,1,0:T(8,128)(2,1)S(1)}, f16[2,6,8,2048]{3,2,1,0:T(8,128)(2,1)S(1)}, u32[]{:S(2)}, u32[]{:S(2)}) %collective-permute-start.4) | collective-permute-done | bytes 393248 | tf_op jit(solution)/shard_map/ppermute | solution.py:250
  26.2 0.2 convert_add_fusion
  26.5 1.8 %collective-permute-done.9 = f16[3,8,2048]{2,1,0:T(8,128)(2,1)S(1)} collective-permute-done((f16[3,8,2048]{2,1,0:T(8,128)(2,1)S(1)}, f16[3,8,2048]{2,1,0:T(8,128)(2,1)S(1)}, u32[]{:S(2)}, u32[]{:S(2)}) %collective-permute-start.9) | collective-permute-done | bytes 98336 | tf_op jit(solution)/shard_map/ppermute | solution.py:250
  28.3 0.1 fusion.19
  28.6 2.6 %collective-permute-start.12 = (f16[6,8,2048]{2,1,0:T(8,128)(2,1)S(1)}, f16[6,8,2048]{2,1,0:T(8,128)(2,1)S(1)}, u32[]{:S(2)}, u32[]{:S(2)}) collective-permute-start(f16[6,8,2048]{2,1,0:T(8,128)(2,1)S(1)} %pad_maximum_fusion.3), channel_id=1, source_target_pairs={{32,224},{48,240},{64,0},{80,16},{96,32},{112,48},{128,64},{144,80... | collective-permute-start | bytes 589832 | tf_op jit(solution)/shard_map/ppermute | solution.py:250
  31.4 1.1 %collective-permute-start.6 = (f16[6,8,2048]{2,1,0:T(8,128)(2,1)S(1)}, f16[6,8,2048]{2,1,0:T(8,128)(2,1)S(1)}, u32[]{:S(2)}, u32[]{:S(2)}) collective-permute-start(f16[6,8,2048]{2,1,0:T(8,128)(2,1)S(1)} %fusion.13), channel_id=1, source_target_pairs={{32,0},{48,16},{64,96},{80,112},{96,64},{112,80},{128,160},{144,17... | collective-permute-start | bytes 589832 | tf_op jit(solution)/shard_map/ppermute | solution.py:250
  32.6 0.2 reshape.41.weights_ref
  32.8 1.1 %collective-permute-done.12 = f16[6,8,2048]{2,1,0:T(8,128)(2,1)S(1)} collective-permute-done((f16[6,8,2048]{2,1,0:T(8,128)(2,1)S(1)}, f16[6,8,2048]{2,1,0:T(8,128)(2,1)S(1)}, u32[]{:S(2)}, u32[]{:S(2)}) %collective-permute-start.12) | collective-permute-done | bytes 196640 | tf_op jit(solution)/shard_map/ppermute | solution.py:250
  33.9 3.2 %collective-permute-done.11 = f16[6,8,2048]{2,1,0:T(8,128)(2,1)S(1)} collective-permute-done((f16[6,8,2048]{2,1,0:T(8,128)(2,1)S(1)}, f16[6,8,2048]{2,1,0:T(8,128)(2,1)S(1)}, u32[]{:S(2)}, u32[]{:S(2)}) %collective-permute-start.11) | collective-permute-done | bytes 196640 | tf_op jit(solution)/shard_map/ppermute | solution.py:250
  37.8 20.0 %all_to_all.10.grad_ref = bf16[16,2,6,8,128]{4,3,2,1,0:T(8,128)(2,1)S(1)} all-to-all(bf16[16,2,6,8,128]{4,3,2,1,0:T(8,128)(2,1)S(1)} %fusion.1), channel_id=1, replica_groups=mesh['scan'=16,'cuts'=16] {'cuts'}, dimensions={0} | all-to-all | bytes 786432 | tf_op jit(solution)/shard_map/all_to_all | solution.py:319
  57.8 1.1 %shard_map.39 = f32[1536,128]{1,0:T(8,128)S(1)} custom-call(bf16[16,2,6,8,128]{4,3,2,1,0:T(8,128)(2,1)S(1)} %all_to_all.10.grad_ref, bf16[96,768]{1,0:T(8,128)(2,1)S(1)} %reshape.41.weights_ref, s32[8,128]{1,0:T(8,128)S(1)} %copy-done), custom_call_target="tpu_custom_call" | custom-call | tf_op jit(solution)/shard_map/pallas_call | solution.py:321
  59.0 14.8 %all_to_all.11 = f16[16,96,128]{2,1,0:T(8,128)(2,1)S(1)} all-to-all(f16[16,96,128]{2,1,0:T(8,128)(2,1)S(1)} %bitcast.107), channel_id=1, replica_groups=mesh['scan'=16,'cuts'=16] {'cuts'}, dimensions={0} | all-to-all | bytes 786432 | tf_op jit(solution)/shard_map/all_to_all | solution.py:328
  73.9 0.2 broadcast_select_fusion
  74.1 6.9 %collective-permute-start.14 = (f16[16,2,32,128]{3,2,1,0:T(8,128)(2,1)S(1)}, f16[16,2,32,128]{3,2,1,0:T(8,128)(2,1)S(1)}, u32[]{:S(2)}, u32[]{:S(2)}) collective-permute-start(f16[16,2,32,128]{3,2,1,0:T(8,128)(2,1)S(1)} %get-tuple-element.45), channel_id=1, source_target_pairs={{0,16},{16,0},{32,48},{48,32},{64,80},{80,64},{96,112},{112,96},{1... | collective-permute-start | bytes 786440 | tf_op jit(solution)/shard_map/ppermute | solution.py:250
  81.0 1.9 %collective-permute-start.13 = (f16[16,2,32,128]{3,2,1,0:T(8,128)(2,1)S(1)}, f16[16,2,32,128]{3,2,1,0:T(8,128)(2,1)S(1)}, u32[]{:S(2)}, u32[]{:S(2)}) collective-permute-start(f16[16,2,32,128]{3,2,1,0:T(8,128)(2,1)S(1)} %get-tuple-element.67), channel_id=1, source_target_pairs={{16,32},{48,64},{80,96},{112,128},{144,160},{176,192},{208,224},{3... | collective-permute-start | bytes 786440 | tf_op jit(solution)/shard_map/ppermute | solution.py:334
  83.1 5.7 %shard_map.40 = (f32[12,128,128]{2,1,0:T(8,128)S(1)}, f32[6,5,2,4,8,128]{5,4,3,2,1,0:T(8,128)S(1)}) custom-call(f32[1536,128]{1,0:T(8,128)S(1)} %bitcast.98, f32[1024,128]{1,0:T(8,128)S(1)} %bitcast.99), custom_call_target="tpu_custom_call" | custom-call | bytes 3145728 | tf_op jit(solution)/shard_map/pallas_call | solution.py:348
  88.8 0.3 collective-permute-done.13
  89.1 6.3 %shard_map.41 = f32[12,128,128]{2,1,0:T(8,128)} custom-call(f32[1024,128]{1,0:T(8,128)S(1)} %bitcast.100, f32[6,5,2,4,8,128]{5,4,3,2,1,0:T(8,128)S(1)} %get-tuple-element.49.refs_1_, f32[12,128,128]{2,1,0:T(8,128)S(1)} %get-tuple-element.50.refs_2_), custom_call_target="tpu_custom_call" | custom-call | tf_op jit(solution)/shard_map/pallas_call | solution.py:356
  (44 shorter events, 2.3 us)
Async XLA Ops:
  1.5 6.0 %collective-permute-start = (bf16[4,6,8,2048]{3,2,1,0:T(8,128)(2,1)S(1)}, bf16[4,6,8,2048]{3,2,1,0:T(8,128)(2,1)S(1)}, u32[]{:S(2)}, u32[]{:S(2)}) collective-permute-start(bf16[4,6,8,2048]{3,2,1,0:T(8,128)(2,1)S(1)} %get-tuple-element.30), channel_id=1, source_target_pairs={{0,16},{16,0},{32,48},{48,32},{64,80},{80,64},{96,112},{112,96},{1... | collective-permute-start | bytes 2359304 | tf_op jit(solution)/shard_map/ppermute | solution.py:250
  7.5 4.6 %collective-permute-start.1 = (bf16[12,6,8,2048]{3,2,1,0:T(8,128)(2,1)S(1)}, bf16[12,6,8,2048]{3,2,1,0:T(8,128)(2,1)S(1)}, u32[]{:S(2)}, u32[]{:S(2)}) collective-permute-start(bf16[12,6,8,2048]{3,2,1,0:T(8,128)(2,1)S(1)} %get-tuple-element.31), channel_id=1, source_target_pairs={{16,0},{32,48},{48,32},{64,80},{80,64},{96,112},{112,96},{128,144}... | collective-permute-start | bytes 7077896 | tf_op jit(solution)/shard_map/ppermute | solution.py:250
  7.9 10.6 %collective-permute-start.7 = (f16[2,6,8,2048]{3,2,1,0:T(8,128)(2,1)S(1)}, f16[2,6,8,2048]{3,2,1,0:T(8,128)(2,1)S(1)}, u32[]{:S(2)}, u32[]{:S(2)}) collective-permute-start(f16[2,6,8,2048]{3,2,1,0:T(8,128)(2,1)S(1)} %get-tuple-element.61), channel_id=1, source_target_pairs={{0,32},{16,48},{32,0},{48,16},{64,96},{80,112},{96,64},{112,80},{1... | collective-permute-start | bytes 1179656 | tf_op jit(solution)/shard_map/ppermute | solution.py:250
  8.1 7.3 %collective-permute-start.2 = (f16[6,8,2048]{2,1,0:T(8,128)(2,1)S(1)}, f16[6,8,2048]{2,1,0:T(8,128)(2,1)S(1)}, u32[]{:S(2)}, u32[]{:S(2)}) collective-permute-start(f16[6,8,2048]{2,1,0:T(8,128)(2,1)S(1)} %get-tuple-element.73), channel_id=1, source_target_pairs={{0,64},{16,80},{32,96},{48,112},{64,128},{80,144},{96,160},{112,17... | collective-permute-start | bytes 589832 | tf_op jit(solution)/shard_map/ppermute | solution.py:250
  8.9 6.5 %collective-permute-start.3 = (f16[6,8,2048]{2,1,0:T(8,128)(2,1)S(1)}, f16[6,8,2048]{2,1,0:T(8,128)(2,1)S(1)}, u32[]{:S(2)}, u32[]{:S(2)}) collective-permute-start(f16[6,8,2048]{2,1,0:T(8,128)(2,1)S(1)} %get-tuple-element.72), channel_id=1, source_target_pairs={{0,192},{16,208},{32,224},{48,240},{64,0},{80,16},{96,32},{112,48}... | collective-permute-start | bytes 589832 | tf_op jit(solution)/shard_map/ppermute | solution.py:250
  13.0 15.3 %collective-permute-start.8 = (f16[2,6,8,2048]{3,2,1,0:T(8,128)(2,1)S(1)}, f16[2,6,8,2048]{3,2,1,0:T(8,128)(2,1)S(1)}, u32[]{:S(2)}, u32[]{:S(2)}) collective-permute-start(f16[2,6,8,2048]{3,2,1,0:T(8,128)(2,1)S(1)} %multiply_convert_fusion.2), channel_id=1, source_target_pairs={{16,48},{32,0},{48,16},{64,96},{80,112},{96,64},{112,80},{128,160}... | collective-permute-start | bytes 1179656 | tf_op jit(solution)/shard_map/ppermute | solution.py:250
  15.6 10.6 %collective-permute-start.4 = (f16[2,6,8,2048]{3,2,1,0:T(8,128)(2,1)S(1)}, f16[2,6,8,2048]{3,2,1,0:T(8,128)(2,1)S(1)}, u32[]{:S(2)}, u32[]{:S(2)}) collective-permute-start(f16[2,6,8,2048]{3,2,1,0:T(8,128)(2,1)S(1)} %pad_maximum_fusion), channel_id=1, source_target_pairs={{0,64},{16,80},{32,96},{48,112},{64,128},{80,144},{96,160},{112,17... | collective-permute-start | bytes 1179656 | tf_op jit(solution)/shard_map/ppermute | solution.py:250
  15.9 10.3 %collective-permute-start.5 = (f16[2,6,8,2048]{3,2,1,0:T(8,128)(2,1)S(1)}, f16[2,6,8,2048]{3,2,1,0:T(8,128)(2,1)S(1)}, u32[]{:S(2)}, u32[]{:S(2)}) collective-permute-start(f16[2,6,8,2048]{3,2,1,0:T(8,128)(2,1)S(1)} %pad_maximum_fusion.1), channel_id=1, source_target_pairs={{0,192},{16,208},{32,224},{48,240},{64,0},{80,16},{96,32},{112,48}... | collective-permute-start | bytes 1179656 | tf_op jit(solution)/shard_map/ppermute | solution.py:250
  18.7 9.6 %collective-permute-start.9 = (f16[3,8,2048]{2,1,0:T(8,128)(2,1)S(1)}, f16[3,8,2048]{2,1,0:T(8,128)(2,1)S(1)}, u32[]{:S(2)}, u32[]{:S(2)}) collective-permute-start(f16[3,8,2048]{2,1,0:T(8,128)(2,1)S(1)} %get-tuple-element.71), channel_id=1, source_target_pairs={{16,80},{32,96},{48,112},{64,128},{80,144},{96,160},{112,176},{128... | collective-permute-start | bytes 294920 | tf_op jit(solution)/shard_map/ppermute | solution.py:250
  18.8 9.5 %collective-permute-start.10 = (f16[3,8,2048]{2,1,0:T(8,128)(2,1)S(1)}, f16[3,8,2048]{2,1,0:T(8,128)(2,1)S(1)}, u32[]{:S(2)}, u32[]{:S(2)}) collective-permute-start(f16[3,8,2048]{2,1,0:T(8,128)(2,1)S(1)} %get-tuple-element.70), channel_id=1, source_target_pairs={{16,208},{32,224},{48,240},{64,0},{80,16},{96,32},{112,48},{128,64... | collective-permute-start | bytes 294920 | tf_op jit(solution)/shard_map/ppermute | solution.py:250
  28.5 4.0 %copy-start.1 = (bf16[8,96,96]{2,1,0:T(8,128)(2,1)S(1)}, bf16[8,96,96]{2,1,0:T(8,128)(2,1)}, u32[]{:S(2)}) copy-start(bf16[8,96,96]{2,1,0:T(8,128)(2,1)} %param.4) | copy-start | bytes 442372
  28.6 5.3 %collective-permute-start.12 = (f16[6,8,2048]{2,1,0:T(8,128)(2,1)S(1)}, f16[6,8,2048]{2,1,0:T(8,128)(2,1)S(1)}, u32[]{:S(2)}, u32[]{:S(2)}) collective-permute-start(f16[6,8,2048]{2,1,0:T(8,128)(2,1)S(1)} %pad_maximum_fusion.3), channel_id=1, source_target_pairs={{32,224},{48,240},{64,0},{80,16},{96,32},{112,48},{128,64},{144,80... | collective-permute-start | bytes 589832 | tf_op jit(solution)/shard_map/ppermute | solution.py:250
  31.3 5.8 %collective-permute-start.11 = (f16[6,8,2048]{2,1,0:T(8,128)(2,1)S(1)}, f16[6,8,2048]{2,1,0:T(8,128)(2,1)S(1)}, u32[]{:S(2)}, u32[]{:S(2)}) collective-permute-start(f16[6,8,2048]{2,1,0:T(8,128)(2,1)S(1)} %pad_maximum_fusion.2), channel_id=1, source_target_pairs={{32,96},{48,112},{64,128},{80,144},{96,160},{112,176},{128,192},{1... | collective-permute-start | bytes 589832 | tf_op jit(solution)/shard_map/ppermute | solution.py:250
  31.4 6.0 %collective-permute-start.6 = (f16[6,8,2048]{2,1,0:T(8,128)(2,1)S(1)}, f16[6,8,2048]{2,1,0:T(8,128)(2,1)S(1)}, u32[]{:S(2)}, u32[]{:S(2)}) collective-permute-start(f16[6,8,2048]{2,1,0:T(8,128)(2,1)S(1)} %fusion.13), channel_id=1, source_target_pairs={{32,0},{48,16},{64,96},{80,112},{96,64},{112,80},{128,160},{144,17... | collective-permute-start | bytes 589832 | tf_op jit(solution)/shard_map/ppermute | solution.py:250
  37.6 20.2 %copy-start = (s32[8,128]{1,0:T(8,128)S(1)}, s32[8,128]{1,0:T(8,128)}, u32[]{:S(2)}) copy-start(s32[8,128]{1,0:T(8,128)} %classes_ref.1) | copy-start | bytes 12292
  74.1 8.8 %collective-permute-start.14 = (f16[16,2,32,128]{3,2,1,0:T(8,128)(2,1)S(1)}, f16[16,2,32,128]{3,2,1,0:T(8,128)(2,1)S(1)}, u32[]{:S(2)}, u32[]{:S(2)}) collective-permute-start(f16[16,2,32,128]{3,2,1,0:T(8,128)(2,1)S(1)} %get-tuple-element.45), channel_id=1, source_target_pairs={{0,16},{16,0},{32,48},{48,32},{64,80},{80,64},{96,112},{112,96},{1... | collective-permute-start | bytes 786440 | tf_op jit(solution)/shard_map/ppermute | solution.py:250
  81.0 8.0 %collective-permute-start.13 = (f16[16,2,32,128]{3,2,1,0:T(8,128)(2,1)S(1)}, f16[16,2,32,128]{3,2,1,0:T(8,128)(2,1)S(1)}, u32[]{:S(2)}, u32[]{:S(2)}) collective-permute-start(f16[16,2,32,128]{3,2,1,0:T(8,128)(2,1)S(1)} %get-tuple-element.67), channel_id=1, source_target_pairs={{16,32},{48,64},{80,96},{112,128},{144,160},{176,192},{208,224},{3... | collective-permute-start | bytes 786440 | tf_op jit(solution)/shard_map/ppermute | solution.py:334

commit v7 on v6

--- a/solution.py
+++ b/solution.py
@@ -7,6 +7,7 @@
 
 ITERS = 5
 WAYS = 4
+MANY = 6
 TILE = 16
 SUM_SCALE = 1024.0
 SCALE = 32.0
@@ -84,15 +85,14 @@
                     value[part * self.groups : (part + 1) * self.groups]
                 )
 
-    def sweep(self, low, high, read, write, edges=()):
+    def sweep(self, count, read, write, scale=None):
         before = None
-        here = read(low - 1)
-        for row in range(low - 1, high):
+        here = read(-1)
+        for row in range(-1, count):
             below = read(row + 1)
             down = [b - h for b, h in zip(below, here)]
-            for edge, factor in edges:
-                if row == edge:
-                    down = [d * factor for d in down]
+            if scale is not None:
+                down = [d * scale(row) for d in down]
             near = pltpu.roll(here[0], self.lanes - 1, 1)
             near = jnp.where(self.at_right, pltpu.roll(near, self.lines - 1, 0), near)
             across = [n - h for n, h in zip(here[1:] + [near], here)]
@@ -108,94 +108,98 @@
                     h + 0.2 * (f - b + s1 - s0)
                     for h, f, b, s1, s0 in zip(here, flux, before, sides, [near] + sides[:-1])
                 ]
-                write(row, here, fresh)
+                write(row, fresh)
             before = flux
             here = below
+
+
+def read_row(ref, *at):
+    return [ref[(*at, m)] for m in range(WAYS)]
+
+
+def write_row(ref, values, *at):
+    for m in range(WAYS):
+        ref[(*at, m)] = values[m]
 
 
 def near_kernel(shape, skipped, own_ref, core_ref, out_ref, edge_ref, field):
     tiles = Tiles(shape)
     rows, depth, halo = tiles.rows, tiles.depth, ITERS
+    upper = lax.rem(lax.axis_index("scan"), 2) == 0
     out_ref[...] = jnp.zeros_like(out_ref)
 
-    def on(upper):
-        def one_slice(s, carry):
-            for step in range(1, ITERS + 1):
-                low, high = (step, rows + ITERS - step) if upper else (step - ITERS, rows - step)
-                side, kept = (low - 1, low) if upper else (high, high - 1)
-
-                def read(row):
-                    if step > 1:
-                        return [field[row + halo, m] for m in range(WAYS)]
-                    if 0 <= row < rows:
-                        return tiles.load(own_ref, row * depth + s)
-                    return tiles.load(core_ref, ((row - rows) if upper else (row + rows)) * depth - (0 if upper else skipped) + s)
-
-                def seen(row):
-                    values = read(row)
-                    if row == side:
-                        for m in range(WAYS):
-                            edge_ref[s, step - 1, 0, m] = values[m]
-                    return values
-
-                def write(row, here, fresh):
-                    if row == kept:
-                        for m in range(WAYS):
-                            edge_ref[s, step - 1, 1, m] = here[m]
-                    if step == ITERS:
-                        tiles.store(out_ref, s, row, fresh)
-                    else:
-                        for m in range(WAYS):
-                            field[row + halo, m] = fresh[m]
-
-                tiles.sweep(low, high, seen, write)
-            return carry
-
-        lax.fori_loop(0, depth, one_slice, 0)
-
-    core = lax.rem(lax.axis_index("scan"), 2)
-    pl.when(core == 0)(lambda: on(True))
-    pl.when(core == 1)(lambda: on(False))
+    def one_slice(s, carry):
+        for row in range(rows):
+            write_row(field, tiles.load(own_ref, row * depth + s), row + halo)
+        for row in range(halo):
+            at = jnp.where(upper, row * depth, (row + rows - halo) * depth - skipped)
+            write_row(field, tiles.load(core_ref, at + s), jnp.where(upper, rows + halo, 0) + row)
+        for step in range(1, ITERS + 1):
+            low = jnp.where(upper, step, step - ITERS) + halo
+            count = rows + ITERS - 2 * step
+            side = jnp.where(upper, low - 1, low + count)
+            kept = jnp.where(upper, low, low + count - 1)
+            write_row(edge_ref, read_row(field, side), s, step - 1, 0)
+            write_row(edge_ref, read_row(field, kept), s, step - 1, 1)
+            tiles.sweep(
+                count,
+                lambda row, low=low: read_row(field, low + row),
+                lambda row, fresh, low=low: write_row(field, fresh, low + row),
+            )
+        for row in range(rows - ITERS):
+            at = jnp.where(upper, ITERS, 0) + row
+            tiles.store(out_ref, s, at, read_row(field, at + halo))
+        return carry
+
+    lax.fori_loop(0, depth, one_slice, 0)
 
 
 def far_kernel(shape, skipped, chip_ref, edge_ref, done_ref, out_ref, field):
     tiles = Tiles(shape)
     rows, depth, halo = tiles.rows, tiles.depth, ITERS
+    many = field.shape[0]
+    me = lax.axis_index("scan")
+    upper = lax.rem(me, 2) == 0
+    stop = jnp.where(me == 0, halo - 1, jnp.where(me == lax.axis_size("scan") - 1, halo + rows - 1, -1))
     out_ref[...] = done_ref[...]
-    me = lax.axis_index("scan")
-    first = jnp.where(me == 0, 0.0, 1.0)
-    last = jnp.where(me == lax.axis_size("scan") - 1, 0.0, 1.0)
-
-    def on(upper):
-        def one_slice(s, carry):
-            for step in range(1, ITERS + 1):
-                low, high = (step - ITERS, step) if upper else (rows - step, rows + ITERS - step)
-                side, kept = (high - 1, high) if upper else (low, low - 1)
-
-                def read(row):
-                    if row == side:
-                        return [edge_ref[s, step - 1, 0, m] for m in range(WAYS)]
-                    if row == kept:
-                        return [edge_ref[s, step - 1, 1, m] for m in range(WAYS)]
-                    if step > 1:
-                        return [field[row + halo, m] for m in range(WAYS)]
-                    return tiles.load(chip_ref, ((row + rows) if upper else (row - rows)) * depth - (skipped if upper else 0) + s)
-
-                def write(row, here, fresh):
-                    if step == ITERS:
-                        tiles.store(out_ref, s, row, fresh)
-                    else:
-                        for m in range(WAYS):
-                            field[row + halo, m] = fresh[m]
-
-                tiles.sweep(low, high, read, write, [(-1, first)] if upper else [(rows - 1, last)])
+
+    def some_slices(group, carry):
+        for i in range(many):
+            for row in range(halo):
+                at = jnp.where(upper, (row + rows - halo) * depth - skipped, row * depth)
+                write_row(
+                    field, tiles.load(chip_ref, at + group * many + i), i, jnp.where(upper, 0, rows + halo) + row
+                )
+
+        def one_step(step, carry):
+            low = jnp.where(upper, step - ITERS, rows - step) + halo
+            side = jnp.where(upper, low + ITERS - 1, low)
+            kept = jnp.where(upper, low + ITERS, low - 1)
+            for i in range(many):
+                s = group * many + i
+                write_row(field, read_row(edge_ref, s, step - 1, 0), i, side)
+                write_row(field, read_row(edge_ref, s, step - 1, 1), i, kept)
+            for i in range(many):
+                tiles.sweep(
+                    ITERS,
+                    lambda row, i=i: read_row(field, i, low + row),
+                    lambda row, fresh, i=i: write_row(field, fresh, i, low + row),
+                    lambda row: jnp.where(low + row == stop, 0.0, 1.0),
+                )
             return carry
 
-        lax.fori_loop(0, depth, one_slice, 0)
-
-    core = lax.rem(me, 2)
-    pl.when(core == 0)(lambda: on(True))
-    pl.when(core == 1)(lambda: on(False))
+        lax.fori_loop(1, ITERS + 1, one_step, 0)
+
+        def one_row(row, carry):
+            at = jnp.where(upper, 0, rows - ITERS) + row
+            for i in range(many):
+                tiles.store(out_ref, group * many + i, at, read_row(field, i, at + halo))
+            return carry
+
+        lax.fori_loop(0, ITERS, one_row, 0)
+        return carry
+
+    lax.fori_loop(0, depth // many, some_slices, 0)
 
 
 def copy_kernel(plan, source_ref, *refs):
@@ -356,7 +360,7 @@
     result = pl.pallas_call(
         lambda *refs: far_kernel(shape, skipped, *refs),
         out_shape=out,
-        scratch_shapes=[field],
+        scratch_shapes=[pltpu.VMEM((MANY, rows + 2 * ITERS, WAYS, lines, lanes), f32)],
         compiler_params=pltpu.CompilerParams(vmem_limit_bytes=12 * 1024 * 1024),
     )(plain(chip), edges, done)
     result = result.reshape(parts, depth, cuts, rows, lanes).transpose(0, 1, 3, 2, 4)

time: 96.3 us -> 96.6 us (level)
  Pallas kernels: 17.2 us -> 18.5 us
    pallas_call x1, Pallas kernels: 5.71 us -> 8.92 us  [on_device(): pl.pallas_call(lambda *refs: near_kernel(shape, skipped, *refs), out_shap...]
    pallas_call x1, Pallas kernels: 6.28 us -> 4.3 us  [on_device(): pl.pallas_call(lambda *refs: far_kernel(shape, skipped, *refs), out_shape...]
  transfers between devices with their start and end apart: 15 -> 15, of which waited for: 7 -> 6; matrix products, arithmetic and copies ran while one was open for 3% -> 3% of each run, Pallas kernels for 9% -> 12%
where the time goes in v7:
time: 96.6 us; the launch traced here: 96.4 us
  blocking collectives  34.8 us (36%)
  starting transfers between devices  24.8 us (26%)
  Pallas kernels  18.5 us (19%)
  waiting for transfers between devices  14.3 us (15%)
  other arithmetic  2.64 us (3%)
  local copies, waits for them, and re-layouts  1.03 us (1%)
    ppermute x14, starting transfers between devices, send(): return lax.ppermute(array, 'scan', pairs[turn:] + pairs[:turn])  22.9 us
    all_to_all x1, blocking collectives, on_device(): grad = lax.all_to_all(grad, 'cuts', 0, 0, tiled=True)  20 us
    all_to_all x1, blocking collectives, on_device(): coded = lax.all_to_all(coded, 'cuts', 0, 0, tiled=True)  14.8 us
    ppermute x14, waiting for transfers between devices, send(): return lax.ppermute(array, 'scan', pairs[turn:] + pairs[:turn])  14.3 us
    pallas_call x1, Pallas kernels, on_device(): pl.pallas_call(lambda *refs: near_kernel(shape, skipped, *refs), out_shap...  8.92 us
    pallas_call x1, Pallas kernels, on_device(): pl.pallas_call(lambda *refs: far_kernel(shape, skipped, *refs), out_shape...  4.3 us
    pallas_call x2, Pallas kernels, copied(): pl.pallas_call(lambda *refs: copy_kernel(plan, *refs), out_shape=[jax.Sha...  4.15 us
  transfers between devices with their start and end apart: 15, of which 6 were waited for; matrix products, arithmetic and copies ran while one was open for 3% of the time, Pallas kernels for 12%

profile of v7, /device:TPU:1, one launch (start us, length us, event | category | flops | bytes accessed | tf_op | source)
XLA Modules:
  0.0 96.4 jit_solution(6933037588254388945)
XLA Ops:
  0.0 1.5 %shard_map.38 = (bf16[4,6,8,2048]{3,2,1,0:T(8,128)(2,1)S(1)}, bf16[4,6,8,2048]{3,2,1,0:T(8,128)(2,1)S(1)}) custom-call(bf16[2,6,4,2,2,8,2048]{6,5,4,3,2,1,0:T(8,128)(2,1)} %bitcast.101), custom_call_target="tpu_custom_call" | custom-call | bytes 3145728 | tf_op jit(solution)/shard_map/pallas_call | solution.py:231
  1.5 3.3 %collective-permute-start = (bf16[4,6,8,2048]{3,2,1,0:T(8,128)(2,1)S(1)}, bf16[4,6,8,2048]{3,2,1,0:T(8,128)(2,1)S(1)}, u32[]{:S(2)}, u32[]{:S(2)}) collective-permute-start(bf16[4,6,8,2048]{3,2,1,0:T(8,128)(2,1)S(1)} %get-tuple-element.30), channel_id=1, source_target_pairs={{0,16},{16,0},{32,48},{48,32},{64,80},{80,64},{96,112},{112,96},{1... | collective-permute-start | bytes 2359304 | tf_op jit(solution)/shard_map/ppermute | solution.py:254
  4.9 2.6 %shard_map.37 = (bf16[12,6,8,2048]{3,2,1,0:T(8,128)(2,1)S(1)}, bf16[12,6,8,2048]{3,2,1,0:T(8,128)(2,1)S(1)}) custom-call(bf16[2,6,4,2,2,8,2048]{6,5,4,3,2,1,0:T(8,128)(2,1)} %bitcast.102), custom_call_target="tpu_custom_call" | custom-call | bytes 9437184 | tf_op jit(solution)/shard_map/pallas_call | solution.py:231
  7.5 0.1 collective-permute-start.1
  7.6 0.3 multiply_convert_fusion.3
  8.1 0.8 collective-permute-start.2
  8.9 1.9 %collective-permute-start.3 = (f16[6,8,2048]{2,1,0:T(8,128)(2,1)S(1)}, f16[6,8,2048]{2,1,0:T(8,128)(2,1)S(1)}, u32[]{:S(2)}, u32[]{:S(2)}) collective-permute-start(f16[6,8,2048]{2,1,0:T(8,128)(2,1)S(1)} %get-tuple-element.72), channel_id=1, source_target_pairs={{0,192},{16,208},{32,224},{48,240},{64,0},{80,16},{96,32},{112,48}... | collective-permute-start | bytes 589832 | tf_op jit(solution)/shard_map/ppermute | solution.py:254
  10.9 1.3 %collective-permute-done.1 = bf16[12,6,8,2048]{3,2,1,0:T(8,128)(2,1)S(1)} collective-permute-done((bf16[12,6,8,2048]{3,2,1,0:T(8,128)(2,1)S(1)}, bf16[12,6,8,2048]{3,2,1,0:T(8,128)(2,1)S(1)}, u32[]{:S(2)}, u32[]{:S(2)}) %collective-permute-start.1) | collective-permute-done | bytes 2359328 | tf_op jit(solution)/shard_map/ppermute | solution.py:254
  12.1 0.6 add_multiply_fusion
  12.8 0.1 multiply_convert_fusion.2
  13.0 0.3 collective-permute-start.8
  13.3 2.1 %collective-permute-done.2 = f16[6,8,2048]{2,1,0:T(8,128)(2,1)S(1)} collective-permute-done((f16[6,8,2048]{2,1,0:T(8,128)(2,1)S(1)}, f16[6,8,2048]{2,1,0:T(8,128)(2,1)S(1)}, u32[]{:S(2)}, u32[]{:S(2)}) %collective-permute-start.2) | collective-permute-done | bytes 196640 | tf_op jit(solution)/shard_map/ppermute | solution.py:254
  15.6 0.2 collective-permute-start.4
  15.9 2.6 %collective-permute-start.5 = (f16[2,6,8,2048]{3,2,1,0:T(8,128)(2,1)S(1)}, f16[2,6,8,2048]{3,2,1,0:T(8,128)(2,1)S(1)}, u32[]{:S(2)}, u32[]{:S(2)}) collective-permute-start(f16[2,6,8,2048]{3,2,1,0:T(8,128)(2,1)S(1)} %pad_maximum_fusion.1), channel_id=1, source_target_pairs={{0,192},{16,208},{32,224},{48,240},{64,0},{80,16},{96,32},{112,48}... | collective-permute-start | bytes 1179656 | tf_op jit(solution)/shard_map/ppermute | solution.py:254
  18.8 2.7 %collective-permute-start.10 = (f16[3,8,2048]{2,1,0:T(8,128)(2,1)S(1)}, f16[3,8,2048]{2,1,0:T(8,128)(2,1)S(1)}, u32[]{:S(2)}, u32[]{:S(2)}) collective-permute-start(f16[3,8,2048]{2,1,0:T(8,128)(2,1)S(1)} %get-tuple-element.70), channel_id=1, source_target_pairs={{16,208},{32,224},{48,240},{64,0},{80,16},{96,32},{112,48},{128,64... | collective-permute-start | bytes 294920 | tf_op jit(solution)/shard_map/ppermute | solution.py:254
  21.5 4.7 %collective-permute-done.4 = f16[2,6,8,2048]{3,2,1,0:T(8,128)(2,1)S(1)} collective-permute-done((f16[2,6,8,2048]{3,2,1,0:T(8,128)(2,1)S(1)}, f16[2,6,8,2048]{3,2,1,0:T(8,128)(2,1)S(1)}, u32[]{:S(2)}, u32[]{:S(2)}) %collective-permute-start.4) | collective-permute-done | bytes 393248 | tf_op jit(solution)/shard_map/ppermute | solution.py:254
  26.2 0.2 convert_add_fusion
  26.5 1.8 %collective-permute-done.9 = f16[3,8,2048]{2,1,0:T(8,128)(2,1)S(1)} collective-permute-done((f16[3,8,2048]{2,1,0:T(8,128)(2,1)S(1)}, f16[3,8,2048]{2,1,0:T(8,128)(2,1)S(1)}, u32[]{:S(2)}, u32[]{:S(2)}) %collective-permute-start.9) | collective-permute-done | bytes 98336 | tf_op jit(solution)/shard_map/ppermute | solution.py:254
  28.3 0.1 fusion.19
  28.6 2.6 %collective-permute-start.12 = (f16[6,8,2048]{2,1,0:T(8,128)(2,1)S(1)}, f16[6,8,2048]{2,1,0:T(8,128)(2,1)S(1)}, u32[]{:S(2)}, u32[]{:S(2)}) collective-permute-start(f16[6,8,2048]{2,1,0:T(8,128)(2,1)S(1)} %pad_maximum_fusion.3), channel_id=1, source_target_pairs={{32,224},{48,240},{64,0},{80,16},{96,32},{112,48},{128,64},{144,80... | collective-permute-start | bytes 589832 | tf_op jit(solution)/shard_map/ppermute | solution.py:254
  31.4 1.1 %collective-permute-start.6 = (f16[6,8,2048]{2,1,0:T(8,128)(2,1)S(1)}, f16[6,8,2048]{2,1,0:T(8,128)(2,1)S(1)}, u32[]{:S(2)}, u32[]{:S(2)}) collective-permute-start(f16[6,8,2048]{2,1,0:T(8,128)(2,1)S(1)} %fusion.13), channel_id=1, source_target_pairs={{32,0},{48,16},{64,96},{80,112},{96,64},{112,80},{128,160},{144,17... | collective-permute-start | bytes 589832 | tf_op jit(solution)/shard_map/ppermute | solution.py:254
  32.6 0.2 reshape.41.weights_ref
  32.8 1.1 %collective-permute-done.12 = f16[6,8,2048]{2,1,0:T(8,128)(2,1)S(1)} collective-permute-done((f16[6,8,2048]{2,1,0:T(8,128)(2,1)S(1)}, f16[6,8,2048]{2,1,0:T(8,128)(2,1)S(1)}, u32[]{:S(2)}, u32[]{:S(2)}) %collective-permute-start.12) | collective-permute-done | bytes 196640 | tf_op jit(solution)/shard_map/ppermute | solution.py:254
  33.9 3.2 %collective-permute-done.11 = f16[6,8,2048]{2,1,0:T(8,128)(2,1)S(1)} collective-permute-done((f16[6,8,2048]{2,1,0:T(8,128)(2,1)S(1)}, f16[6,8,2048]{2,1,0:T(8,128)(2,1)S(1)}, u32[]{:S(2)}, u32[]{:S(2)}) %collective-permute-start.11) | collective-permute-done | bytes 196640 | tf_op jit(solution)/shard_map/ppermute | solution.py:254
  37.8 20.0 %all_to_all.10.grad_ref = bf16[16,2,6,8,128]{4,3,2,1,0:T(8,128)(2,1)S(1)} all-to-all(bf16[16,2,6,8,128]{4,3,2,1,0:T(8,128)(2,1)S(1)} %fusion.1), channel_id=1, replica_groups=mesh['scan'=16,'cuts'=16] {'cuts'}, dimensions={0} | all-to-all | bytes 786432 | tf_op jit(solution)/shard_map/all_to_all | solution.py:323
  57.8 1.1 %shard_map.39 = f32[1536,128]{1,0:T(8,128)S(1)} custom-call(bf16[16,2,6,8,128]{4,3,2,1,0:T(8,128)(2,1)S(1)} %all_to_all.10.grad_ref, bf16[96,768]{1,0:T(8,128)(2,1)S(1)} %reshape.41.weights_ref, s32[8,128]{1,0:T(8,128)S(1)} %copy-done), custom_call_target="tpu_custom_call" | custom-call | tf_op jit(solution)/shard_map/pallas_call | solution.py:325
  59.0 14.8 %all_to_all.11 = f16[16,96,128]{2,1,0:T(8,128)(2,1)S(1)} all-to-all(f16[16,96,128]{2,1,0:T(8,128)(2,1)S(1)} %bitcast.107), channel_id=1, replica_groups=mesh['scan'=16,'cuts'=16] {'cuts'}, dimensions={0} | all-to-all | bytes 786432 | tf_op jit(solution)/shard_map/all_to_all | solution.py:332
  73.9 0.2 broadcast_select_fusion
  74.1 6.9 %collective-permute-start.14 = (f16[16,2,32,128]{3,2,1,0:T(8,128)(2,1)S(1)}, f16[16,2,32,128]{3,2,1,0:T(8,128)(2,1)S(1)}, u32[]{:S(2)}, u32[]{:S(2)}) collective-permute-start(f16[16,2,32,128]{3,2,1,0:T(8,128)(2,1)S(1)} %get-tuple-element.45), channel_id=1, source_target_pairs={{0,16},{16,0},{32,48},{48,32},{64,80},{80,64},{96,112},{112,96},{1... | collective-permute-start | bytes 786440 | tf_op jit(solution)/shard_map/ppermute | solution.py:254
  81.0 1.9 %collective-permute-start.13 = (f16[16,2,32,128]{3,2,1,0:T(8,128)(2,1)S(1)}, f16[16,2,32,128]{3,2,1,0:T(8,128)(2,1)S(1)}, u32[]{:S(2)}, u32[]{:S(2)}) collective-permute-start(f16[16,2,32,128]{3,2,1,0:T(8,128)(2,1)S(1)} %get-tuple-element.67), channel_id=1, source_target_pairs={{16,32},{48,64},{80,96},{112,128},{144,160},{176,192},{208,224},{3... | collective-permute-start | bytes 786440 | tf_op jit(solution)/shard_map/ppermute | solution.py:338
  83.1 8.9 %shard_map.40 = (f32[12,128,128]{2,1,0:T(8,128)S(1)}, f32[6,5,2,4,8,128]{5,4,3,2,1,0:T(8,128)S(1)}) custom-call(f32[1536,128]{1,0:T(8,128)S(1)} %bitcast.98, f32[1024,128]{1,0:T(8,128)S(1)} %bitcast.99), custom_call_target="tpu_custom_call" | custom-call | bytes 3145728 | tf_op jit(solution)/shard_map/pallas_call | solution.py:352
  92.1 4.3 %shard_map.41 = f32[12,128,128]{2,1,0:T(8,128)} custom-call(f32[1024,128]{1,0:T(8,128)S(1)} %bitcast.100, f32[6,5,2,4,8,128]{5,4,3,2,1,0:T(8,128)S(1)} %get-tuple-element.49.refs_1_, f32[12,128,128]{2,1,0:T(8,128)S(1)} %get-tuple-element.50.refs_2_), custom_call_target="tpu_custom_call" | custom-call | tf_op jit(solution)/shard_map/pallas_call | solution.py:360
  (44 shorter events, 2.2 us)
Async XLA Ops:
  1.5 6.0 %collective-permute-start = (bf16[4,6,8,2048]{3,2,1,0:T(8,128)(2,1)S(1)}, bf16[4,6,8,2048]{3,2,1,0:T(8,128)(2,1)S(1)}, u32[]{:S(2)}, u32[]{:S(2)}) collective-permute-start(bf16[4,6,8,2048]{3,2,1,0:T(8,128)(2,1)S(1)} %get-tuple-element.30), channel_id=1, source_target_pairs={{0,16},{16,0},{32,48},{48,32},{64,80},{80,64},{96,112},{112,96},{1... | collective-permute-start | bytes 2359304 | tf_op jit(solution)/shard_map/ppermute | solution.py:254
  7.5 4.6 %collective-permute-start.1 = (bf16[12,6,8,2048]{3,2,1,0:T(8,128)(2,1)S(1)}, bf16[12,6,8,2048]{3,2,1,0:T(8,128)(2,1)S(1)}, u32[]{:S(2)}, u32[]{:S(2)}) collective-permute-start(bf16[12,6,8,2048]{3,2,1,0:T(8,128)(2,1)S(1)} %get-tuple-element.31), channel_id=1, source_target_pairs={{16,0},{32,48},{48,32},{64,80},{80,64},{96,112},{112,96},{128,144}... | collective-permute-start | bytes 7077896 | tf_op jit(solution)/shard_map/ppermute | solution.py:254
  7.9 10.6 %collective-permute-start.7 = (f16[2,6,8,2048]{3,2,1,0:T(8,128)(2,1)S(1)}, f16[2,6,8,2048]{3,2,1,0:T(8,128)(2,1)S(1)}, u32[]{:S(2)}, u32[]{:S(2)}) collective-permute-start(f16[2,6,8,2048]{3,2,1,0:T(8,128)(2,1)S(1)} %get-tuple-element.61), channel_id=1, source_target_pairs={{0,32},{16,48},{32,0},{48,16},{64,96},{80,112},{96,64},{112,80},{1... | collective-permute-start | bytes 1179656 | tf_op jit(solution)/shard_map/ppermute | solution.py:254
  8.1 7.3 %collective-permute-start.2 = (f16[6,8,2048]{2,1,0:T(8,128)(2,1)S(1)}, f16[6,8,2048]{2,1,0:T(8,128)(2,1)S(1)}, u32[]{:S(2)}, u32[]{:S(2)}) collective-permute-start(f16[6,8,2048]{2,1,0:T(8,128)(2,1)S(1)} %get-tuple-element.73), channel_id=1, source_target_pairs={{0,64},{16,80},{32,96},{48,112},{64,128},{80,144},{96,160},{112,17... | collective-permute-start | bytes 589832 | tf_op jit(solution)/shard_map/ppermute | solution.py:254
  8.9 6.5 %collective-permute-start.3 = (f16[6,8,2048]{2,1,0:T(8,128)(2,1)S(1)}, f16[6,8,2048]{2,1,0:T(8,128)(2,1)S(1)}, u32[]{:S(2)}, u32[]{:S(2)}) collective-permute-start(f16[6,8,2048]{2,1,0:T(8,128)(2,1)S(1)} %get-tuple-element.72), channel_id=1, source_target_pairs={{0,192},{16,208},{32,224},{48,240},{64,0},{80,16},{96,32},{112,48}... | collective-permute-start | bytes 589832 | tf_op jit(solution)/shard_map/ppermute | solution.py:254
  13.0 15.3 %collective-permute-start.8 = (f16[2,6,8,2048]{3,2,1,0:T(8,128)(2,1)S(1)}, f16[2,6,8,2048]{3,2,1,0:T(8,128)(2,1)S(1)}, u32[]{:S(2)}, u32[]{:S(2)}) collective-permute-start(f16[2,6,8,2048]{3,2,1,0:T(8,128)(2,1)S(1)} %multiply_convert_fusion.2), channel_id=1, source_target_pairs={{16,48},{32,0},{48,16},{64,96},{80,112},{96,64},{112,80},{128,160}... | collective-permute-start | bytes 1179656 | tf_op jit(solution)/shard_map/ppermute | solution.py:254
  15.6 10.6 %collective-permute-start.4 = (f16[2,6,8,2048]{3,2,1,0:T(8,128)(2,1)S(1)}, f16[2,6,8,2048]{3,2,1,0:T(8,128)(2,1)S(1)}, u32[]{:S(2)}, u32[]{:S(2)}) collective-permute-start(f16[2,6,8,2048]{3,2,1,0:T(8,128)(2,1)S(1)} %pad_maximum_fusion), channel_id=1, source_target_pairs={{0,64},{16,80},{32,96},{48,112},{64,128},{80,144},{96,160},{112,17... | collective-permute-start | bytes 1179656 | tf_op jit(solution)/shard_map/ppermute | solution.py:254
  15.9 10.3 %collective-permute-start.5 = (f16[2,6,8,2048]{3,2,1,0:T(8,128)(2,1)S(1)}, f16[2,6,8,2048]{3,2,1,0:T(8,128)(2,1)S(1)}, u32[]{:S(2)}, u32[]{:S(2)}) collective-permute-start(f16[2,6,8,2048]{3,2,1,0:T(8,128)(2,1)S(1)} %pad_maximum_fusion.1), channel_id=1, source_target_pairs={{0,192},{16,208},{32,224},{48,240},{64,0},{80,16},{96,32},{112,48}... | collective-permute-start | bytes 1179656 | tf_op jit(solution)/shard_map/ppermute | solution.py:254
  18.7 9.6 %collective-permute-start.9 = (f16[3,8,2048]{2,1,0:T(8,128)(2,1)S(1)}, f16[3,8,2048]{2,1,0:T(8,128)(2,1)S(1)}, u32[]{:S(2)}, u32[]{:S(2)}) collective-permute-start(f16[3,8,2048]{2,1,0:T(8,128)(2,1)S(1)} %get-tuple-element.71), channel_id=1, source_target_pairs={{16,80},{32,96},{48,112},{64,128},{80,144},{96,160},{112,176},{128... | collective-permute-start | bytes 294920 | tf_op jit(solution)/shard_map/ppermute | solution.py:254
  18.8 9.5 %collective-permute-start.10 = (f16[3,8,2048]{2,1,0:T(8,128)(2,1)S(1)}, f16[3,8,2048]{2,1,0:T(8,128)(2,1)S(1)}, u32[]{:S(2)}, u32[]{:S(2)}) collective-permute-start(f16[3,8,2048]{2,1,0:T(8,128)(2,1)S(1)} %get-tuple-element.70), channel_id=1, source_target_pairs={{16,208},{32,224},{48,240},{64,0},{80,16},{96,32},{112,48},{128,64... | collective-permute-start | bytes 294920 | tf_op jit(solution)/shard_map/ppermute | solution.py:254
  28.5 4.0 %copy-start.1 = (bf16[8,96,96]{2,1,0:T(8,128)(2,1)S(1)}, bf16[8,96,96]{2,1,0:T(8,128)(2,1)}, u32[]{:S(2)}) copy-start(bf16[8,96,96]{2,1,0:T(8,128)(2,1)} %param.4) | copy-start | bytes 442372
  28.6 5.3 %collective-permute-start.12 = (f16[6,8,2048]{2,1,0:T(8,128)(2,1)S(1)}, f16[6,8,2048]{2,1,0:T(8,128)(2,1)S(1)}, u32[]{:S(2)}, u32[]{:S(2)}) collective-permute-start(f16[6,8,2048]{2,1,0:T(8,128)(2,1)S(1)} %pad_maximum_fusion.3), channel_id=1, source_target_pairs={{32,224},{48,240},{64,0},{80,16},{96,32},{112,48},{128,64},{144,80... | collective-permute-start | bytes 589832 | tf_op jit(solution)/shard_map/ppermute | solution.py:254
  31.3 5.8 %collective-permute-start.11 = (f16[6,8,2048]{2,1,0:T(8,128)(2,1)S(1)}, f16[6,8,2048]{2,1,0:T(8,128)(2,1)S(1)}, u32[]{:S(2)}, u32[]{:S(2)}) collective-permute-start(f16[6,8,2048]{2,1,0:T(8,128)(2,1)S(1)} %pad_maximum_fusion.2), channel_id=1, source_target_pairs={{32,96},{48,112},{64,128},{80,144},{96,160},{112,176},{128,192},{1... | collective-permute-start | bytes 589832 | tf_op jit(solution)/shard_map/ppermute | solution.py:254
  31.4 6.0 %collective-permute-start.6 = (f16[6,8,2048]{2,1,0:T(8,128)(2,1)S(1)}, f16[6,8,2048]{2,1,0:T(8,128)(2,1)S(1)}, u32[]{:S(2)}, u32[]{:S(2)}) collective-permute-start(f16[6,8,2048]{2,1,0:T(8,128)(2,1)S(1)} %fusion.13), channel_id=1, source_target_pairs={{32,0},{48,16},{64,96},{80,112},{96,64},{112,80},{128,160},{144,17... | collective-permute-start | bytes 589832 | tf_op jit(solution)/shard_map/ppermute | solution.py:254
  37.6 20.2 %copy-start = (s32[8,128]{1,0:T(8,128)S(1)}, s32[8,128]{1,0:T(8,128)}, u32[]{:S(2)}) copy-start(s32[8,128]{1,0:T(8,128)} %classes_ref.1) | copy-start | bytes 12292
  74.1 8.8 %collective-permute-start.14 = (f16[16,2,32,128]{3,2,1,0:T(8,128)(2,1)S(1)}, f16[16,2,32,128]{3,2,1,0:T(8,128)(2,1)S(1)}, u32[]{:S(2)}, u32[]{:S(2)}) collective-permute-start(f16[16,2,32,128]{3,2,1,0:T(8,128)(2,1)S(1)} %get-tuple-element.45), channel_id=1, source_target_pairs={{0,16},{16,0},{32,48},{48,32},{64,80},{80,64},{96,112},{112,96},{1... | collective-permute-start | bytes 786440 | tf_op jit(solution)/shard_map/ppermute | solution.py:254
  81.0 11.0 %collective-permute-start.13 = (f16[16,2,32,128]{3,2,1,0:T(8,128)(2,1)S(1)}, f16[16,2,32,128]{3,2,1,0:T(8,128)(2,1)S(1)}, u32[]{:S(2)}, u32[]{:S(2)}) collective-permute-start(f16[16,2,32,128]{3,2,1,0:T(8,128)(2,1)S(1)} %get-tuple-element.67), channel_id=1, source_target_pairs={{16,32},{48,64},{80,96},{112,128},{144,160},{176,192},{208,224},{3... | collective-permute-start | bytes 786440 | tf_op jit(solution)/shard_map/ppermute | solution.py:338

commit v8 on v7

--- a/solution.py
+++ b/solution.py
@@ -85,10 +85,10 @@
                     value[part * self.groups : (part + 1) * self.groups]
                 )
 
-    def sweep(self, count, read, write, scale=None):
+    def sweep(self, low, high, read, write, scale=None):
         before = None
-        here = read(-1)
-        for row in range(-1, count):
+        here = read(low - 1)
+        for row in range(low - 1, high):
             below = read(row + 1)
             down = [b - h for b, h in zip(below, here)]
             if scale is not None:
@@ -108,7 +108,7 @@
                     h + 0.2 * (f - b + s1 - s0)
                     for h, f, b, s1, s0 in zip(here, flux, before, sides, [near] + sides[:-1])
                 ]
-                write(row, fresh)
+                write(row, here, fresh)
             before = flux
             here = below
 
@@ -125,33 +125,46 @@
 def near_kernel(shape, skipped, own_ref, core_ref, out_ref, edge_ref, field):
     tiles = Tiles(shape)
     rows, depth, halo = tiles.rows, tiles.depth, ITERS
-    upper = lax.rem(lax.axis_index("scan"), 2) == 0
     out_ref[...] = jnp.zeros_like(out_ref)
 
-    def one_slice(s, carry):
-        for row in range(rows):
-            write_row(field, tiles.load(own_ref, row * depth + s), row + halo)
-        for row in range(halo):
-            at = jnp.where(upper, row * depth, (row + rows - halo) * depth - skipped)
-            write_row(field, tiles.load(core_ref, at + s), jnp.where(upper, rows + halo, 0) + row)
-        for step in range(1, ITERS + 1):
-            low = jnp.where(upper, step, step - ITERS) + halo
-            count = rows + ITERS - 2 * step
-            side = jnp.where(upper, low - 1, low + count)
-            kept = jnp.where(upper, low, low + count - 1)
-            write_row(edge_ref, read_row(field, side), s, step - 1, 0)
-            write_row(edge_ref, read_row(field, kept), s, step - 1, 1)
-            tiles.sweep(
-                count,
-                lambda row, low=low: read_row(field, low + row),
-                lambda row, fresh, low=low: write_row(field, fresh, low + row),
-            )
-        for row in range(rows - ITERS):
-            at = jnp.where(upper, ITERS, 0) + row
-            tiles.store(out_ref, s, at, read_row(field, at + halo))
-        return carry
-
-    lax.fori_loop(0, depth, one_slice, 0)
+    def on(upper):
+        def one_slice(s, carry):
+            for step in range(1, ITERS + 1):
+                low, high = (step, rows + ITERS - step) if upper else (step - ITERS, rows - step)
+                side, kept = (low - 1, low) if upper else (high, high - 1)
+
+                def read(row):
+                    if step > 1:
+                        return [field[row + halo, m] for m in range(WAYS)]
+                    if 0 <= row < rows:
+                        return tiles.load(own_ref, row * depth + s)
+                    return tiles.load(core_ref, ((row - rows) if upper else (row + rows)) * depth - (0 if upper else skipped) + s)
+
+                def seen(row):
+                    values = read(row)
+                    if row == side:
+                        for m in range(WAYS):
+                            edge_ref[s, step - 1, 0, m] = values[m]
+                    return values
+
+                def write(row, here, fresh):
+                    if row == kept:
+                        for m in range(WAYS):
+                            edge_ref[s, step - 1, 1, m] = here[m]
+                    if step == ITERS:
+                        tiles.store(out_ref, s, row, fresh)
+                    else:
+                        for m in range(WAYS):
+                            field[row + halo, m] = fresh[m]
+
+                tiles.sweep(low, high, seen, write)
+            return carry
+
+        lax.fori_loop(0, depth, one_slice, 0)
+
+    core = lax.rem(lax.axis_index("scan"), 2)
+    pl.when(core == 0)(lambda: on(True))
+    pl.when(core == 1)(lambda: on(False))
 
 
 def far_kernel(shape, skipped, chip_ref, edge_ref, done_ref, out_ref, field):
@@ -181,9 +194,10 @@
                 write_row(field, read_row(edge_ref, s, step - 1, 1), i, kept)
             for i in range(many):
                 tiles.sweep(
+                    0,
                     ITERS,
                     lambda row, i=i: read_row(field, i, low + row),
-                    lambda row, fresh, i=i: write_row(field, fresh, i, low + row),
+                    lambda row, here, fresh, i=i: write_row(field, fresh, i, low + row),
                     lambda row: jnp.where(low + row == stop, 0.0, 1.0),
                 )
             return carry

time: 96.6 us -> 94.3 us (0.976)
  Pallas kernels: 18.5 us -> 15.3 us
    pallas_call x1, Pallas kernels: 8.92 us -> 5.71 us  [on_device(): pl.pallas_call(lambda *refs: near_kernel(shape, skipped, *refs), out_shap...]
  transfers between devices with their start and end apart: 15 -> 15, of which waited for: 6 -> 7; matrix products, arithmetic and copies ran while one was open for 3% -> 3% of each run, Pallas kernels for 12% -> 9%
where the time goes in v8:
time: 94.3 us; the launch traced here: 93.4 us
  blocking collectives  34.8 us (37%)
  starting transfers between devices  24.8 us (26%)
  Pallas kernels  15.3 us (16%)
  waiting for transfers between devices  14.6 us (15%)
  other arithmetic  2.63 us (3%)
  local copies, waits for them, and re-layouts  1.03 us (1%)
    ppermute x14, starting transfers between devices, send(): return lax.ppermute(array, 'scan', pairs[turn:] + pairs[:turn])  22.9 us
    all_to_all x1, blocking collectives, on_device(): grad = lax.all_to_all(grad, 'cuts', 0, 0, tiled=True)  20 us
    all_to_all x1, blocking collectives, on_device(): coded = lax.all_to_all(coded, 'cuts', 0, 0, tiled=True)  14.8 us
    ppermute x14, waiting for transfers between devices, send(): return lax.ppermute(array, 'scan', pairs[turn:] + pairs[:turn])  14.3 us
    pallas_call x1, Pallas kernels, on_device(): pl.pallas_call(lambda *refs: near_kernel(shape, skipped, *refs), out_shap...  5.71 us
    pallas_call x1, Pallas kernels, on_device(): pl.pallas_call(lambda *refs: far_kernel(shape, skipped, *refs), out_shape...  4.3 us
    pallas_call x2, Pallas kernels, copied(): pl.pallas_call(lambda *refs: copy_kernel(plan, *refs), out_shape=[jax.Sha...  4.15 us
    ppermute x1, starting transfers between devices, on_device(): lax.ppermute(jnp.where(upper, top, bottom), 'scan', [(i, i + 1) for i in...  1.91 us
  transfers between devices with their start and end apart: 15, of which 7 were waited for; matrix products, arithmetic and copies ran while one was open for 3% of the time, Pallas kernels for 9%

profile of v8, /device:TPU:1, one launch (start us, length us, event | category | flops | bytes accessed | tf_op | source)
XLA Modules:
  0.0 93.4 jit_solution(534058436083856235)
XLA Ops:
  0.0 1.5 %shard_map.38 = (bf16[4,6,8,2048]{3,2,1,0:T(8,128)(2,1)S(1)}, bf16[4,6,8,2048]{3,2,1,0:T(8,128)(2,1)S(1)}) custom-call(bf16[2,6,4,2,2,8,2048]{6,5,4,3,2,1,0:T(8,128)(2,1)} %bitcast.101), custom_call_target="tpu_custom_call" | custom-call | bytes 3145728 | tf_op jit(solution)/shard_map/pallas_call | solution.py:245
  1.5 3.3 %collective-permute-start = (bf16[4,6,8,2048]{3,2,1,0:T(8,128)(2,1)S(1)}, bf16[4,6,8,2048]{3,2,1,0:T(8,128)(2,1)S(1)}, u32[]{:S(2)}, u32[]{:S(2)}) collective-permute-start(bf16[4,6,8,2048]{3,2,1,0:T(8,128)(2,1)S(1)} %get-tuple-element.30), channel_id=1, source_target_pairs={{0,16},{16,0},{32,48},{48,32},{64,80},{80,64},{96,112},{112,96},{1... | collective-permute-start | bytes 2359304 | tf_op jit(solution)/shard_map/ppermute | solution.py:268
  4.9 2.6 %shard_map.37 = (bf16[12,6,8,2048]{3,2,1,0:T(8,128)(2,1)S(1)}, bf16[12,6,8,2048]{3,2,1,0:T(8,128)(2,1)S(1)}) custom-call(bf16[2,6,4,2,2,8,2048]{6,5,4,3,2,1,0:T(8,128)(2,1)} %bitcast.102), custom_call_target="tpu_custom_call" | custom-call | bytes 9437184 | tf_op jit(solution)/shard_map/pallas_call | solution.py:245
  7.6 0.3 multiply_convert_fusion.3
  8.1 0.8 collective-permute-start.2
  8.9 1.9 %collective-permute-start.3 = (f16[6,8,2048]{2,1,0:T(8,128)(2,1)S(1)}, f16[6,8,2048]{2,1,0:T(8,128)(2,1)S(1)}, u32[]{:S(2)}, u32[]{:S(2)}) collective-permute-start(f16[6,8,2048]{2,1,0:T(8,128)(2,1)S(1)} %get-tuple-element.72), channel_id=1, source_target_pairs={{0,192},{16,208},{32,224},{48,240},{64,0},{80,16},{96,32},{112,48}... | collective-permute-start | bytes 589832 | tf_op jit(solution)/shard_map/ppermute | solution.py:268
  10.9 1.3 %collective-permute-done.1 = bf16[12,6,8,2048]{3,2,1,0:T(8,128)(2,1)S(1)} collective-permute-done((bf16[12,6,8,2048]{3,2,1,0:T(8,128)(2,1)S(1)}, bf16[12,6,8,2048]{3,2,1,0:T(8,128)(2,1)S(1)}, u32[]{:S(2)}, u32[]{:S(2)}) %collective-permute-start.1) | collective-permute-done | bytes 2359328 | tf_op jit(solution)/shard_map/ppermute | solution.py:268
  12.1 0.6 add_multiply_fusion
  12.8 0.1 multiply_convert_fusion.2
  13.0 0.3 collective-permute-start.8
  13.3 2.1 %collective-permute-done.2 = f16[6,8,2048]{2,1,0:T(8,128)(2,1)S(1)} collective-permute-done((f16[6,8,2048]{2,1,0:T(8,128)(2,1)S(1)}, f16[6,8,2048]{2,1,0:T(8,128)(2,1)S(1)}, u32[]{:S(2)}, u32[]{:S(2)}) %collective-permute-start.2) | collective-permute-done | bytes 196640 | tf_op jit(solution)/shard_map/ppermute | solution.py:268
  15.6 0.2 collective-permute-start.4
  15.9 2.6 %collective-permute-start.5 = (f16[2,6,8,2048]{3,2,1,0:T(8,128)(2,1)S(1)}, f16[2,6,8,2048]{3,2,1,0:T(8,128)(2,1)S(1)}, u32[]{:S(2)}, u32[]{:S(2)}) collective-permute-start(f16[2,6,8,2048]{3,2,1,0:T(8,128)(2,1)S(1)} %pad_maximum_fusion.1), channel_id=1, source_target_pairs={{0,192},{16,208},{32,224},{48,240},{64,0},{80,16},{96,32},{112,48}... | collective-permute-start | bytes 1179656 | tf_op jit(solution)/shard_map/ppermute | solution.py:268
  18.8 2.7 %collective-permute-start.10 = (f16[3,8,2048]{2,1,0:T(8,128)(2,1)S(1)}, f16[3,8,2048]{2,1,0:T(8,128)(2,1)S(1)}, u32[]{:S(2)}, u32[]{:S(2)}) collective-permute-start(f16[3,8,2048]{2,1,0:T(8,128)(2,1)S(1)} %get-tuple-element.70), channel_id=1, source_target_pairs={{16,208},{32,224},{48,240},{64,0},{80,16},{96,32},{112,48},{128,64... | collective-permute-start | bytes 294920 | tf_op jit(solution)/shard_map/ppermute | solution.py:268
  21.5 4.7 %collective-permute-done.4 = f16[2,6,8,2048]{3,2,1,0:T(8,128)(2,1)S(1)} collective-permute-done((f16[2,6,8,2048]{3,2,1,0:T(8,128)(2,1)S(1)}, f16[2,6,8,2048]{3,2,1,0:T(8,128)(2,1)S(1)}, u32[]{:S(2)}, u32[]{:S(2)}) %collective-permute-start.4) | collective-permute-done | bytes 393248 | tf_op jit(solution)/shard_map/ppermute | solution.py:268
  26.2 0.2 convert_add_fusion
  26.5 1.8 %collective-permute-done.9 = f16[3,8,2048]{2,1,0:T(8,128)(2,1)S(1)} collective-permute-done((f16[3,8,2048]{2,1,0:T(8,128)(2,1)S(1)}, f16[3,8,2048]{2,1,0:T(8,128)(2,1)S(1)}, u32[]{:S(2)}, u32[]{:S(2)}) %collective-permute-start.9) | collective-permute-done | bytes 98336 | tf_op jit(solution)/shard_map/ppermute | solution.py:268
  28.3 0.1 fusion.19
  28.6 2.6 %collective-permute-start.12 = (f16[6,8,2048]{2,1,0:T(8,128)(2,1)S(1)}, f16[6,8,2048]{2,1,0:T(8,128)(2,1)S(1)}, u32[]{:S(2)}, u32[]{:S(2)}) collective-permute-start(f16[6,8,2048]{2,1,0:T(8,128)(2,1)S(1)} %pad_maximum_fusion.3), channel_id=1, source_target_pairs={{32,224},{48,240},{64,0},{80,16},{96,32},{112,48},{128,64},{144,80... | collective-permute-start | bytes 589832 | tf_op jit(solution)/shard_map/ppermute | solution.py:268
  31.4 1.1 %collective-permute-start.6 = (f16[6,8,2048]{2,1,0:T(8,128)(2,1)S(1)}, f16[6,8,2048]{2,1,0:T(8,128)(2,1)S(1)}, u32[]{:S(2)}, u32[]{:S(2)}) collective-permute-start(f16[6,8,2048]{2,1,0:T(8,128)(2,1)S(1)} %fusion.13), channel_id=1, source_target_pairs={{32,0},{48,16},{64,96},{80,112},{96,64},{112,80},{128,160},{144,17... | collective-permute-start | bytes 589832 | tf_op jit(solution)/shard_map/ppermute | solution.py:268
  32.6 0.2 reshape.41.weights_ref
  32.8 1.1 %collective-permute-done.12 = f16[6,8,2048]{2,1,0:T(8,128)(2,1)S(1)} collective-permute-done((f16[6,8,2048]{2,1,0:T(8,128)(2,1)S(1)}, f16[6,8,2048]{2,1,0:T(8,128)(2,1)S(1)}, u32[]{:S(2)}, u32[]{:S(2)}) %collective-permute-start.12) | collective-permute-done | bytes 196640 | tf_op jit(solution)/shard_map/ppermute | solution.py:268
  33.9 3.2 %collective-permute-done.11 = f16[6,8,2048]{2,1,0:T(8,128)(2,1)S(1)} collective-permute-done((f16[6,8,2048]{2,1,0:T(8,128)(2,1)S(1)}, f16[6,8,2048]{2,1,0:T(8,128)(2,1)S(1)}, u32[]{:S(2)}, u32[]{:S(2)}) %collective-permute-start.11) | collective-permute-done | bytes 196640 | tf_op jit(solution)/shard_map/ppermute | solution.py:268
  37.8 20.0 %all_to_all.10.grad_ref = bf16[16,2,6,8,128]{4,3,2,1,0:T(8,128)(2,1)S(1)} all-to-all(bf16[16,2,6,8,128]{4,3,2,1,0:T(8,128)(2,1)S(1)} %fusion.1), channel_id=1, replica_groups=mesh['scan'=16,'cuts'=16] {'cuts'}, dimensions={0} | all-to-all | bytes 786432 | tf_op jit(solution)/shard_map/all_to_all | solution.py:337
  57.8 1.1 %shard_map.39 = f32[1536,128]{1,0:T(8,128)S(1)} custom-call(bf16[16,2,6,8,128]{4,3,2,1,0:T(8,128)(2,1)S(1)} %all_to_all.10.grad_ref, bf16[96,768]{1,0:T(8,128)(2,1)S(1)} %reshape.41.weights_ref, s32[8,128]{1,0:T(8,128)S(1)} %copy-done), custom_call_target="tpu_custom_call" | custom-call | tf_op jit(solution)/shard_map/pallas_call | solution.py:339
  59.0 14.8 %all_to_all.11 = f16[16,96,128]{2,1,0:T(8,128)(2,1)S(1)} all-to-all(f16[16,96,128]{2,1,0:T(8,128)(2,1)S(1)} %bitcast.107), channel_id=1, replica_groups=mesh['scan'=16,'cuts'=16] {'cuts'}, dimensions={0} | all-to-all | bytes 786432 | tf_op jit(solution)/shard_map/all_to_all | solution.py:346
  73.9 0.2 broadcast_select_fusion
  74.1 6.9 %collective-permute-start.14 = (f16[16,2,32,128]{3,2,1,0:T(8,128)(2,1)S(1)}, f16[16,2,32,128]{3,2,1,0:T(8,128)(2,1)S(1)}, u32[]{:S(2)}, u32[]{:S(2)}) collective-permute-start(f16[16,2,32,128]{3,2,1,0:T(8,128)(2,1)S(1)} %get-tuple-element.45), channel_id=1, source_target_pairs={{0,16},{16,0},{32,48},{48,32},{64,80},{80,64},{96,112},{112,96},{1... | collective-permute-start | bytes 786440 | tf_op jit(solution)/shard_map/ppermute | solution.py:268
  81.0 1.9 %collective-permute-start.13 = (f16[16,2,32,128]{3,2,1,0:T(8,128)(2,1)S(1)}, f16[16,2,32,128]{3,2,1,0:T(8,128)(2,1)S(1)}, u32[]{:S(2)}, u32[]{:S(2)}) collective-permute-start(f16[16,2,32,128]{3,2,1,0:T(8,128)(2,1)S(1)} %get-tuple-element.67), channel_id=1, source_target_pairs={{16,32},{48,64},{80,96},{112,128},{144,160},{176,192},{208,224},{3... | collective-permute-start | bytes 786440 | tf_op jit(solution)/shard_map/ppermute | solution.py:352
  83.1 5.7 %shard_map.40 = (f32[12,128,128]{2,1,0:T(8,128)S(1)}, f32[6,5,2,4,8,128]{5,4,3,2,1,0:T(8,128)S(1)}) custom-call(f32[1536,128]{1,0:T(8,128)S(1)} %bitcast.98, f32[1024,128]{1,0:T(8,128)S(1)} %bitcast.99), custom_call_target="tpu_custom_call" | custom-call | bytes 3145728 | tf_op jit(solution)/shard_map/pallas_call | solution.py:366
  88.8 0.3 collective-permute-done.13
  89.1 4.3 %shard_map.41 = f32[12,128,128]{2,1,0:T(8,128)} custom-call(f32[1024,128]{1,0:T(8,128)S(1)} %bitcast.100, f32[6,5,2,4,8,128]{5,4,3,2,1,0:T(8,128)S(1)} %get-tuple-element.49.refs_1_, f32[12,128,128]{2,1,0:T(8,128)S(1)} %get-tuple-element.50.refs_2_), custom_call_target="tpu_custom_call" | custom-call | tf_op jit(solution)/shard_map/pallas_call | solution.py:374
  (44 shorter events, 2.3 us)
Async XLA Ops:
  1.5 6.0 %collective-permute-start = (bf16[4,6,8,2048]{3,2,1,0:T(8,128)(2,1)S(1)}, bf16[4,6,8,2048]{3,2,1,0:T(8,128)(2,1)S(1)}, u32[]{:S(2)}, u32[]{:S(2)}) collective-permute-start(bf16[4,6,8,2048]{3,2,1,0:T(8,128)(2,1)S(1)} %get-tuple-element.30), channel_id=1, source_target_pairs={{0,16},{16,0},{32,48},{48,32},{64,80},{80,64},{96,112},{112,96},{1... | collective-permute-start | bytes 2359304 | tf_op jit(solution)/shard_map/ppermute | solution.py:268
  7.5 4.6 %collective-permute-start.1 = (bf16[12,6,8,2048]{3,2,1,0:T(8,128)(2,1)S(1)}, bf16[12,6,8,2048]{3,2,1,0:T(8,128)(2,1)S(1)}, u32[]{:S(2)}, u32[]{:S(2)}) collective-permute-start(bf16[12,6,8,2048]{3,2,1,0:T(8,128)(2,1)S(1)} %get-tuple-element.31), channel_id=1, source_target_pairs={{16,0},{32,48},{48,32},{64,80},{80,64},{96,112},{112,96},{128,144}... | collective-permute-start | bytes 7077896 | tf_op jit(solution)/shard_map/ppermute | solution.py:268
  7.9 10.6 %collective-permute-start.7 = (f16[2,6,8,2048]{3,2,1,0:T(8,128)(2,1)S(1)}, f16[2,6,8,2048]{3,2,1,0:T(8,128)(2,1)S(1)}, u32[]{:S(2)}, u32[]{:S(2)}) collective-permute-start(f16[2,6,8,2048]{3,2,1,0:T(8,128)(2,1)S(1)} %get-tuple-element.61), channel_id=1, source_target_pairs={{0,32},{16,48},{32,0},{48,16},{64,96},{80,112},{96,64},{112,80},{1... | collective-permute-start | bytes 1179656 | tf_op jit(solution)/shard_map/ppermute | solution.py:268
  8.1 7.3 %collective-permute-start.2 = (f16[6,8,2048]{2,1,0:T(8,128)(2,1)S(1)}, f16[6,8,2048]{2,1,0:T(8,128)(2,1)S(1)}, u32[]{:S(2)}, u32[]{:S(2)}) collective-permute-start(f16[6,8,2048]{2,1,0:T(8,128)(2,1)S(1)} %get-tuple-element.73), channel_id=1, source_target_pairs={{0,64},{16,80},{32,96},{48,112},{64,128},{80,144},{96,160},{112,17... | collective-permute-start | bytes 589832 | tf_op jit(solution)/shard_map/ppermute | solution.py:268
  8.9 6.5 %collective-permute-start.3 = (f16[6,8,2048]{2,1,0:T(8,128)(2,1)S(1)}, f16[6,8,2048]{2,1,0:T(8,128)(2,1)S(1)}, u32[]{:S(2)}, u32[]{:S(2)}) collective-permute-start(f16[6,8,2048]{2,1,0:T(8,128)(2,1)S(1)} %get-tuple-element.72), channel_id=1, source_target_pairs={{0,192},{16,208},{32,224},{48,240},{64,0},{80,16},{96,32},{112,48}... | collective-permute-start | bytes 589832 | tf_op jit(solution)/shard_map/ppermute | solution.py:268
  13.0 15.3 %collective-permute-start.8 = (f16[2,6,8,2048]{3,2,1,0:T(8,128)(2,1)S(1)}, f16[2,6,8,2048]{3,2,1,0:T(8,128)(2,1)S(1)}, u32[]{:S(2)}, u32[]{:S(2)}) collective-permute-start(f16[2,6,8,2048]{3,2,1,0:T(8,128)(2,1)S(1)} %multiply_convert_fusion.2), channel_id=1, source_target_pairs={{16,48},{32,0},{48,16},{64,96},{80,112},{96,64},{112,80},{128,160}... | collective-permute-start | bytes 1179656 | tf_op jit(solution)/shard_map/ppermute | solution.py:268
  15.6 10.6 %collective-permute-start.4 = (f16[2,6,8,2048]{3,2,1,0:T(8,128)(2,1)S(1)}, f16[2,6,8,2048]{3,2,1,0:T(8,128)(2,1)S(1)}, u32[]{:S(2)}, u32[]{:S(2)}) collective-permute-start(f16[2,6,8,2048]{3,2,1,0:T(8,128)(2,1)S(1)} %pad_maximum_fusion), channel_id=1, source_target_pairs={{0,64},{16,80},{32,96},{48,112},{64,128},{80,144},{96,160},{112,17... | collective-permute-start | bytes 1179656 | tf_op jit(solution)/shard_map/ppermute | solution.py:268
  15.9 10.3 %collective-permute-start.5 = (f16[2,6,8,2048]{3,2,1,0:T(8,128)(2,1)S(1)}, f16[2,6,8,2048]{3,2,1,0:T(8,128)(2,1)S(1)}, u32[]{:S(2)}, u32[]{:S(2)}) collective-permute-start(f16[2,6,8,2048]{3,2,1,0:T(8,128)(2,1)S(1)} %pad_maximum_fusion.1), channel_id=1, source_target_pairs={{0,192},{16,208},{32,224},{48,240},{64,0},{80,16},{96,32},{112,48}... | collective-permute-start | bytes 1179656 | tf_op jit(solution)/shard_map/ppermute | solution.py:268
  18.7 9.6 %collective-permute-start.9 = (f16[3,8,2048]{2,1,0:T(8,128)(2,1)S(1)}, f16[3,8,2048]{2,1,0:T(8,128)(2,1)S(1)}, u32[]{:S(2)}, u32[]{:S(2)}) collective-permute-start(f16[3,8,2048]{2,1,0:T(8,128)(2,1)S(1)} %get-tuple-element.71), channel_id=1, source_target_pairs={{16,80},{32,96},{48,112},{64,128},{80,144},{96,160},{112,176},{128... | collective-permute-start | bytes 294920 | tf_op jit(solution)/shard_map/ppermute | solution.py:268
  18.8 9.5 %collective-permute-start.10 = (f16[3,8,2048]{2,1,0:T(8,128)(2,1)S(1)}, f16[3,8,2048]{2,1,0:T(8,128)(2,1)S(1)}, u32[]{:S(2)}, u32[]{:S(2)}) collective-permute-start(f16[3,8,2048]{2,1,0:T(8,128)(2,1)S(1)} %get-tuple-element.70), channel_id=1, source_target_pairs={{16,208},{32,224},{48,240},{64,0},{80,16},{96,32},{112,48},{128,64... | collective-permute-start | bytes 294920 | tf_op jit(solution)/shard_map/ppermute | solution.py:268
  28.5 4.0 %copy-start.1 = (bf16[8,96,96]{2,1,0:T(8,128)(2,1)S(1)}, bf16[8,96,96]{2,1,0:T(8,128)(2,1)}, u32[]{:S(2)}) copy-start(bf16[8,96,96]{2,1,0:T(8,128)(2,1)} %param.4) | copy-start | bytes 442372
  28.6 5.3 %collective-permute-start.12 = (f16[6,8,2048]{2,1,0:T(8,128)(2,1)S(1)}, f16[6,8,2048]{2,1,0:T(8,128)(2,1)S(1)}, u32[]{:S(2)}, u32[]{:S(2)}) collective-permute-start(f16[6,8,2048]{2,1,0:T(8,128)(2,1)S(1)} %pad_maximum_fusion.3), channel_id=1, source_target_pairs={{32,224},{48,240},{64,0},{80,16},{96,32},{112,48},{128,64},{144,80... | collective-permute-start | bytes 589832 | tf_op jit(solution)/shard_map/ppermute | solution.py:268
  31.3 5.8 %collective-permute-start.11 = (f16[6,8,2048]{2,1,0:T(8,128)(2,1)S(1)}, f16[6,8,2048]{2,1,0:T(8,128)(2,1)S(1)}, u32[]{:S(2)}, u32[]{:S(2)}) collective-permute-start(f16[6,8,2048]{2,1,0:T(8,128)(2,1)S(1)} %pad_maximum_fusion.2), channel_id=1, source_target_pairs={{32,96},{48,112},{64,128},{80,144},{96,160},{112,176},{128,192},{1... | collective-permute-start | bytes 589832 | tf_op jit(solution)/shard_map/ppermute | solution.py:268
  31.4 6.0 %collective-permute-start.6 = (f16[6,8,2048]{2,1,0:T(8,128)(2,1)S(1)}, f16[6,8,2048]{2,1,0:T(8,128)(2,1)S(1)}, u32[]{:S(2)}, u32[]{:S(2)}) collective-permute-start(f16[6,8,2048]{2,1,0:T(8,128)(2,1)S(1)} %fusion.13), channel_id=1, source_target_pairs={{32,0},{48,16},{64,96},{80,112},{96,64},{112,80},{128,160},{144,17... | collective-permute-start | bytes 589832 | tf_op jit(solution)/shard_map/ppermute | solution.py:268
  37.6 20.2 %copy-start = (s32[8,128]{1,0:T(8,128)S(1)}, s32[8,128]{1,0:T(8,128)}, u32[]{:S(2)}) copy-start(s32[8,128]{1,0:T(8,128)} %classes_ref.1) | copy-start | bytes 12292
  74.1 8.8 %collective-permute-start.14 = (f16[16,2,32,128]{3,2,1,0:T(8,128)(2,1)S(1)}, f16[16,2,32,128]{3,2,1,0:T(8,128)(2,1)S(1)}, u32[]{:S(2)}, u32[]{:S(2)}) collective-permute-start(f16[16,2,32,128]{3,2,1,0:T(8,128)(2,1)S(1)} %get-tuple-element.45), channel_id=1, source_target_pairs={{0,16},{16,0},{32,48},{48,32},{64,80},{80,64},{96,112},{112,96},{1... | collective-permute-start | bytes 786440 | tf_op jit(solution)/shard_map/ppermute | solution.py:268
  81.0 8.0 %collective-permute-start.13 = (f16[16,2,32,128]{3,2,1,0:T(8,128)(2,1)S(1)}, f16[16,2,32,128]{3,2,1,0:T(8,128)(2,1)S(1)}, u32[]{:S(2)}, u32[]{:S(2)}) collective-permute-start(f16[16,2,32,128]{3,2,1,0:T(8,128)(2,1)S(1)} %get-tuple-element.67), channel_id=1, source_target_pairs={{16,32},{48,64},{80,96},{112,128},{144,160},{176,192},{208,224},{3... | collective-permute-start | bytes 786440 | tf_op jit(solution)/shard_map/ppermute | solution.py:352

commit v9 on v8

--- a/solution.py
+++ b/solution.py
@@ -57,6 +57,7 @@
         self.lane = lax.broadcasted_iota(jnp.int32, (self.lines, self.lanes), 1)
         line = lax.broadcasted_iota(jnp.int32, (self.lines, self.lanes), 0)
         self.at_left = self.lane == 0
+        self.homes = [home(self.lane, b, self.lanes) for b in range(WAYS)]
         self.at_right = self.lane == self.lanes - 1
         self.inner = jnp.where(self.at_right & (lax.rem(line, self.groups) == self.groups - 1), 0.0, 1.0)
 
@@ -79,7 +80,7 @@
     def store(self, out_ref, s, row, values):
         values = self.skewed([pltpu.roll(v, self.size * m, 1) for m, v in enumerate(values)])
         for b in range(WAYS):
-            value = jnp.take_along_axis(values[b], home(self.lane, b, self.lanes), axis=1)
+            value = jnp.take_along_axis(values[b], self.homes[b], axis=1)
             for part in range(self.parts):
                 out_ref[part * self.depth + s, pl.ds(b * self.rows + row, self.groups, stride=WAYS * self.rows), :] = (
                     value[part * self.groups : (part + 1) * self.groups]

time: 94.3 us -> 94.3 us (level)
  no operation moved by 1% of the time
where the time goes in v9:
time: 94.3 us; the launch traced here: 93.4 us
  blocking collectives  34.8 us (37%)
  starting transfers between devices  24.8 us (26%)
  Pallas kernels  15.3 us (16%)
  waiting for transfers between devices  14.5 us (15%)
  other arithmetic  2.63 us (3%)
  local copies, waits for them, and re-layouts  1.03 us (1%)
    ppermute x14, starting transfers between devices, send(): return lax.ppermute(array, 'scan', pairs[turn:] + pairs[:turn])  22.9 us
    all_to_all x1, blocking collectives, on_device(): grad = lax.all_to_all(grad, 'cuts', 0, 0, tiled=True)  20 us
    all_to_all x1, blocking collectives, on_device(): coded = lax.all_to_all(coded, 'cuts', 0, 0, tiled=True)  14.8 us
    ppermute x14, waiting for transfers between devices, send(): return lax.ppermute(array, 'scan', pairs[turn:] + pairs[:turn])  14.3 us
    pallas_call x1, Pallas kernels, on_device(): pl.pallas_call(lambda *refs: near_kernel(shape, skipped, *refs), out_shap...  5.73 us
    pallas_call x1, Pallas kernels, on_device(): pl.pallas_call(lambda *refs: far_kernel(shape, skipped, *refs), out_shape...  4.29 us
    pallas_call x2, Pallas kernels, copied(): pl.pallas_call(lambda *refs: copy_kernel(plan, *refs), out_shape=[jax.Sha...  4.15 us
    ppermute x1, starting transfers between devices, on_device(): lax.ppermute(jnp.where(upper, top, bottom), 'scan', [(i, i + 1) for i in...  1.91 us
  transfers between devices with their start and end apart: 15, of which 7 were waited for; matrix products, arithmetic and copies ran while one was open for 3% of the time, Pallas kernels for 9%

profile of v9, /device:TPU:1, one launch (start us, length us, event | category | flops | bytes accessed | tf_op | source)
XLA Modules:
  0.0 93.4 jit_solution(12421027293404208158)
XLA Ops:
  0.0 1.5 %shard_map.38 = (bf16[4,6,8,2048]{3,2,1,0:T(8,128)(2,1)S(1)}, bf16[4,6,8,2048]{3,2,1,0:T(8,128)(2,1)S(1)}) custom-call(bf16[2,6,4,2,2,8,2048]{6,5,4,3,2,1,0:T(8,128)(2,1)} %bitcast.101), custom_call_target="tpu_custom_call" | custom-call | bytes 3145728 | tf_op jit(solution)/shard_map/pallas_call | solution.py:246
  1.5 3.3 %collective-permute-start = (bf16[4,6,8,2048]{3,2,1,0:T(8,128)(2,1)S(1)}, bf16[4,6,8,2048]{3,2,1,0:T(8,128)(2,1)S(1)}, u32[]{:S(2)}, u32[]{:S(2)}) collective-permute-start(bf16[4,6,8,2048]{3,2,1,0:T(8,128)(2,1)S(1)} %get-tuple-element.30), channel_id=1, source_target_pairs={{0,16},{16,0},{32,48},{48,32},{64,80},{80,64},{96,112},{112,96},{1... | collective-permute-start | bytes 2359304 | tf_op jit(solution)/shard_map/ppermute | solution.py:269
  4.9 2.6 %shard_map.37 = (bf16[12,6,8,2048]{3,2,1,0:T(8,128)(2,1)S(1)}, bf16[12,6,8,2048]{3,2,1,0:T(8,128)(2,1)S(1)}) custom-call(bf16[2,6,4,2,2,8,2048]{6,5,4,3,2,1,0:T(8,128)(2,1)} %bitcast.102), custom_call_target="tpu_custom_call" | custom-call | bytes 9437184 | tf_op jit(solution)/shard_map/pallas_call | solution.py:246
  7.6 0.3 multiply_convert_fusion.3
  8.1 0.8 collective-permute-start.2
  8.9 1.9 %collective-permute-start.3 = (f16[6,8,2048]{2,1,0:T(8,128)(2,1)S(1)}, f16[6,8,2048]{2,1,0:T(8,128)(2,1)S(1)}, u32[]{:S(2)}, u32[]{:S(2)}) collective-permute-start(f16[6,8,2048]{2,1,0:T(8,128)(2,1)S(1)} %get-tuple-element.72), channel_id=1, source_target_pairs={{0,192},{16,208},{32,224},{48,240},{64,0},{80,16},{96,32},{112,48}... | collective-permute-start | bytes 589832 | tf_op jit(solution)/shard_map/ppermute | solution.py:269
  10.9 1.3 %collective-permute-done.1 = bf16[12,6,8,2048]{3,2,1,0:T(8,128)(2,1)S(1)} collective-permute-done((bf16[12,6,8,2048]{3,2,1,0:T(8,128)(2,1)S(1)}, bf16[12,6,8,2048]{3,2,1,0:T(8,128)(2,1)S(1)}, u32[]{:S(2)}, u32[]{:S(2)}) %collective-permute-start.1) | collective-permute-done | bytes 2359328 | tf_op jit(solution)/shard_map/ppermute | solution.py:269
  12.1 0.6 add_multiply_fusion
  12.8 0.1 multiply_convert_fusion.2
  13.0 0.3 collective-permute-start.8
  13.3 2.1 %collective-permute-done.2 = f16[6,8,2048]{2,1,0:T(8,128)(2,1)S(1)} collective-permute-done((f16[6,8,2048]{2,1,0:T(8,128)(2,1)S(1)}, f16[6,8,2048]{2,1,0:T(8,128)(2,1)S(1)}, u32[]{:S(2)}, u32[]{:S(2)}) %collective-permute-start.2) | collective-permute-done | bytes 196640 | tf_op jit(solution)/shard_map/ppermute | solution.py:269
  15.6 0.2 collective-permute-start.4
  15.9 2.6 %collective-permute-start.5 = (f16[2,6,8,2048]{3,2,1,0:T(8,128)(2,1)S(1)}, f16[2,6,8,2048]{3,2,1,0:T(8,128)(2,1)S(1)}, u32[]{:S(2)}, u32[]{:S(2)}) collective-permute-start(f16[2,6,8,2048]{3,2,1,0:T(8,128)(2,1)S(1)} %pad_maximum_fusion.1), channel_id=1, source_target_pairs={{0,192},{16,208},{32,224},{48,240},{64,0},{80,16},{96,32},{112,48}... | collective-permute-start | bytes 1179656 | tf_op jit(solution)/shard_map/ppermute | solution.py:269
  18.8 2.7 %collective-permute-start.10 = (f16[3,8,2048]{2,1,0:T(8,128)(2,1)S(1)}, f16[3,8,2048]{2,1,0:T(8,128)(2,1)S(1)}, u32[]{:S(2)}, u32[]{:S(2)}) collective-permute-start(f16[3,8,2048]{2,1,0:T(8,128)(2,1)S(1)} %get-tuple-element.70), channel_id=1, source_target_pairs={{16,208},{32,224},{48,240},{64,0},{80,16},{96,32},{112,48},{128,64... | collective-permute-start | bytes 294920 | tf_op jit(solution)/shard_map/ppermute | solution.py:269
  21.5 4.7 %collective-permute-done.4 = f16[2,6,8,2048]{3,2,1,0:T(8,128)(2,1)S(1)} collective-permute-done((f16[2,6,8,2048]{3,2,1,0:T(8,128)(2,1)S(1)}, f16[2,6,8,2048]{3,2,1,0:T(8,128)(2,1)S(1)}, u32[]{:S(2)}, u32[]{:S(2)}) %collective-permute-start.4) | collective-permute-done | bytes 393248 | tf_op jit(solution)/shard_map/ppermute | solution.py:269
  26.2 0.2 convert_add_fusion
  26.5 1.8 %collective-permute-done.9 = f16[3,8,2048]{2,1,0:T(8,128)(2,1)S(1)} collective-permute-done((f16[3,8,2048]{2,1,0:T(8,128)(2,1)S(1)}, f16[3,8,2048]{2,1,0:T(8,128)(2,1)S(1)}, u32[]{:S(2)}, u32[]{:S(2)}) %collective-permute-start.9) | collective-permute-done | bytes 98336 | tf_op jit(solution)/shard_map/ppermute | solution.py:269
  28.3 0.1 fusion.19
  28.6 2.6 %collective-permute-start.12 = (f16[6,8,2048]{2,1,0:T(8,128)(2,1)S(1)}, f16[6,8,2048]{2,1,0:T(8,128)(2,1)S(1)}, u32[]{:S(2)}, u32[]{:S(2)}) collective-permute-start(f16[6,8,2048]{2,1,0:T(8,128)(2,1)S(1)} %pad_maximum_fusion.3), channel_id=1, source_target_pairs={{32,224},{48,240},{64,0},{80,16},{96,32},{112,48},{128,64},{144,80... | collective-permute-start | bytes 589832 | tf_op jit(solution)/shard_map/ppermute | solution.py:269
  31.4 1.1 %collective-permute-start.6 = (f16[6,8,2048]{2,1,0:T(8,128)(2,1)S(1)}, f16[6,8,2048]{2,1,0:T(8,128)(2,1)S(1)}, u32[]{:S(2)}, u32[]{:S(2)}) collective-permute-start(f16[6,8,2048]{2,1,0:T(8,128)(2,1)S(1)} %fusion.13), channel_id=1, source_target_pairs={{32,0},{48,16},{64,96},{80,112},{96,64},{112,80},{128,160},{144,17... | collective-permute-start | bytes 589832 | tf_op jit(solution)/shard_map/ppermute | solution.py:269
  32.6 0.2 reshape.41.weights_ref
  32.8 1.1 %collective-permute-done.12 = f16[6,8,2048]{2,1,0:T(8,128)(2,1)S(1)} collective-permute-done((f16[6,8,2048]{2,1,0:T(8,128)(2,1)S(1)}, f16[6,8,2048]{2,1,0:T(8,128)(2,1)S(1)}, u32[]{:S(2)}, u32[]{:S(2)}) %collective-permute-start.12) | collective-permute-done | bytes 196640 | tf_op jit(solution)/shard_map/ppermute | solution.py:269
  33.9 3.2 %collective-permute-done.11 = f16[6,8,2048]{2,1,0:T(8,128)(2,1)S(1)} collective-permute-done((f16[6,8,2048]{2,1,0:T(8,128)(2,1)S(1)}, f16[6,8,2048]{2,1,0:T(8,128)(2,1)S(1)}, u32[]{:S(2)}, u32[]{:S(2)}) %collective-permute-start.11) | collective-permute-done | bytes 196640 | tf_op jit(solution)/shard_map/ppermute | solution.py:269
  37.8 20.0 %all_to_all.10.grad_ref = bf16[16,2,6,8,128]{4,3,2,1,0:T(8,128)(2,1)S(1)} all-to-all(bf16[16,2,6,8,128]{4,3,2,1,0:T(8,128)(2,1)S(1)} %fusion.1), channel_id=1, replica_groups=mesh['scan'=16,'cuts'=16] {'cuts'}, dimensions={0} | all-to-all | bytes 786432 | tf_op jit(solution)/shard_map/all_to_all | solution.py:338
  57.8 1.1 %shard_map.39 = f32[1536,128]{1,0:T(8,128)S(1)} custom-call(bf16[16,2,6,8,128]{4,3,2,1,0:T(8,128)(2,1)S(1)} %all_to_all.10.grad_ref, bf16[96,768]{1,0:T(8,128)(2,1)S(1)} %reshape.41.weights_ref, s32[8,128]{1,0:T(8,128)S(1)} %copy-done), custom_call_target="tpu_custom_call" | custom-call | tf_op jit(solution)/shard_map/pallas_call | solution.py:340
  59.0 14.8 %all_to_all.11 = f16[16,96,128]{2,1,0:T(8,128)(2,1)S(1)} all-to-all(f16[16,96,128]{2,1,0:T(8,128)(2,1)S(1)} %bitcast.107), channel_id=1, replica_groups=mesh['scan'=16,'cuts'=16] {'cuts'}, dimensions={0} | all-to-all | bytes 786432 | tf_op jit(solution)/shard_map/all_to_all | solution.py:347
  73.9 0.2 broadcast_select_fusion
  74.1 6.9 %collective-permute-start.14 = (f16[16,2,32,128]{3,2,1,0:T(8,128)(2,1)S(1)}, f16[16,2,32,128]{3,2,1,0:T(8,128)(2,1)S(1)}, u32[]{:S(2)}, u32[]{:S(2)}) collective-permute-start(f16[16,2,32,128]{3,2,1,0:T(8,128)(2,1)S(1)} %get-tuple-element.45), channel_id=1, source_target_pairs={{0,16},{16,0},{32,48},{48,32},{64,80},{80,64},{96,112},{112,96},{1... | collective-permute-start | bytes 786440 | tf_op jit(solution)/shard_map/ppermute | solution.py:269
  81.0 1.9 %collective-permute-start.13 = (f16[16,2,32,128]{3,2,1,0:T(8,128)(2,1)S(1)}, f16[16,2,32,128]{3,2,1,0:T(8,128)(2,1)S(1)}, u32[]{:S(2)}, u32[]{:S(2)}) collective-permute-start(f16[16,2,32,128]{3,2,1,0:T(8,128)(2,1)S(1)} %get-tuple-element.67), channel_id=1, source_target_pairs={{16,32},{48,64},{80,96},{112,128},{144,160},{176,192},{208,224},{3... | collective-permute-start | bytes 786440 | tf_op jit(solution)/shard_map/ppermute | solution.py:353
  83.1 5.7 %shard_map.40 = (f32[12,128,128]{2,1,0:T(8,128)S(1)}, f32[6,5,2,4,8,128]{5,4,3,2,1,0:T(8,128)S(1)}) custom-call(f32[1536,128]{1,0:T(8,128)S(1)} %bitcast.98, f32[1024,128]{1,0:T(8,128)S(1)} %bitcast.99), custom_call_target="tpu_custom_call" | custom-call | bytes 3145728 | tf_op jit(solution)/shard_map/pallas_call | solution.py:367
  88.8 0.2 collective-permute-done.13
  89.1 4.3 %shard_map.41 = f32[12,128,128]{2,1,0:T(8,128)} custom-call(f32[1024,128]{1,0:T(8,128)S(1)} %bitcast.100, f32[6,5,2,4,8,128]{5,4,3,2,1,0:T(8,128)S(1)} %get-tuple-element.49.refs_1_, f32[12,128,128]{2,1,0:T(8,128)S(1)} %get-tuple-element.50.refs_2_), custom_call_target="tpu_custom_call" | custom-call | tf_op jit(solution)/shard_map/pallas_call | solution.py:375
  (44 shorter events, 2.3 us)
Async XLA Ops:
  1.5 6.0 %collective-permute-start = (bf16[4,6,8,2048]{3,2,1,0:T(8,128)(2,1)S(1)}, bf16[4,6,8,2048]{3,2,1,0:T(8,128)(2,1)S(1)}, u32[]{:S(2)}, u32[]{:S(2)}) collective-permute-start(bf16[4,6,8,2048]{3,2,1,0:T(8,128)(2,1)S(1)} %get-tuple-element.30), channel_id=1, source_target_pairs={{0,16},{16,0},{32,48},{48,32},{64,80},{80,64},{96,112},{112,96},{1... | collective-permute-start | bytes 2359304 | tf_op jit(solution)/shard_map/ppermute | solution.py:269
  7.5 4.6 %collective-permute-start.1 = (bf16[12,6,8,2048]{3,2,1,0:T(8,128)(2,1)S(1)}, bf16[12,6,8,2048]{3,2,1,0:T(8,128)(2,1)S(1)}, u32[]{:S(2)}, u32[]{:S(2)}) collective-permute-start(bf16[12,6,8,2048]{3,2,1,0:T(8,128)(2,1)S(1)} %get-tuple-element.31), channel_id=1, source_target_pairs={{16,0},{32,48},{48,32},{64,80},{80,64},{96,112},{112,96},{128,144}... | collective-permute-start | bytes 7077896 | tf_op jit(solution)/shard_map/ppermute | solution.py:269
  7.9 10.6 %collective-permute-start.7 = (f16[2,6,8,2048]{3,2,1,0:T(8,128)(2,1)S(1)}, f16[2,6,8,2048]{3,2,1,0:T(8,128)(2,1)S(1)}, u32[]{:S(2)}, u32[]{:S(2)}) collective-permute-start(f16[2,6,8,2048]{3,2,1,0:T(8,128)(2,1)S(1)} %get-tuple-element.61), channel_id=1, source_target_pairs={{0,32},{16,48},{32,0},{48,16},{64,96},{80,112},{96,64},{112,80},{1... | collective-permute-start | bytes 1179656 | tf_op jit(solution)/shard_map/ppermute | solution.py:269
  8.1 7.3 %collective-permute-start.2 = (f16[6,8,2048]{2,1,0:T(8,128)(2,1)S(1)}, f16[6,8,2048]{2,1,0:T(8,128)(2,1)S(1)}, u32[]{:S(2)}, u32[]{:S(2)}) collective-permute-start(f16[6,8,2048]{2,1,0:T(8,128)(2,1)S(1)} %get-tuple-element.73), channel_id=1, source_target_pairs={{0,64},{16,80},{32,96},{48,112},{64,128},{80,144},{96,160},{112,17... | collective-permute-start | bytes 589832 | tf_op jit(solution)/shard_map/ppermute | solution.py:269
  8.9 6.5 %collective-permute-start.3 = (f16[6,8,2048]{2,1,0:T(8,128)(2,1)S(1)}, f16[6,8,2048]{2,1,0:T(8,128)(2,1)S(1)}, u32[]{:S(2)}, u32[]{:S(2)}) collective-permute-start(f16[6,8,2048]{2,1,0:T(8,128)(2,1)S(1)} %get-tuple-element.72), channel_id=1, source_target_pairs={{0,192},{16,208},{32,224},{48,240},{64,0},{80,16},{96,32},{112,48}... | collective-permute-start | bytes 589832 | tf_op jit(solution)/shard_map/ppermute | solution.py:269
  13.0 15.3 %collective-permute-start.8 = (f16[2,6,8,2048]{3,2,1,0:T(8,128)(2,1)S(1)}, f16[2,6,8,2048]{3,2,1,0:T(8,128)(2,1)S(1)}, u32[]{:S(2)}, u32[]{:S(2)}) collective-permute-start(f16[2,6,8,2048]{3,2,1,0:T(8,128)(2,1)S(1)} %multiply_convert_fusion.2), channel_id=1, source_target_pairs={{16,48},{32,0},{48,16},{64,96},{80,112},{96,64},{112,80},{128,160}... | collective-permute-start | bytes 1179656 | tf_op jit(solution)/shard_map/ppermute | solution.py:269
  15.6 10.6 %collective-permute-start.4 = (f16[2,6,8,2048]{3,2,1,0:T(8,128)(2,1)S(1)}, f16[2,6,8,2048]{3,2,1,0:T(8,128)(2,1)S(1)}, u32[]{:S(2)}, u32[]{:S(2)}) collective-permute-start(f16[2,6,8,2048]{3,2,1,0:T(8,128)(2,1)S(1)} %pad_maximum_fusion), channel_id=1, source_target_pairs={{0,64},{16,80},{32,96},{48,112},{64,128},{80,144},{96,160},{112,17... | collective-permute-start | bytes 1179656 | tf_op jit(solution)/shard_map/ppermute | solution.py:269
  15.9 10.3 %collective-permute-start.5 = (f16[2,6,8,2048]{3,2,1,0:T(8,128)(2,1)S(1)}, f16[2,6,8,2048]{3,2,1,0:T(8,128)(2,1)S(1)}, u32[]{:S(2)}, u32[]{:S(2)}) collective-permute-start(f16[2,6,8,2048]{3,2,1,0:T(8,128)(2,1)S(1)} %pad_maximum_fusion.1), channel_id=1, source_target_pairs={{0,192},{16,208},{32,224},{48,240},{64,0},{80,16},{96,32},{112,48}... | collective-permute-start | bytes 1179656 | tf_op jit(solution)/shard_map/ppermute | solution.py:269
  18.7 9.6 %collective-permute-start.9 = (f16[3,8,2048]{2,1,0:T(8,128)(2,1)S(1)}, f16[3,8,2048]{2,1,0:T(8,128)(2,1)S(1)}, u32[]{:S(2)}, u32[]{:S(2)}) collective-permute-start(f16[3,8,2048]{2,1,0:T(8,128)(2,1)S(1)} %get-tuple-element.71), channel_id=1, source_target_pairs={{16,80},{32,96},{48,112},{64,128},{80,144},{96,160},{112,176},{128... | collective-permute-start | bytes 294920 | tf_op jit(solution)/shard_map/ppermute | solution.py:269
  18.8 9.5 %collective-permute-start.10 = (f16[3,8,2048]{2,1,0:T(8,128)(2,1)S(1)}, f16[3,8,2048]{2,1,0:T(8,128)(2,1)S(1)}, u32[]{:S(2)}, u32[]{:S(2)}) collective-permute-start(f16[3,8,2048]{2,1,0:T(8,128)(2,1)S(1)} %get-tuple-element.70), channel_id=1, source_target_pairs={{16,208},{32,224},{48,240},{64,0},{80,16},{96,32},{112,48},{128,64... | collective-permute-start | bytes 294920 | tf_op jit(solution)/shard_map/ppermute | solution.py:269
  28.5 4.0 %copy-start.1 = (bf16[8,96,96]{2,1,0:T(8,128)(2,1)S(1)}, bf16[8,96,96]{2,1,0:T(8,128)(2,1)}, u32[]{:S(2)}) copy-start(bf16[8,96,96]{2,1,0:T(8,128)(2,1)} %param.4) | copy-start | bytes 442372
  28.6 5.3 %collective-permute-start.12 = (f16[6,8,2048]{2,1,0:T(8,128)(2,1)S(1)}, f16[6,8,2048]{2,1,0:T(8,128)(2,1)S(1)}, u32[]{:S(2)}, u32[]{:S(2)}) collective-permute-start(f16[6,8,2048]{2,1,0:T(8,128)(2,1)S(1)} %pad_maximum_fusion.3), channel_id=1, source_target_pairs={{32,224},{48,240},{64,0},{80,16},{96,32},{112,48},{128,64},{144,80... | collective-permute-start | bytes 589832 | tf_op jit(solution)/shard_map/ppermute | solution.py:269
  31.3 5.8 %collective-permute-start.11 = (f16[6,8,2048]{2,1,0:T(8,128)(2,1)S(1)}, f16[6,8,2048]{2,1,0:T(8,128)(2,1)S(1)}, u32[]{:S(2)}, u32[]{:S(2)}) collective-permute-start(f16[6,8,2048]{2,1,0:T(8,128)(2,1)S(1)} %pad_maximum_fusion.2), channel_id=1, source_target_pairs={{32,96},{48,112},{64,128},{80,144},{96,160},{112,176},{128,192},{1... | collective-permute-start | bytes 589832 | tf_op jit(solution)/shard_map/ppermute | solution.py:269
  31.4 6.0 %collective-permute-start.6 = (f16[6,8,2048]{2,1,0:T(8,128)(2,1)S(1)}, f16[6,8,2048]{2,1,0:T(8,128)(2,1)S(1)}, u32[]{:S(2)}, u32[]{:S(2)}) collective-permute-start(f16[6,8,2048]{2,1,0:T(8,128)(2,1)S(1)} %fusion.13), channel_id=1, source_target_pairs={{32,0},{48,16},{64,96},{80,112},{96,64},{112,80},{128,160},{144,17... | collective-permute-start | bytes 589832 | tf_op jit(solution)/shard_map/ppermute | solution.py:269
  37.6 20.2 %copy-start = (s32[8,128]{1,0:T(8,128)S(1)}, s32[8,128]{1,0:T(8,128)}, u32[]{:S(2)}) copy-start(s32[8,128]{1,0:T(8,128)} %classes_ref.1) | copy-start | bytes 12292
  74.1 8.8 %collective-permute-start.14 = (f16[16,2,32,128]{3,2,1,0:T(8,128)(2,1)S(1)}, f16[16,2,32,128]{3,2,1,0:T(8,128)(2,1)S(1)}, u32[]{:S(2)}, u32[]{:S(2)}) collective-permute-start(f16[16,2,32,128]{3,2,1,0:T(8,128)(2,1)S(1)} %get-tuple-element.45), channel_id=1, source_target_pairs={{0,16},{16,0},{32,48},{48,32},{64,80},{80,64},{96,112},{112,96},{1... | collective-permute-start | bytes 786440 | tf_op jit(solution)/shard_map/ppermute | solution.py:269
  81.0 8.0 %collective-permute-start.13 = (f16[16,2,32,128]{3,2,1,0:T(8,128)(2,1)S(1)}, f16[16,2,32,128]{3,2,1,0:T(8,128)(2,1)S(1)}, u32[]{:S(2)}, u32[]{:S(2)}) collective-permute-start(f16[16,2,32,128]{3,2,1,0:T(8,128)(2,1)S(1)} %get-tuple-element.67), channel_id=1, source_target_pairs={{16,32},{48,64},{80,96},{112,128},{144,160},{176,192},{208,224},{3... | collective-permute-start | bytes 786440 | tf_op jit(solution)/shard_map/ppermute | solution.py:353
